TPU v7x, 32 devices: a whole 2x2x4 slice. The times are simulated.
32 devices in a mesh: rep: 2 (over y), ep: 8 (over z, core), tp: 2 (over x).
Axes of the slice: x: 2, y: 2, z: 4, core: 2. Of those that a mesh axis runs over, the one named last changes fastest.
Arguments:
- hidden_states: bfloat16 [2, 1024, 2048], P(None, ('rep', 'ep'), 'tp'), parts along dimension 1, may hold values from -8 to 8
- queries: bfloat16 [2, 1024, 4096], P(None, ('rep', 'ep'), 'tp'), parts along dimension 1, may hold values from -8 to 8
- fresh_key_value: bfloat16 [2, 1024, 2, 512], P(None, ('rep', 'ep'), None, 'tp'), parts along dimension 1, may hold values from -8 to 8
- cache: bfloat16 [16, 2, 1024, 512], P(('rep', 'ep'), None, None, 'tp'), parts along dimension 0, may hold values from -8 to 8
- cache_lengths: int32 [16], P(('rep', 'ep')), parts along dimension 0, may hold values from 1 to 1024, 4096 in all
- out_weight: bfloat16 [4096, 2048], P('tp', 'ep'), may hold values from -1 to 1
- router_weight: bfloat16 [2048, 16], P('tp'), may hold values from -0.125 to 0.125
- expert_weights: bfloat16 [16, 3, 2048, 384], P('ep', None, 'tp'), may hold values from -0.21875 to 0.21875
- expert_ids: int32 [2, 1024, 8], P(None, ('rep', 'ep')), parts along dimension 1, may hold values from 0 to 15, all different within a row; in each aligned block of 64 rows (0 to 63, 64 to 127, ..., all dimensions but the last counted through in order) at most 48 rows name the same one
- old_slots: int32 [16], replicated, may hold values from 0 to 15, as said below
- new_slots: int32 [16], replicated, may hold values from 0 to 15, as said below
- moved_experts: int32 [4], replicated, may hold values from 0 to 15, as said below
Outputs:
- mixed: bfloat16 [2, 1024, 2048], P(None, ('rep', 'ep'), 'tp'), parts along dimension 1
There are 2 independent parts, one for each index of `rep`. A program takes and returns all parts, laid end to end along the dimension named above; an argument that names none is the same for every part. Nothing has to cross between parts.
Inputs may be any that keep to these rules, and one draw needn't show every extreme that they name: `expert_ids`: each row names 8 different experts. Within the 64 rows of one request in one token block, no expert is named by more than 48 rows, a bound that some block reaches. `old_slots`: A permutation: each slot holds one expert. `new_slots`: equal to old_slots except at the moved experts, which take one another's old slots, none keeping its own. `moved_experts`: 4 different experts; no two of their old slots s share the same s // 2.
All inputs are finite; a program needn't handle non-finite values. No bound on the sum of `cache_lengths` on one device may be relied on, other than what follows from the above.
Results may differ from a plain program's by a relative error of at most 0.017.
Values may be sent and summed in bfloat16 or wider, within the bound.
No kernel may reach another device: no remote copies, remote signals or barrier semaphores. Data moves between devices by JAX's collectives and lax.ppermute only.
A program may use at most 64 MiB of HBM per device.

v0:
```python
import jax
import jax.numpy as jnp
from jax import lax
from jax.sharding import PartitionSpec as P

D = 2048
HEAD_SIZE = 128


def lookup(entries, wanted_keys):
    return jnp.sum(
        jnp.where(
            wanted_keys[..., None] == jnp.arange(entries.shape[0], dtype=jnp.int32), entries, 0
        ),
        -1,
    )


def attend_local(queries, fresh_key_value, cache, cache_lengths):
    tokens_dev = queries.shape[1]
    kv_heads = fresh_key_value.shape[3] // HEAD_SIZE
    query_group_width = queries.shape[2] // HEAD_SIZE // kv_heads
    key_matrix = jnp.concatenate(
        [cache[0, 0], fresh_key_value[0, :, 0], fresh_key_value[1, :, 0]], 0
    )
    value_matrix = jnp.concatenate(
        [cache[0, 1], fresh_key_value[0, :, 1], fresh_key_value[1, :, 1]], 0
    )
    key_total = key_matrix.shape[0]
    context = cache.shape[2]
    query_matrix = queries.reshape(2 * tokens_dev, kv_heads, query_group_width, HEAD_SIZE)
    attention_scores = jnp.einsum(
        "meqt,wet->eqmw",
        query_matrix,
        key_matrix.reshape(key_total, kv_heads, HEAD_SIZE),
        preferred_element_type=jnp.float32,
    ) * HEAD_SIZE ** (-0.5)
    position = jnp.arange(key_total, dtype=jnp.int32)[None, :]
    row_index = jnp.arange(2 * tokens_dev, dtype=jnp.int32)[:, None]
    visible = jnp.where(
        position < context, position < cache_lengths[0], position - context <= row_index
    )
    attention_scores = jnp.where(visible, attention_scores, jnp.float32(-1e30))
    largest = jnp.max(attention_scores, -1, keepdims=True)
    weights = jnp.where(visible, jnp.exp(attention_scores - largest), jnp.float32(0.0))
    route_probability = (weights / jnp.sum(weights, -1, keepdims=True)).astype(jnp.bfloat16)
    layer_result = jnp.einsum(
        "qizo,oqx->zqix",
        route_probability,
        value_matrix.reshape(key_total, kv_heads, HEAD_SIZE),
        preferred_element_type=jnp.float32,
    )
    return layer_result.reshape(2 * tokens_dev, -1).astype(jnp.bfloat16)


def run_slots(weights, received):
    gate_up = jnp.einsum(
        "secq,egqf->secgf", received, weights[:, :2], preferred_element_type=jnp.float32
    )
    summed = lax.psum(gate_up.astype(jnp.bfloat16), "tp").astype(jnp.float32)
    hidden = (jax.nn.silu(summed[:, :, :, 0]) * summed[:, :, :, 1]).astype(jnp.bfloat16)
    layer_result = jnp.einsum(
        "secf,eqf->secq", hidden, weights[:, 2], preferred_element_type=jnp.float32
    ).astype(jnp.bfloat16)
    return lax.all_to_all(layer_result, "ep", split_axis=0, concat_axis=0, tiled=True)


def mix_block(normed_rows, resid_rows, routed, combine, slot_table, weights, capacity, groups):
    tokens_dev, top_count = routed.shape
    experts = slot_table.shape[0]
    local_slots = weights.shape[0]
    quarter = normed_rows.shape[1]
    slot_index = lookup(slot_table, routed)
    picked_mask = routed[:, :, None] == jnp.arange(experts, dtype=jnp.int32)[None, None, :]
    expert_marks = picked_mask.any(1).astype(jnp.bfloat16)
    earlier = (jnp.arange(tokens_dev)[:, None] > jnp.arange(tokens_dev)[None, :]).astype(
        jnp.bfloat16
    )
    before = jnp.dot(earlier, expert_marks, preferred_element_type=jnp.float32)
    slot_rank = jnp.sum(jnp.where(picked_mask, before[:, None, :], 0.0), -1).astype(jnp.int32)
    buffer_row = (slot_index * capacity + slot_rank).reshape(-1)
    buffer_rows = (
        jnp.zeros((groups * local_slots * capacity, quarter), jnp.bfloat16)
        .at[buffer_row]
        .set(jnp.repeat(normed_rows, top_count, axis=0))
    )
    outgoing = buffer_rows.reshape(groups, local_slots, capacity, quarter)
    returned = run_slots(
        weights, lax.all_to_all(outgoing, "ep", split_axis=0, concat_axis=0, tiled=True)
    )
    gathered = returned.reshape(-1, quarter)[buffer_row].reshape(tokens_dev, top_count, quarter)
    mixed_rows = resid_rows.astype(jnp.float32) + jnp.sum(
        combine[:, :, None] * gathered.astype(jnp.float32), 1
    )
    return mixed_rows.astype(jnp.bfloat16)


def relocate(expert_weights, old_slots, new_slots, moved_experts):
    local_slots = expert_weights.shape[0]
    groups = lax.axis_size("ep")
    flat_weights = expert_weights.reshape(local_slots, groups, -1)
    old_moved = lookup(old_slots, moved_experts)
    new_moved = lookup(new_slots, moved_experts)
    own_slots = lax.axis_index("ep") * local_slots + jnp.arange(local_slots, dtype=jnp.int32)
    leaving = (own_slots[:, None] == old_moved[None, :]).any(1)
    outgoing = jnp.sum(jnp.where(leaving[:, None, None], flat_weights, jnp.bfloat16(0.0)), 0)
    spread = lax.all_to_all(outgoing, "ep", split_axis=0, concat_axis=0, tiled=True)
    target_dev = new_moved // local_slots
    anchor_dev = old_moved // local_slots
    matches = jnp.arange(groups, dtype=jnp.int32)[:, None] == target_dev[None, :]
    anchor = jnp.sum(jnp.where(matches, anchor_dev[None, :], 0), 1)
    picked = jnp.where(matches.any(1)[:, None], spread[anchor], jnp.bfloat16(0.0))
    landed = lax.all_to_all(picked, "ep", split_axis=0, concat_axis=0, tiled=True)
    arriving = (own_slots[:, None] == new_moved[None, :]).any(1)
    return jnp.where(
        arriving[:, None, None, None],
        landed.reshape(expert_weights.shape[1:])[None],
        expert_weights,
    )


def per_device(
    hidden_states,
    queries,
    fresh_key_value,
    cache,
    cache_lengths,
    out_weight,
    router_weight,
    expert_weights,
    expert_ids,
    old_slots,
    new_slots,
    moved_experts,
):
    tokens_dev = hidden_states.shape[1]
    quarter = hidden_states.shape[2]
    experts = router_weight.shape[1]
    top_count = expert_ids.shape[2]
    groups = lax.axis_size("ep")
    capacity = min(tokens_dev, 3 * tokens_dev * top_count // (2 * experts))
    attention = attend_local(queries, fresh_key_value, cache, cache_lengths)
    head_terms = jnp.dot(
        attention,
        lax.all_gather(out_weight, "ep", axis=1, tiled=True),
        preferred_element_type=jnp.float32,
    )
    attn_out = lax.psum_scatter(
        head_terms.astype(jnp.bfloat16), "tp", scatter_dimension=1, tiled=True
    ).astype(jnp.float32)
    residual = (
        hidden_states.reshape(2 * tokens_dev, quarter).astype(jnp.float32) + attn_out
    ).astype(jnp.bfloat16)
    wide = residual.astype(jnp.float32)
    squares = lax.psum(jnp.sum(wide * wide, 1), "tp")
    normed = (wide * lax.rsqrt(squares / D + 1e-06)[:, None]).astype(jnp.bfloat16)
    logits = lax.psum(
        jnp.dot(normed, router_weight, preferred_element_type=jnp.float32).astype(jnp.bfloat16),
        "tp",
    ).astype(jnp.float32)
    routed = expert_ids.reshape(2 * tokens_dev, top_count)
    selected = jnp.sum(
        jnp.where(
            routed[:, :, None] == jnp.arange(experts, dtype=jnp.int32)[None, None, :],
            logits[:, None, :],
            0.0,
        ),
        -1,
    )
    raised = jnp.exp(selected)
    combine = raised / jnp.sum(raised, 1, keepdims=True)
    weights_two = relocate(expert_weights, old_slots, new_slots, moved_experts)
    outputs = []
    for block_index, slot_table, weights in (
        (0, old_slots, expert_weights),
        (1, new_slots, weights_two),
    ):
        lower = block_index * tokens_dev
        upper = lower + tokens_dev
        outputs.append(
            mix_block(
                normed[lower:upper],
                residual[lower:upper],
                routed[lower:upper],
                combine[lower:upper],
                slot_table,
                weights,
                capacity,
                groups,
            )
        )
    return jnp.stack(outputs)


def solution(mesh):
    return jax.shard_map(
        per_device,
        mesh=mesh,
        in_specs=(
            P(None, ("rep", "ep"), "tp"),
            P(None, ("rep", "ep"), "tp"),
            P(None, ("rep", "ep"), None, "tp"),
            P(("rep", "ep"), None, None, "tp"),
            P(("rep", "ep")),
            P("tp", "ep"),
            P("tp", None),
            P("ep", None, "tp", None),
            P(None, ("rep", "ep"), None),
            P(),
            P(),
            P(),
        ),
        out_specs=P(None, ("rep", "ep"), "tp"),
        check_vma=False,
    )
```

profile of v0, /device:TPU:0, one launch (start us, length us, event | category | flops | bytes accessed | tf_op | source)
XLA Modules:
  0.0 493.2 jit_solution(13353196676988205239)
XLA Ops:
  7.6 4.8 select_reduce_fusion
  12.4 3.9 all_to_all.32
  17.0 15.5 %reduce.7 = bf16[8,147456]{1,0:T(8,128)(2,1)S(1)} reduce(bf16[8,1,147456]{2,1,0:T(2,128)(2,1)} %all_to_all.32, bf16[]{:T(256)} %broadcast.258), dimensions={1}, to_apply=%all_to_all.32.reduce_sub_computation | reduce | bytes 4718594 | tf_op jit(solution)/shard_map/all_to_all | solution.py:107
  36.0 6.3 %all-to-all-start.2 = ((bf16[8,2,73728]{2,1,0:T(2,128)(2,1)}), bf16[8,2,73728]{2,1,0:T(2,128)(2,1)S(1)}, u32[]{:S(2)}, u32[]{:S(2)}) async-start(bf16[8,2,73728]{2,1,0:T(2,128)(2,1)} %reshape.319), calls=%async_computation.3 | async-start | bytes 4718592 | tf_op jit(solution)/shard_map/all_to_all | solution.py:107
  53.5 9.3 %fusion.94 = (f32[2,8,128]{2,1,0:T(8,128)}, f32[2,8,128,1152]{2,3,1,0:T(8,128)}) fusion(pred[128,1152]{0,1:T(8,128)(4,1)} %fusion.61, bf16[128,2,8,128]{3,2,1,0:T(8,128)(2,1)S(1)} %bitcast.180, bf16[64,2,128]{2,0,1:T(8,128)(2,1)S(1)} %get-tuple-element.35, bf16[64,2,128]{2,0,1:T(8,128)(2,1)} %get-tuple-element.36, bf16[1024,2,128]{2,0,1:T(8,128)(2,1)} %copy.102), kind=kOutput, calls=%fused_computation.146 | convolution fusion | flops 617546880 | bytes 10706944 | tf_op jit(solution)/shard_map/sub | solution.py:45
  62.7 86.7 %all-to-all-done.2 = bf16[8,2,73728]{2,1,0:T(2,128)(2,1)S(1)} async-done(((bf16[8,2,73728]{2,1,0:T(2,128)(2,1)}), bf16[8,2,73728]{2,1,0:T(2,128)(2,1)S(1)}, u32[]{:S(2)}, u32[]{:S(2)}) %all-to-all-start.2) | async-done | bytes 2359328 | tf_op jit(solution)/shard_map/all_to_all | solution.py:107
  149.4 4.6 reshape.320
  154.0 5.5 %copy.171 = bf16[8,1,147456]{2,0,1:T(8,128)(2,1)S(1)} copy(bf16[8,1,147456]{2,1,0:T(2,128)(2,1)} %reshape.320) | data formatting | bytes 4718592
  170.6 5.2 %reshape.321 = bf16[8,2,73728]{2,1,0:T(2,128)(2,1)} reshape(bf16[8,147456]{1,0:T(8,128)(2,1)} %reduce.8) | data formatting | bytes 4718592
  175.8 6.1 %all-to-all-start.3 = ((bf16[8,2,73728]{2,1,0:T(2,128)(2,1)}), bf16[8,2,73728]{2,1,0:T(2,128)(2,1)S(1)}, u32[]{:S(2)}, u32[]{:S(2)}) async-start(bf16[8,2,73728]{2,1,0:T(2,128)(2,1)} %reshape.321), calls=%async_computation.4 | async-start | bytes 4718592 | tf_op jit(solution)/shard_map/all_to_all | solution.py:113
  184.9 4.6 fusion.45
  189.6 5.5 %convolution_convert_fusion = bf16[128,2048]{1,0:T(8,128)(2,1)} fusion(bf16[128,2048]{0,1:T(8,128)(2,1)S(1)} %bitcast.178, bf16[2048,2048]{1,0:T(8,128)(2,1)} %all-gather.2.cloned.1.call-done), kind=kOutput, calls=%fused_computation.23 | convolution fusion | flops 1074003968 | bytes 9437184 | tf_op jit(solution)/shard_map/dot_general | solution.py:143
  195.8 15.4 %reduce-scatter.2.cloned.1.call-done = bf16[128,1024]{1,0:T(8,128)(2,1)} async-done(((bf16[128,2048]{1,0:T(8,128)(2,1)}), bf16[128,1024]{1,0:T(8,128)(2,1)}) %reduce-scatter.2.cloned.1.call-update) | async-done | bytes 262160 | tf_op jit(solution)/shard_map/reduce_scatter | solution.py:148
  212.3 4.9 %psum.28 = f32[128]{0:T(128)S(1)} all-reduce(f32[128]{0:T(128)S(1)} %get-tuple-element.13), channel_id=1, replica_groups=mesh['rep'=2,'ep'=8,'tp'=2] {'tp'}, use_global_device_ids=true, to_apply=%region_4.5 | all-reduce | flops 128 | bytes 1024 | tf_op jit(solution)/shard_map/psum | solution.py:155
  217.4 3.9 scatter_custom_fusion
  221.3 15.2 %all-to-all-done.3 = bf16[8,2,73728]{2,1,0:T(2,128)(2,1)S(1)} async-done(((bf16[8,2,73728]{2,1,0:T(2,128)(2,1)}), bf16[8,2,73728]{2,1,0:T(2,128)(2,1)S(1)}, u32[]{:S(2)}, u32[]{:S(2)}) %all-to-all-start.3) | async-done | bytes 2359328 | tf_op jit(solution)/shard_map/all_to_all | solution.py:113
  236.6 4.3 all-to-all-start
  241.1 3.8 scatter_custom_fusion.1
  244.9 33.8 %all-to-all-done = bf16[8,2,48,1024]{3,2,1,0:T(8,128)(2,1)} async-done(((bf16[8,2,48,1024]{3,2,1,0:T(8,128)(2,1)}), bf16[8,2,48,1024]{3,2,1,0:T(8,128)(2,1)}, u32[]{:S(2)}, u32[]{:S(2)}) %all-to-all-start) | async-done | bytes 1572896 | tf_op jit(solution)/shard_map/all_to_all | solution.py:89
  278.7 4.3 all-to-all-start.4
  283.3 4.6 reshape.322
  287.9 14.8 %reduce.4 = bf16[8,147456]{1,0:T(8,128)(2,1)S(1)} reduce(bf16[8,1,147456]{2,1,0:T(2,128)(2,1)} %reshape.322, bf16[]{:T(256)} %constant.67), dimensions={1}, to_apply=%all_to_all.29.reduce_sub_computation | reduce | bytes 4718594 | tf_op jit(solution)/shard_map/all_to_all | solution.py:113
  305.3 6.0 %broadcast_select_fusion = bf16[2,3,1024,384]{3,2,1,0:T(8,128)(2,1)} fusion(bf16[2,3,1024,384]{3,2,1,0:T(8,128)(2,1)} %param.19, pred[2]{0:T(512)(128)(4,1)S(1)} %get-tuple-element.8, bf16[3,1024,384]{2,1,0:T(8,128)(2,1)} %broadcast_in_dim.207), kind=kLoop, calls=%fused_computation.14 | loop fusion | flops 2359296 | bytes 11796482 | tf_op jit(solution)/shard_map/jit(_where)/select_n | solution.py:115
  311.3 3.8 fusion.33
  315.1 5.7 %all-to-all-done.4 = bf16[8,2,48,1024]{3,2,1,0:T(8,128)(2,1)} async-done(((bf16[8,2,48,1024]{3,2,1,0:T(8,128)(2,1)}), bf16[8,2,48,1024]{3,2,1,0:T(8,128)(2,1)}, u32[]{:S(2)}, u32[]{:S(2)}) %all-to-all-start.4) | async-done | bytes 1572896 | tf_op jit(solution)/shard_map/all_to_all | solution.py:89
  320.8 4.8 fusion.38
  325.6 67.8 %all-reduce.3.cloned.1.call-done = (bf16[8,2,48,2,384]{4,2,0,1,3:T(8,128)(2,1)}, bf16[8,2,48,2,384]{4,2,3,0,1:T(8,128)(2,1)}) async-done(((bf16[8,2,48,2,384]{4,2,0,1,3:T(8,128)(2,1)}, bf16[8,2,48,2,384]{4,2,3,0,1:T(8,128)(2,1)}), (bf16[8,2,48,2,384]{4,2,0,1,3:T(8,128)(2,1)}, bf16[8,2,48,2,384]{4,2,3,0,1:T(8,128)(2,1)})) %all-reduce.3.cloned.1.call-update) | async-done | bytes 2359312 | tf_op jit(solution)/shard_map/psum | solution.py:60
  398.7 4.7 all-to-all-start.5
  407.5 33.8 %all-to-all-done.5 = bf16[8,2,48,1024]{3,2,1,0:T(8,128)(2,1)S(1)} async-done(((bf16[8,2,48,1024]{3,2,1,0:T(8,128)(2,1)}), bf16[8,2,48,1024]{3,2,1,0:T(8,128)(2,1)S(1)}, u32[]{:S(2)}, u32[]{:S(2)}) %all-to-all-start.5) | async-done | bytes 1572896 | tf_op jit(solution)/shard_map/all_to_all | solution.py:65
  441.2 3.6 all-to-all-start.1
  445.1 5.2 %psum.29 = bf16[128,16]{0,1:T(8,128)(2,1)S(1)} all-reduce(bf16[128,16]{0,1:T(8,128)(2,1)S(1)} %convolution_convert_fusion.3), channel_id=1, replica_groups=mesh['rep'=2,'ep'=8,'tp'=2] {'tp'}, use_global_device_ids=true, to_apply=%region_5.6 | all-reduce | flops 2048 | bytes 8192 | tf_op jit(solution)/shard_map/psum | solution.py:157
  455.4 27.2 %all-to-all-done.1 = bf16[8,2,48,1024]{3,2,1,0:T(8,128)(2,1)S(1)} async-done(((bf16[8,2,48,1024]{3,2,1,0:T(8,128)(2,1)}), bf16[8,2,48,1024]{3,2,1,0:T(8,128)(2,1)S(1)}, u32[]{:S(2)}, u32[]{:S(2)}) %all-to-all-start.1) | async-done | bytes 1572896 | tf_op jit(solution)/shard_map/all_to_all | solution.py:65
  (104 shorter events, 52.7 us)
Async XLA Ops:
  6.5 438.4 %copy-start = (bf16[1024,16]{0,1:T(8,128)(2,1)S(1)}, bf16[1024,16]{0,1:T(8,128)(2,1)}, u32[]{:S(2)}) copy-start(bf16[1024,16]{0,1:T(8,128)(2,1)} %param.18) | copy-start | bytes 98308
  36.0 113.5 %all-to-all-start.2 = ((bf16[8,2,73728]{2,1,0:T(2,128)(2,1)}), bf16[8,2,73728]{2,1,0:T(2,128)(2,1)S(1)}, u32[]{:S(2)}, u32[]{:S(2)}) async-start(bf16[8,2,73728]{2,1,0:T(2,128)(2,1)} %reshape.319), calls=%async_computation.3 | async-start | bytes 4718592 | tf_op jit(solution)/shard_map/all_to_all | solution.py:107
  42.3 147.2 %all-gather.2.cloned.1.call-start = ((), (), s32[]{:S(2)}) async-start(), calls=%async_computation.7 | async-start | bytes 9437184 | tf_op jit(solution)/shard_map/all_gather | solution.py:145
  175.8 6.4 %copy-start.6 = (s32[2,64,8]{1,2,0:T(8,128)S(1)}, s32[2,64,8]{1,2,0:T(8,128)}, u32[]{:S(2)}) copy-start(s32[2,64,8]{1,2,0:T(8,128)} %param.20) | copy-start | bytes 12292
  175.8 6.4 %copy-start.4 = (bf16[1,64,1,256]{3,2,1,0:T(2,128)(2,1)S(1)}, bf16[1,64,1,256]{3,2,1,0:T(2,128)(2,1)}, u32[]{:S(2)}) copy-start(bf16[1,64,1,256]{3,2,1,0:T(2,128)(2,1)} %get-tuple-element.24) | copy-start | bytes 98308
  175.8 60.8 %all-to-all-start.3 = ((bf16[8,2,73728]{2,1,0:T(2,128)(2,1)}), bf16[8,2,73728]{2,1,0:T(2,128)(2,1)S(1)}, u32[]{:S(2)}, u32[]{:S(2)}) async-start(bf16[8,2,73728]{2,1,0:T(2,128)(2,1)} %reshape.321), calls=%async_computation.4 | async-start | bytes 4718592 | tf_op jit(solution)/shard_map/all_to_all | solution.py:113
  181.9 3.0 copy-start.9
  181.9 29.3 %reduce-scatter.2.cloned.1.call-start = ((), (), s32[]{:S(2)}) async-start(), calls=%async_computation.8 | async-start | bytes 786432 | tf_op jit(solution)/shard_map/reduce_scatter | solution.py:148
  189.5 5.9 %copy-start.7 = (s32[16]{0:T(128)S(1)}, s32[16]{0:T(128)}, u32[]{:S(2)}) copy-start(s32[16]{0:T(128)} %param.22) | copy-start | bytes 196
  189.5 5.9 %copy-start.8 = (s32[16]{0:T(128)S(1)}, s32[16]{0:T(128)}, u32[]{:S(2)}) copy-start(s32[16]{0:T(128)} %param.21) | copy-start | bytes 196
  189.6 21.7 %copy-start.5 = (bf16[2,64,1024]{2,1,0:T(8,128)(2,1)S(1)}, bf16[2,64,1024]{2,1,0:T(8,128)(2,1)}, u32[]{:S(2)}) copy-start(bf16[2,64,1024]{2,1,0:T(8,128)(2,1)} %param.12) | copy-start | bytes 786436
  212.3 24.2 %copy-start.1 = (bf16[128,1024]{1,0:T(8,128)(2,1)}, bf16[128,1024]{1,0:T(8,128)(2,1)S(1)}, u32[]{:S(2)}) copy-start(bf16[128,1024]{1,0:T(8,128)(2,1)S(1)} %get-tuple-element.14) | copy-start | bytes 786436
  236.6 42.1 %all-to-all-start = ((bf16[8,2,48,1024]{3,2,1,0:T(8,128)(2,1)}), bf16[8,2,48,1024]{3,2,1,0:T(8,128)(2,1)}, u32[]{:S(2)}, u32[]{:S(2)}) async-start(bf16[8,2,48,1024]{3,2,1,0:T(8,128)(2,1)} %bitcast.175), calls=%async_computation.1 | async-start | bytes 3145728 | tf_op jit(solution)/shard_map/all_to_all | solution.py:89
  278.7 42.1 %all-to-all-start.4 = ((bf16[8,2,48,1024]{3,2,1,0:T(8,128)(2,1)}), bf16[8,2,48,1024]{3,2,1,0:T(8,128)(2,1)}, u32[]{:S(2)}, u32[]{:S(2)}) async-start(bf16[8,2,48,1024]{3,2,1,0:T(8,128)(2,1)} %bitcast.174), calls=%async_computation.5 | async-start | bytes 3145728 | tf_op jit(solution)/shard_map/all_to_all | solution.py:89
  283.0 110.4 %all-reduce.3.cloned.1.call-start = ((), (), s32[]{:S(2)}) async-start(), calls=%async_computation.9 | async-start | bytes 4718592 | tf_op jit(solution)/shard_map/psum | solution.py:60
  302.8 8.5 %slice-start = ((s8[4718592]{0:T(1024)(128)(4,1)}), s8[524288]{0:T(1024)(128)(4,1)S(1)}, s32[]{:S(2)}) async-start(s8[4718592]{0:T(1024)(128)(4,1)} %bitcast.171), calls=%async_computation.10 | async-start | bytes 1048576
  305.3 6.0 %slice-start.1 = ((s8[4718592]{0:T(1024)(128)(4,1)}), s8[4194304]{0:T(1024)(128)(4,1)S(1)}, s32[]{:S(2)}) async-start(s8[4718592]{0:T(1024)(128)(4,1)} %bitcast.171), calls=%async_computation.11 | async-start | bytes 8388608
  398.7 4.7 copy-start.3
  398.7 42.6 %all-to-all-start.5 = ((bf16[8,2,48,1024]{3,2,1,0:T(8,128)(2,1)}), bf16[8,2,48,1024]{3,2,1,0:T(8,128)(2,1)S(1)}, u32[]{:S(2)}, u32[]{:S(2)}) async-start(bf16[8,2,48,1024]{3,2,1,0:T(8,128)(2,1)} %copy.120), calls=%async_computation.6 | async-start | bytes 3145728 | tf_op jit(solution)/shard_map/all_to_all | solution.py:65
  441.2 41.3 %all-to-all-start.1 = ((bf16[8,2,48,1024]{3,2,1,0:T(8,128)(2,1)}), bf16[8,2,48,1024]{3,2,1,0:T(8,128)(2,1)S(1)}, u32[]{:S(2)}, u32[]{:S(2)}) async-start(bf16[8,2,48,1024]{3,2,1,0:T(8,128)(2,1)} %copy.113), calls=%async_computation.2 | async-start | bytes 3145728 | tf_op jit(solution)/shard_map/all_to_all | solution.py:65
  482.6 2.8 copy-start.2
Sparse Core Ops, SparseCore 0:
  44.7 121.8 all-gather.1
  195.2 15.9 reduce-scatter.1
  325.7 67.6 all-reduce.2
where the time goes:
time: 500 us; the launch traced here: 493 us
  waiting for transfers between devices  286 us (57%)
  local copies, waits for them, and re-layouts  61.8 us (12%)
  other arithmetic  56.9 us (11%)
  matrix products  33.3 us (7%)
  starting transfers between devices  30 us (6%)
  between operations  14.7 us (3%)
  blocking collectives  10.2 us (2%)
    all_to_all x1, waiting for transfers between devices, relocate(): lax.all_to_all(outgoing, 'ep', split_axis=0, concat_axis=0, tiled=True)  86.7 us
    psum x1, waiting for transfers between devices, run_slots(): summed = lax.psum(gate_up.astype(jnp.bfloat16), 'tp').astype(jnp.float32)  67.8 us
    all_to_all x2, waiting for transfers between devices, run_slots(): lax.all_to_all(layer_result, 'ep', split_axis=0, concat_axis=0, tiled=True)  61 us
    all_to_all x2, waiting for transfers between devices, mix_block(): lax.all_to_all(outgoing, 'ep', split_axis=0, concat_axis=0, tiled=True)  39.5 us
    unnamed x32, local copies, waits for them, and re-layouts  25.8 us
    all_to_all x1, other arithmetic, relocate(): lax.all_to_all(outgoing, 'ep', split_axis=0, concat_axis=0, tiled=True)  15.5 us
    reduce_scatter x1, waiting for transfers between devices, per_device(): lax.psum_scatter(head_terms.astype(jnp.bfloat16), 'tp', scatter_dimension...  15.4 us
    all_to_all x1, waiting for transfers between devices, relocate(): lax.all_to_all(picked, 'ep', split_axis=0, concat_axis=0, tiled=True)  15.2 us
  transfers between devices with their start and end apart: 9, of which 8 were waited for; matrix products, arithmetic and copies ran while one was open for 22% of the time, Pallas kernels for 0%

commit v1 on v0

v1 whole, which is shorter than its diff:
```python
import functools
import math

import jax
import jax.numpy as jnp
from jax import lax
from jax.experimental import pallas as pl
from jax.experimental.pallas import tpu as pltpu
from jax.sharding import PartitionSpec as P

HEAD_SIZE = 128
LANES = 128
CORES = 2
MIB = 1 << 20
BF16 = jnp.bfloat16
F32 = jnp.float32
COST = pl.CostEstimate(flops=1000, bytes_accessed=1000, transcendentals=0)


def whole():
    return pl.BlockSpec(memory_space=pltpu.VMEM)


def scalars():
    return pl.BlockSpec(memory_space=pltpu.SMEM)


def unplaced():
    return pl.BlockSpec(memory_space=pl.ANY)


def params(mib):
    return pltpu.CompilerParams(vmem_limit_bytes=mib * MIB)


def after(array, earlier):
    return lax.optimization_barrier((array, earlier))[0]


def lookup(entries, wanted_keys):
    return jnp.sum(
        jnp.where(
            wanted_keys[..., None] == jnp.arange(entries.shape[0], dtype=jnp.int32), entries, 0
        ),
        -1,
    )


def slot_tables(old_slots, new_slots, moved_experts):
    slots_all = jnp.arange(old_slots.shape[0], dtype=jnp.int32)
    old_moved = lookup(old_slots, moved_experts)
    new_moved = lookup(new_slots, moved_experts)
    matches = slots_all[:, None] == new_moved[None, :]
    source = jnp.where(
        matches.any(1), jnp.sum(jnp.where(matches, old_moved[None, :], 0), 1), slots_all
    )
    return jnp.stack([old_slots, lookup(source, new_slots)])


def attention_kernel(groups, length_ref, q_ref, cache_ref, fresh_ref, out_ref):
    tokens, width = q_ref.shape[1], q_ref.shape[2]
    rows = 2 * tokens
    context = cache_ref.shape[2]
    heads = width // HEAD_SIZE // groups
    fresh_width = fresh_ref.shape[1] // 2
    length = length_ref[0]
    scale = HEAD_SIZE ** (-0.5) * 1.4426950408889634
    past = lax.broadcasted_iota(jnp.int32, (1, context), 1)
    past_bias = jnp.where(past < length, F32(0.0), F32(-1e30))
    fresh_seen = lax.broadcasted_iota(jnp.int32, (rows, rows), 1) <= (
        lax.broadcasted_iota(jnp.int32, (rows, rows), 0)
    )
    fresh_bias = jnp.where(fresh_seen, F32(0.0), F32(-1e30))
    batch = min(4, heads)
    contract_last = (((1,), (1,)), ((), ()))
    for g in range(groups):
        lanes = pl.ds(g * HEAD_SIZE, HEAD_SIZE)
        past_keys = cache_ref[0, 0, :, lanes]
        past_values = cache_ref[0, 1, :, lanes]
        fresh_keys = fresh_ref[:, lanes]
        fresh_values = fresh_ref[:, pl.ds(fresh_width + g * HEAD_SIZE, HEAD_SIZE)]
        for first in range(0, heads, batch):
            columns = [(g * heads + first + h) * HEAD_SIZE for h in range(batch)]
            q = jnp.concatenate(
                [q_ref[:, :, pl.ds(at, HEAD_SIZE)].reshape(rows, HEAD_SIZE) for at in columns], 0
            )
            past_scores = lax.dot_general(
                q, past_keys, contract_last, preferred_element_type=F32
            ) + past_bias
            fresh_scores = lax.dot_general(
                q, fresh_keys, contract_last, preferred_element_type=F32
            )
            fresh_scores = (
                fresh_scores.reshape(batch, rows, rows) + fresh_bias[None]
            ).reshape(batch * rows, rows)
            largest = jnp.maximum(
                jnp.max(past_scores, 1, keepdims=True), jnp.max(fresh_scores, 1, keepdims=True)
            )
            past_weights = jnp.exp2((past_scores - largest) * scale)
            fresh_weights = jnp.exp2((fresh_scores - largest) * scale)
            total = jnp.sum(past_weights, 1, keepdims=True) + jnp.sum(
                fresh_weights, 1, keepdims=True
            )
            result = jnp.dot(
                past_weights.astype(BF16), past_values, preferred_element_type=F32
            ) + jnp.dot(fresh_weights.astype(BF16), fresh_values, preferred_element_type=F32)
            result = (result / total).astype(BF16)
            for h, at in enumerate(columns):
                out_ref[:, pl.ds(at, HEAD_SIZE)] = result[h * rows : (h + 1) * rows]


def attend(lengths, queries, cache, fresh):
    rows = 2 * queries.shape[1]
    return pl.pallas_call(
        functools.partial(attention_kernel, cache.shape[3] // HEAD_SIZE),
        out_shape=jax.ShapeDtypeStruct((rows, queries.shape[2]), BF16),
        in_specs=[scalars(), whole(), whole(), whole()],
        out_specs=whole(),
        compiler_params=params(40),
        cost_estimate=COST,
        name="attention",
    )(lengths, queries, cache, fresh)


def project_kernel(n_tp, place_ref, *refs):
    t, z_hi = place_ref[0], place_ref[5]
    pieces, weights, out_ref = refs[:n_tp], refs[n_tp:-1], refs[-1]
    chunk = pieces[0].shape[0] // n_tp
    rows = []
    for dt in range(n_tp):
        row = pl.multiple_of(lax.rem(t + dt, n_tp) * chunk, chunk)
        rows += [piece[pl.ds(row, chunk), :] for piece in pieces]
    rows = jnp.concatenate(rows, 0)
    at = 0
    for weight in weights:
        span = weight.shape[1]
        out_ref[:, pl.ds(at, span)] = jnp.dot(rows, weight[...], preferred_element_type=F32)
        at += span


def project(n_tp, place, pieces, weights):
    rows = pieces[0].shape[0] // n_tp * len(pieces) * n_tp
    columns = sum(weight.shape[1] for weight in weights)
    return pl.pallas_call(
        functools.partial(project_kernel, n_tp),
        out_shape=jax.ShapeDtypeStruct((rows, columns), F32),
        in_specs=[scalars()] + [whole()] * (len(pieces) + len(weights)),
        out_specs=whole(),
        compiler_params=params(24),
        cost_estimate=COST,
        name="out_projection",
    )(place, *pieces, *weights)


def finish_kernel(n_tp, spans, place_ref, router_ref, *refs):
    t, core, z_lo, z_hi = place_ref[0], place_ref[2], place_ref[4], place_ref[5]
    pieces, refs = refs[:n_tp], refs[n_tp:]
    weight, early, outs = refs[0], refs[1:-n_tp], refs[-n_tp:]
    chunk = pieces[0].shape[0] // n_tp
    rows = []
    for dt in range(n_tp):
        row = pl.multiple_of(lax.rem(t + dt, n_tp) * chunk, chunk)
        rows += [piece[pl.ds(row, chunk), :] for piece in pieces]
    terms = jnp.dot(jnp.concatenate(rows, 0), weight[...], preferred_element_type=F32)
    for out in outs[1:]:
        out[pl.ds(n_tp * chunk, router_ref.shape[0]), :] = router_ref[...]
    span = weight.shape[1]
    for n in range(spans):
        column = 0
        if spans > 1:
            number = ((z_lo ^ (n // CORES)) * CORES) + (core ^ (n % CORES))
            column = pl.multiple_of(number * span, span)
        for i in range(n_tp * n_tp):
            block = pl.ds(i * chunk, chunk)
            if n + 1 == spans:
                value = terms[i * chunk : (i + 1) * chunk]
            else:
                value = early[0][block, pl.ds(n * span, span)]
            dt, dh = i // n_tp, i % n_tp
            at = pl.multiple_of((z_hi ^ dh) * chunk, chunk)
            outs[dt][pl.ds(at, chunk), pl.ds(column, span)] = value.astype(outs[dt].dtype)


def finish(n_tp, place, router, pieces, weight, early):
    columns = weight.shape[1] + sum(array.shape[1] for array in early)
    spans = columns // weight.shape[1]
    rows = pieces[0].shape[0]
    return pl.pallas_call(
        functools.partial(finish_kernel, n_tp, spans),
        out_shape=[jax.ShapeDtypeStruct((rows, columns), F32)]
        + [jax.ShapeDtypeStruct((rows + router.shape[0], columns), BF16)] * (n_tp - 1),
        in_specs=[scalars()] + [whole()] * (2 + len(pieces) + len(early)),
        out_specs=[whole()] * n_tp,
        compiler_params=params(24),
        cost_estimate=COST,
        name="finish_projection",
    )(place, router, *pieces, weight, *early)


def residual_kernel(n_tp, place_ref, keep_ref, *refs):
    t = place_ref[0]
    terms, hidden, out_ref, marked_ref = refs[: n_tp - 1], refs[n_tp - 1 : -2], refs[-2], refs[-1]
    chunk, columns = hidden[0].shape[0], keep_ref.shape[1]
    for beta, piece in enumerate(hidden):
        rows = pl.ds(pl.multiple_of(lax.rem(t - beta + n_tp, n_tp) * chunk, chunk), chunk)
        total = keep_ref[rows, :]
        for term in terms:
            total = total + term[rows, :].astype(F32)
        total = (piece[:, pl.ds(0, columns)].astype(F32) + total).astype(BF16)
        out_ref[rows, :] = total
        marked_ref[rows, pl.ds(0, columns)] = total
        lanes = pl.ds(columns, piece.shape[1] - columns)
        marked_ref[rows, lanes] = piece[:, lanes]


def add_residual(n_tp, place, keep, terms, hidden):
    marked = (keep.shape[0], hidden[0].shape[1])
    return pl.pallas_call(
        functools.partial(residual_kernel, n_tp),
        out_shape=[jax.ShapeDtypeStruct(keep.shape, BF16), jax.ShapeDtypeStruct(marked, BF16)],
        in_specs=[scalars()] + [whole()] * (1 + len(terms) + len(hidden)),
        out_specs=[whole()] * 2,
        compiler_params=params(16),
        cost_estimate=COST,
        name="residual",
    )(place, keep, *terms, *hidden)


def units_kernel(n_tp, n_z, n_rep, place_ref, table_ref, *refs):
    t, z, core, rep = place_ref[0], place_ref[1], place_ref[2], place_ref[3]
    z_lo, z_hi = place_ref[4], place_ref[5]
    m = n_z // n_tp
    routers, pieces, refs = refs[:n_tp], refs[n_tp : n_tp + n_z], refs[n_tp + n_z :]
    own_refs, refs = refs[:CORES], refs[CORES:]
    n_far = CORES * (n_tp - 1) * n_rep
    far_refs, refs = refs[:n_far], refs[n_far:]
    hidden_ref, resid_ref, *outs = refs[:-6]
    normed, chosen_ref, total, near_held, far_held, sems = refs[-6:]
    local, _, quarter, units = own_refs[0].shape
    tokens, width = resid_ref.shape
    chunk = tokens // n_z
    experts = routers[0].shape[0]
    slots = CORES * local

    arriving, later = [[] for _ in range(slots)], []
    for slot in range(slots):
        other, s = slot // local, slot % local
        sources = [(own_refs[other].at[s, pl.ds(0, 2)], near_held.at[slot, pl.ds(0, 2)])]
        for dt in range(1, n_tp):
            for dy in range(n_rep):
                far = far_refs[((dt - 1) * CORES + other) * n_rep + dy]
                size = far.shape[2]
                row = lax.rem(rep + dy, n_rep) * (quarter - size)
                rows = pl.ds(pl.multiple_of(row, math.gcd(size, quarter - size)), size)
                sources.append((far.at[s], far_held.at[dt - 1, slot, :, rows]))
        for n, (source, target) in enumerate(sources):
            copy = pltpu.make_async_copy(source, target, sems.at[slot, n])
            copy.start()
            arriving[slot].append(copy)
    for slot in range(slots):
        copy = pltpu.make_async_copy(
            own_refs[slot // local].at[slot % local, 2], near_held.at[slot, 2], sems.at[slot, len(sources)]
        )
        copy.start()
        later.append(copy)

    for dz in range(n_z):
        row = pl.multiple_of((z_lo ^ (dz % m)) * (n_tp * chunk), n_tp * chunk)
        column = pl.multiple_of((z_hi ^ (dz // m)) * quarter, quarter)
        rows = pl.ds(row, n_tp * chunk)
        resid_ref[rows, pl.ds(column, quarter)] = pieces[dz][:, pl.ds(0, quarter)]
        if dz < m:
            chosen_ref[rows, :] = pieces[dz][:, pl.ds(quarter, chosen_ref.shape[1])]
    wide = resid_ref[...].astype(F32)
    squares = jnp.sum(wide * wide, 1, keepdims=True)
    normed[...] = (wide * lax.rsqrt(squares / width + 1e-06)).astype(BF16)
    logits = jnp.zeros((tokens, experts), F32)
    for dt, router in enumerate(routers):
        at = pl.multiple_of(lax.rem(t - dt + n_tp, n_tp) * quarter, quarter)
        logits = logits + lax.dot_general(
            normed[:, pl.ds(at, quarter)],
            router[pl.ds(router.shape[0] - experts, experts), :],
            (((1,), (1,)), ((), ())),
            preferred_element_type=F32,
        )
    chosen = chosen_ref[:, :experts].astype(F32)
    raised = jnp.where(chosen > 0, jnp.exp(logits), F32(0.0))
    combine = raised / jnp.sum(raised, 1, keepdims=True)

    for slot in range(slots):
        other, s = slot // local, slot % local
        holder = jnp.where(core == 0, other, 1 - other)
        number = (z * CORES + holder) * local + s
        share_of = jnp.sum(
            jnp.where(table_ref[...] == number, combine, F32(0.0)), 1, keepdims=True
        )
        for copy in arriving[slot]:
            copy.wait()
        x = normed[:, pl.ds(pl.multiple_of(t * quarter, quarter), quarter)]
        gate = jnp.dot(x, near_held[slot, 0], preferred_element_type=F32)
        up = jnp.dot(x, near_held[slot, 1], preferred_element_type=F32)
        for dt in range(1, n_tp):
            at = lax.rem(t - dt + n_tp, n_tp) * quarter
            x = normed[:, pl.ds(pl.multiple_of(at, quarter), quarter)]
            gate = gate + jnp.dot(x, far_held[dt - 1, slot, 0], preferred_element_type=F32)
            up = up + jnp.dot(x, far_held[dt - 1, slot, 1], preferred_element_type=F32)
        acted = (gate / (1.0 + jnp.exp(-gate))) * up
        hidden_ref[:, pl.ds(slot * units, units)] = (acted * share_of).astype(BF16)

    for copy in later:
        copy.wait()
    lower([(near_held, slot, 2) for slot in range(slots)], hidden_ref, total, 0)
    resid_lanes = pl.ds(pl.multiple_of(t * quarter, quarter), quarter)
    for dz in range(n_z):
        rows = token_rows(z_lo, z_hi, dz, m, n_tp, chunk)
        value = total[rows, :]
        if dz == 0:
            value = value + resid_ref[rows, resid_lanes].astype(F32)
        outs[dz][...] = value.astype(outs[dz].dtype)


def token_rows(z_lo, z_hi, dz, m, n_tp, chunk):
    at = (z_lo ^ (dz % m)) * n_tp + (z_hi ^ (dz // m))
    return pl.ds(pl.multiple_of(at * chunk, chunk), chunk)


def lower(down, hidden_ref, total, start):
    units = hidden_ref.shape[1] // len(down)
    width = down[0][0].shape[-2]
    step = min(512, width)
    for at in range(0, width, step):
        part = None
        for i, (ref, *index) in enumerate(down):
            term = lax.dot_general(
                hidden_ref[:, pl.ds(i * units, units)],
                ref[(*index, pl.ds(at, step))],
                (((1,), (1,)), ((), ())),
                preferred_element_type=F32,
            )
            part = term if part is None else part + term
        total[:, pl.ds(pl.multiple_of(start + at, step), step)] = part


def features_kernel(n_tp, n_z, dt, place_ref, hidden_ref, resid_ref, *refs):
    t, z_lo, z_hi = place_ref[0], place_ref[4], place_ref[5]
    m = n_z // n_tp
    sources, outs, (total, held, sems) = refs[:-3][: -n_z], refs[:-3][-n_z:], refs[-3:]
    local = sources[0].shape[0]
    parts = len(sources) // CORES
    quarter = total.shape[1]
    chunk = hidden_ref.shape[0] // n_z
    copies, at = [], 0
    for part in range(parts):
        size = sources[part * CORES].shape[2]
        for other in range(CORES):
            copy = pltpu.make_async_copy(
                sources[part * CORES + other].at[:, 0],
                held.at[pl.ds(other * local, local), pl.ds(at, size), :],
                sems.at[part, other],
            )
            copy.start()
            copies.append((copy, at, size))
        at += size
    for part in range(parts):
        for copy, at, size in copies[part * CORES : (part + 1) * CORES]:
            copy.wait()
        down = [(held.at[:, pl.ds(at, size)], slot) for slot in range(CORES * local)]
        lower(down, hidden_ref, total, at)
    resid_lanes = pl.ds(pl.multiple_of(lax.rem(t - dt + n_tp, n_tp) * quarter, quarter), quarter)
    for dz in range(n_z):
        rows = token_rows(z_lo, z_hi, dz, m, n_tp, chunk)
        value = total[rows, :]
        if dz == 0:
            value = value + resid_ref[rows, resid_lanes].astype(F32)
        outs[dz][...] = value.astype(outs[dz].dtype)


def run_units(n_tp, n_rep, place, table, routers, pieces, weights):
    n_z = len(pieces)
    local, _, quarter, units = weights[0].shape
    width = quarter * n_tp
    lanes = pieces[0].shape[1] - quarter
    tokens = pieces[0].shape[0] * (n_z // n_tp)
    part = (tokens // n_z, quarter)
    slots = CORES * local
    found = pl.pallas_call(
        functools.partial(units_kernel, n_tp, n_z, n_rep),
        out_shape=[
            jax.ShapeDtypeStruct((tokens, CORES * local * units), BF16),
            jax.ShapeDtypeStruct((tokens, width), BF16),
        ]
        + [jax.ShapeDtypeStruct(part, BF16 if dz else F32) for dz in range(n_z)],
        in_specs=[scalars()]
        + [whole()] * (1 + n_tp + len(pieces))
        + [unplaced()] * len(weights),
        out_specs=[whole()] * (2 + n_z),
        scratch_shapes=[
            pltpu.VMEM((tokens, width), BF16),
            pltpu.VMEM((tokens, lanes), BF16),
            pltpu.VMEM((tokens, quarter), F32),
            pltpu.VMEM((slots, 3, quarter, units), BF16),
            pltpu.VMEM((n_tp - 1, slots, 2, quarter, units), BF16),
            pltpu.SemaphoreType.DMA((slots, 2 + (n_tp - 1) * n_rep)),
        ],
        compiler_params=params(56),
        cost_estimate=COST,
        name="units",
    )(place, table, *routers, *pieces, *weights)
    return found[0], found[1], found[2:]


def run_features(n_tp, n_z, dt, place, hidden, resid, quarter, weights):
    tokens = hidden.shape[0]
    local = weights[0].shape[0]
    part = (tokens // n_z, quarter)
    return pl.pallas_call(
        functools.partial(features_kernel, n_tp, n_z, dt),
        out_shape=[jax.ShapeDtypeStruct(part, BF16)] * n_z,
        in_specs=[scalars()] + [whole()] * 2 + [unplaced()] * len(weights),
        out_specs=[whole()] * n_z,
        scratch_shapes=[
            pltpu.VMEM((tokens, quarter), F32),
            pltpu.VMEM((CORES * local, quarter, hidden.shape[1] // (CORES * local)), BF16),
            pltpu.SemaphoreType.DMA((len(weights) // CORES, CORES)),
        ],
        compiler_params=params(56),
        cost_estimate=COST,
        name="features",
    )(place, hidden, resid, *weights)


def message_kernel(n_tp, place_ref, hidden_ref, ids_ref, *outs):
    z_hi = place_ref[5]
    chunk, lanes = outs[0].shape[0], outs[0].shape[1] - hidden_ref.shape[1]
    experts = lax.broadcasted_iota(jnp.int32, (chunk, lanes), 1)
    for beta, out_ref in enumerate(outs):
        rows = pl.ds(pl.multiple_of(lax.rem(z_hi + beta, n_tp) * chunk, chunk), chunk)
        ids = ids_ref[rows, :]
        found = jnp.zeros((chunk, lanes), F32)
        for k in range(ids.shape[1]):
            found = found + jnp.where(ids[:, k : k + 1] == experts, F32(1.0), F32(0.0))
        out_ref[:, pl.ds(0, hidden_ref.shape[1])] = hidden_ref[rows, :]
        out_ref[:, pl.ds(hidden_ref.shape[1], lanes)] = found.astype(BF16)


def messages(n_tp, place, hidden, ids, experts):
    shape = (ids.shape[0] // n_tp, hidden.shape[1] + experts + -experts % LANES)
    return pl.pallas_call(
        functools.partial(message_kernel, n_tp),
        out_shape=[jax.ShapeDtypeStruct(shape, BF16)] * n_tp,
        in_specs=[scalars(), whole(), whole()],
        out_specs=[whole()] * n_tp,
        compiler_params=params(16),
        cost_estimate=COST,
        name="messages",
    )(place, hidden, ids)


def mix_kernel(n_tp, n_z, place_ref, *refs):
    t = place_ref[0]
    parts, out_ref = refs[:-1], refs[-1]
    chunk = parts[0].shape[0]
    for dt in range(n_tp):
        value = parts[dt * n_z][...].astype(F32)
        for dz in range(1, n_z):
            value = value + parts[dt * n_z + dz][...].astype(F32)
        row = pl.multiple_of(lax.rem(t + dt, n_tp) * chunk, chunk)
        out_ref[pl.ds(row, chunk), :] = value.astype(BF16)


def mix(n_tp, n_z, place, parts):
    chunk, span = parts[0].shape
    return pl.pallas_call(
        functools.partial(mix_kernel, n_tp, n_z),
        out_shape=jax.ShapeDtypeStruct((chunk * n_tp, span), BF16),
        in_specs=[scalars()] + [whole()] * len(parts),
        out_specs=whole(),
        compiler_params=params(16),
        cost_estimate=COST,
        name="mix",
    )(place, *parts)


def per_device(
    hidden_states,
    queries,
    fresh_key_value,
    cache,
    cache_lengths,
    out_weight,
    router_weight,
    expert_weights,
    expert_ids,
    old_slots,
    new_slots,
    moved_experts,
):
    n_tp, n_ep, n_rep = lax.axis_size("tp"), lax.axis_size("ep"), lax.axis_size("rep")
    n_z = n_ep // CORES
    m = n_z // n_tp
    tokens, quarter = hidden_states.shape[1:]
    rows = 2 * tokens
    chunk = rows // n_tp
    experts = router_weight.shape[1]
    t, e, y = lax.axis_index("tp"), lax.axis_index("ep"), lax.axis_index("rep")
    z, core = e // CORES, e % CORES
    z_hi, z_lo = z // m, z % m
    place = jnp.stack([t, z, core, y, z_lo, z_hi]).astype(jnp.int32)

    def send(array, target):
        pairs = []
        for i in range(n_ep):
            for k in range(n_tp):
                to_ep, to_tp = target(i, k)
                pairs.append((i * n_tp + k, to_ep * n_tp + to_tp % n_tp))
        return lax.ppermute(array, ("ep", "tp"), pairs)

    def to_core(array):
        return lax.ppermute(array, "ep", [(i, i ^ 1) for i in range(n_ep)])

    def to_tp(array, shift):
        return lax.ppermute(array, "tp", [(i, (i + shift) % n_tp) for i in range(n_tp)])

    def to_rep(array, shift):
        return lax.ppermute(array, "rep", [(i, (i + shift) % n_rep) for i in range(n_rep)])

    def to_z(array, dz, dt=0):
        return send(array, lambda i, k: (i ^ (dz * CORES), k + dt))

    def over_z(array, low, high):
        found = {0: array}
        for dz in range(low, high, low):
            step = low
            while not dz & step:
                step *= 2
            found[dz] = to_z(found[dz ^ step], step)
        return [found[dz] for dz in range(0, high, low)]

    def block_of(array, matrices, first_row, size):
        first, last = matrices
        return lax.dynamic_slice(
            array, (0, first, first_row, 0), (array.shape[0], last - first, size, array.shape[3])
        )

    def far(block):
        return [send(block, lambda i, k: (i ^ 1, k + dt)) for dt in range(1, n_tp)]

    near = over_z(out_weight, 1, m)
    out_other = to_core(out_weight)
    share = quarter // n_rep - quarter // 32
    first = far(block_of(expert_weights, (0, 2), y * share, quarter - share))

    queries = after(queries, out_other)
    fresh = fresh_key_value.reshape(rows, -1)
    attention = attend(cache_lengths, queries, cache, fresh)
    pieces = over_z(attention, m, n_z)
    own_other = to_core(expert_weights)
    hidden_states, weights = after((hidden_states, expert_weights), attention)
    outgoing = messages(
        n_tp, place, hidden_states.reshape(rows, quarter), expert_ids.reshape(rows, -1), experts
    )
    blocks = [
        block_of(weights, (2, 3), first * quarter // 4, size * quarter // 4)
        for first, size in ((0, 1), (1, 1), (2, 2))
    ]
    near, old_slots, router, outgoing, blocks, first = after(
        (near, old_slots, router_weight, outgoing, blocks, first), (pieces[1], own_other)
    )
    router = router.T
    tables = slot_tables(old_slots, new_slots, moved_experts)
    table = lax.dynamic_slice_in_dim(tables, t * chunk // tokens, 1, 0)
    crossed = [out_other] + [to_core(array) for array in near[1:]]
    early = [array for pair in zip(near, crossed) for array in pair]
    last = early.pop()
    if out_weight.shape[1] % LANES:
        order = (jnp.arange(m)[:, None] ^ z_lo) * CORES + (jnp.arange(CORES) ^ core)
        together = jnp.stack(early + [last])[order.reshape(-1)]
        last, early = together.transpose(1, 0, 2).reshape(together.shape[1], -1), []
    else:
        early = [project(n_tp, place, pieces, early)]
    hidden = [
        send(
            block,
            lambda i, k: (
                (m * k + (i // CORES) % m) * CORES + i % CORES,
                (i // CORES) // m + beta,
            ),
        )
        for beta, block in enumerate(outgoing)
    ]
    last = after(last, hidden[0])
    sums = finish(n_tp, place, router, pieces, last, early)
    terms = [to_tp(sums[dt], dt) for dt in range(1, n_tp)]
    first_other = [to_core(array) for array in after(first, sums)]
    first = after(first, terms)
    passed = [
        to_rep(lax.dynamic_slice_in_dim(array, y * (quarter - 2 * share), share, 2), 1)
        for array in first
    ]

    resid, marked = add_residual(n_tp, place, sums[0], after(terms, first_other), hidden)
    near = over_z(marked, 1, m)
    wide = to_z(resid, m)
    blocks = after(blocks, resid)
    down = [far(blocks[0])]
    wide, blocks = after((wide, blocks), (wide, near, down))
    down.append(far(blocks[1]))
    gathered = near + [wide]
    for dz in range(m + 1, n_z):
        step = dz & -dz
        gathered.append(to_z(gathered[dz ^ step] if dz ^ step else resid, step))
    gathered, blocks = after((gathered, blocks), (gathered, down))
    down.append(far(blocks[2]))

    passed = after(passed, gathered)
    passed_other = [to_core(array) for array in passed]
    weights = [expert_weights, own_other]
    for dt in range(n_tp - 1):
        weights += [first_other[dt], passed_other[dt], first[dt], passed[dt]]
    units, resid_all, own_parts = run_units(
        n_tp, n_rep, place, table, [router] + terms, gathered, weights
    )
    parts = [own_parts[0]] + [to_z(own_parts[dz], dz) for dz in range(1, n_z)]
    down = after(down, units)
    for dt in range(1, n_tp):
        sources = []
        for arrays in down:
            sources += [to_core(arrays[dt - 1]), arrays[dt - 1]]
        found = run_features(n_tp, n_z, dt, place, units, resid_all, quarter, sources)
        parts += [to_z(found[dz], dz, n_tp - dt) for dz in range(n_z)]
    return mix(n_tp, n_z, place, parts).reshape(2, tokens, quarter)


def solution(mesh):
    return jax.shard_map(
        per_device,
        mesh=mesh,
        in_specs=(
            P(None, ("rep", "ep"), "tp"),
            P(None, ("rep", "ep"), "tp"),
            P(None, ("rep", "ep"), None, "tp"),
            P(("rep", "ep"), None, None, "tp"),
            P(("rep", "ep")),
            P("tp", "ep"),
            P("tp", None),
            P("ep", None, "tp", None),
            P(None, ("rep", "ep"), None),
            P(),
            P(),
            P(),
        ),
        out_specs=P(None, ("rep", "ep"), "tp"),
        check_vma=False,
    )
```

time: 500 us -> 157 us (0.31); the launches traced: 493 us -> 156 us
  waiting for transfers between devices: 286 us -> 68.6 us
  other arithmetic: 56.9 us -> 0.56 us
  local copies, waits for them, and re-layouts: 61.8 us -> 14.5 us
  matrix products: 33.3 us -> 0 us
  Pallas kernels: 0 us -> 26.4 us
  starting transfers between devices: 30 us -> 45.4 us
  between operations: 14.7 us -> 0.93 us
  blocking collectives: 10.2 us -> 0 us
    all_to_all x6 -> x0, waiting for transfers between devices: 202 us -> none  [the longest x1 86.7 us: relocate(): lax.all_to_all(outgoing, 'ep', split_axis=0, concat_axis=0, tiled=True)]
    ppermute x0 -> x28, waiting for transfers between devices: none -> 68.6 us  [the longest x18 59.2 us: send(): return lax.ppermute(array, ('ep', 'tp'), pairs)]
    psum x1 -> x0, waiting for transfers between devices: 67.8 us -> none  [run_slots(): summed = lax.psum(gate_up.astype(jnp.bfloat16), 'tp').astype(jnp.float32)]
    ppermute x0 -> x28, starting transfers between devices: none -> 45.4 us  [the longest x18 30.5 us: send(): return lax.ppermute(array, ('ep', 'tp'), pairs)]
    all_to_all x2 -> x0, other arithmetic: 30.3 us -> none  [the longest x1 15.5 us: relocate(): lax.all_to_all(outgoing, 'ep', split_axis=0, concat_axis=0, tiled=True)]
    all_to_all x6 -> x0, starting transfers between devices: 29.4 us -> none  [the longest x2 8.6 us: mix_block(): lax.all_to_all(outgoing, 'ep', split_axis=0, concat_axis=0, tiled=True)]
    pallas_call x0 -> x8, Pallas kernels: none -> 26.4 us  [the longest x1 11.5 us: run_units(): pl.pallas_call(functools.partial(units_kernel, n_tp, n_z, n_rep), out_sha...]
    dot_general x9 -> x0, matrix products: 24 us -> none  [the longest x2 8.6 us: run_slots(): jnp.einsum('secq,egqf->secgf', received, weights[:, :2], preferred_elemen...]
  transfers between devices with their start and end apart: 9 -> 28, of which waited for: 8 -> 14; matrix products, arithmetic and copies ran while one was open for 22% -> 7% of each run, Pallas kernels for 0% -> 15%
where the time goes in v1:
time: 157 us; the launch traced here: 156 us
  waiting for transfers between devices  68.6 us (44%)
  starting transfers between devices  45.4 us (29%)
  Pallas kernels  26.4 us (17%)
  local copies, waits for them, and re-layouts  14.5 us (9%)
    ppermute x18, waiting for transfers between devices, send(): return lax.ppermute(array, ('ep', 'tp'), pairs)  59.2 us
    ppermute x18, starting transfers between devices, send(): return lax.ppermute(array, ('ep', 'tp'), pairs)  30.5 us
    ppermute x1, starting transfers between devices, to_tp(): lax.ppermute(array, 'tp', [(i, (i + shift) % n_tp) for i in range(n_tp)])  11.6 us
    pallas_call x1, Pallas kernels, run_units(): pl.pallas_call(functools.partial(units_kernel, n_tp, n_z, n_rep), out_sha...  11.5 us
    ppermute x1, waiting for transfers between devices, to_tp(): lax.ppermute(array, 'tp', [(i, (i + shift) % n_tp) for i in range(n_tp)])  7.58 us
    dynamic_slice x3, local copies, waits for them, and re-layouts, block_of(): lax.dynamic_slice(array, (0, first, first_row, 0), (array.shape[0], last...  7.35 us
    pallas_call x1, Pallas kernels, run_features(): pl.pallas_call(functools.partial(features_kernel, n_tp, n_z, dt), out_sha...  5.66 us
    unnamed x66, local copies, waits for them, and re-layouts  4.9 us
  transfers between devices with their start and end apart: 28, of which 14 were waited for; matrix products, arithmetic and copies ran while one was open for 7% of the time, Pallas kernels for 15%

profile of v1, /device:TPU:0, one launch (start us, length us, event | category | flops | bytes accessed | tf_op | source)
XLA Modules:
  0.0 156.4 jit_solution(5519131775043211990)
XLA Ops:
  0.5 3.0 %constant_dynamic-slice_fusion.2 = bf16[2,2,544,384]{3,2,1,0:T(8,128)(2,1)} fusion(bf16[2,3,1024,384]{3,2,1,0:T(8,128)(2,1)} %refs_6_.1, s32[]{:T(128)S(6)} %select_n.53), kind=kLoop, calls=%fused_computation.11 | loop fusion | bytes 3342340 | tf_op jit(solution)/shard_map/dynamic_slice | solution.py:541
  3.5 2.6 %collective-permute-start.2 = (bf16[2,2,544,384]{3,2,1,0:T(8,128)(2,1)}, bf16[2,2,544,384]{3,2,1,0:T(8,128)(2,1)}, u32[]{:S(2)}, u32[]{:S(2)}) collective-permute-start(bf16[2,2,544,384]{3,2,1,0:T(8,128)(2,1)} %constant_dynamic-slice_fusion.2), channel_id=1, source_target_pairs={{0,3},{1,2},{2,1},{3,0},{4,7},{5,6},{6,5},{7,4},{8,11},{9,10},{10,... | collective-permute-start | bytes 5013512 | tf_op jit(solution)/shard_map/ppermute | solution.py:516
  6.1 1.6 %collective-permute-start = (bf16[2048,256]{1,0:T(8,128)(2,1)S(1)}, bf16[2048,256]{1,0:T(8,128)(2,1)S(1)}, u32[]{:S(2)}, u32[]{:S(2)}) collective-permute-start(bf16[2048,256]{1,0:T(8,128)(2,1)S(1)} %copy-done.1), channel_id=1, source_target_pairs={{0,4},{1,5},{2,6},{3,7},{4,0},{5,1},{6,2},{7,3},{8,12},{9,13},{10,... | collective-permute-start | bytes 3145736 | tf_op jit(solution)/shard_map/ppermute | solution.py:516
  10.5 4.0 %attention.1.refs_0_ = bf16[128,2048]{1,0:T(8,128)(2,1)S(1)} custom-call(s32[1]{0:T(128)S(6)} %copy.16.length_ref, bf16[2,64,2048]{2,1,0:T(8,128)(2,1)S(1)} %copy-done.5, bf16[1,2,1024,256]{3,2,1,0:T(8,128)(2,1)S(1)} %copy-done.4, bf16[128,512]{1,0:T(8,128)(2,1)S(1)} %bitcast.15), custom_call_target="tpu_custom_call" | custom-call | flops 1000 | bytes 1000 | tf_op jit(solution)/shard_map/attention/pallas_call | solution.py:114
  14.5 4.0 %collective-permute-start.3 = (bf16[128,2048]{1,0:T(8,128)(2,1)S(1)}, bf16[128,2048]{1,0:T(8,128)(2,1)S(1)}, u32[]{:S(2)}, u32[]{:S(2)}) collective-permute-start(bf16[128,2048]{1,0:T(8,128)(2,1)S(1)} %attention.1.refs_0_), channel_id=1, source_target_pairs={{0,8},{1,9},{2,10},{3,11},{4,12},{5,13},{6,14},{7,15},{8,0},{9,1},... | collective-permute-start | bytes 1572872 | tf_op jit(solution)/shard_map/ppermute | solution.py:516
  19.6 2.2 %dynamic_slice.20 = bf16[2,1,512,384]{3,2,1,0:T(8,128)(2,1)} slice(bf16[2,3,1024,384]{3,2,1,0:T(8,128)(2,1)} %refs_6_.1), slice={[0:2], [2:3], [512:1024], [0:384]} | slice | bytes 1572864 | tf_op jit(solution)/shard_map/dynamic_slice | solution.py:541
  21.8 2.1 %fusion.1 = (bf16[2,1,256,384]{3,2,1,0:T(8,128)(2,1)}, bf16[2,1,256,384]{3,2,1,0:T(8,128)(2,1)}) fusion(bf16[2,3,1024,384]{3,2,1,0:T(8,128)(2,1)} %refs_6_.1), kind=kLoop, calls=%fused_computation.13 | loop fusion | bytes 1572864 | tf_op jit(solution)/shard_map/dynamic_slice | solution.py:541
  23.9 19.0 %collective-permute-done.refs_4_ = bf16[2048,256]{1,0:T(8,128)(2,1)S(1)} collective-permute-done((bf16[2048,256]{1,0:T(8,128)(2,1)S(1)}, bf16[2048,256]{1,0:T(8,128)(2,1)S(1)}, u32[]{:S(2)}, u32[]{:S(2)}) %collective-permute-start) | collective-permute-done | bytes 1048608 | tf_op jit(solution)/shard_map/ppermute | solution.py:516
  44.1 1.5 out_projection.1.refs_3_
  47.1 11.6 %collective-permute-start.7 = (bf16[144,1024]{1,0:T(8,128)(2,1)S(1)}, bf16[144,1024]{1,0:T(8,128)(2,1)S(1)}, u32[]{:S(2)}, u32[]{:S(2)}) collective-permute-start(bf16[144,1024]{1,0:T(8,128)(2,1)S(1)} %get-tuple-element.64), channel_id=1, source_target_pairs={{0,1},{1,0},{2,3},{3,2},{4,5},{5,4},{6,7},{7,6},{8,9},{9,8},{10,11... | collective-permute-start | bytes 884744 | tf_op jit(solution)/shard_map/ppermute | solution.py:522
  58.8 7.6 %collective-permute-done.7.refs_0_.refs_1_ = bf16[144,1024]{1,0:T(8,128)(2,1)S(1)} collective-permute-done((bf16[144,1024]{1,0:T(8,128)(2,1)S(1)}, bf16[144,1024]{1,0:T(8,128)(2,1)S(1)}, u32[]{:S(2)}, u32[]{:S(2)}) %collective-permute-start.7) | collective-permute-done | bytes 294944 | tf_op jit(solution)/shard_map/ppermute | solution.py:522
  66.4 1.6 %constant_dynamic-slice_fusion.1 = bf16[2,2,480,384]{3,2,1,0:T(8,128)(2,1)S(1)} fusion(bf16[2,2,544,384]{3,2,1,0:T(8,128)(2,1)} %collective-permute-done.2.refs_10_, s32[]{:T(128)S(6)} %select_n.61), kind=kLoop, calls=%fused_computation.10 | loop fusion | bytes 2949124 | tf_op jit(solution)/shard_map/dynamic_slice | solution.py:597
  68.0 1.6 %collective-permute-start.15 = (bf16[2,2,480,384]{3,2,1,0:T(8,128)(2,1)S(1)}, bf16[2,2,480,384]{3,2,1,0:T(8,128)(2,1)}, u32[]{:S(2)}, u32[]{:S(2)}) collective-permute-start(bf16[2,2,480,384]{3,2,1,0:T(8,128)(2,1)S(1)} %constant_dynamic-slice_fusion.1), channel_id=1, source_target_pairs={{0,16},{16,0},{1,17},{17,1},{2,18},{18,2},{3,19},{19,3},{4,20},{20... | collective-permute-start | bytes 4423688 | tf_op jit(solution)/shard_map/ppermute | solution.py:525
  69.6 1.8 %collective-permute-start.9 = (bf16[64,1152]{1,0:T(8,128)(2,1)S(1)}, bf16[64,1152]{1,0:T(8,128)(2,1)S(1)}, u32[]{:S(2)}, u32[]{:S(2)}) collective-permute-start(bf16[64,1152]{1,0:T(8,128)(2,1)S(1)} %copy-done.13), channel_id=1, source_target_pairs={{0,1},{1,9},{2,3},{3,11},{4,5},{5,13},{6,7},{7,15},{8,0},{9,8},{10... | collective-permute-start | bytes 442376 | tf_op jit(solution)/shard_map/ppermute | solution.py:516
  71.3 7.6 %collective-permute-done.9.refs_2_ = bf16[64,1152]{1,0:T(8,128)(2,1)S(1)} collective-permute-done((bf16[64,1152]{1,0:T(8,128)(2,1)S(1)}, bf16[64,1152]{1,0:T(8,128)(2,1)S(1)}, u32[]{:S(2)}, u32[]{:S(2)}) %collective-permute-start.9) | collective-permute-done | bytes 147488 | tf_op jit(solution)/shard_map/ppermute | solution.py:516
  79.8 2.8 %collective-permute-start.11 = (bf16[128,1024]{1,0:T(8,128)(2,1)S(1)}, bf16[128,1024]{1,0:T(8,128)(2,1)S(1)}, u32[]{:S(2)}, u32[]{:S(2)}) collective-permute-start(bf16[128,1024]{1,0:T(8,128)(2,1)S(1)} %get-tuple-element.71), channel_id=1, source_target_pairs={{0,8},{1,9},{2,10},{3,11},{4,12},{5,13},{6,14},{7,15},{8,0},{9,1},... | collective-permute-start | bytes 786440 | tf_op jit(solution)/shard_map/ppermute | solution.py:516
  82.6 9.2 %collective-permute-done.11.refs_4_ = bf16[128,1024]{1,0:T(8,128)(2,1)S(1)} collective-permute-done((bf16[128,1024]{1,0:T(8,128)(2,1)S(1)}, bf16[128,1024]{1,0:T(8,128)(2,1)S(1)}, u32[]{:S(2)}, u32[]{:S(2)}) %collective-permute-start.11) | collective-permute-done | bytes 262176 | tf_op jit(solution)/shard_map/ppermute | solution.py:516
  91.8 1.5 collective-permute-done.10.refs_3_
  94.1 2.3 %collective-permute-start.14 = (bf16[2,1,256,384]{3,2,1,0:T(8,128)(2,1)S(1)}, bf16[2,1,256,384]{3,2,1,0:T(8,128)(2,1)S(1)}, u32[]{:S(2)}, u32[]{:S(2)}) collective-permute-start(bf16[2,1,256,384]{3,2,1,0:T(8,128)(2,1)S(1)} %copy-done.22), channel_id=1, source_target_pairs={{0,3},{1,2},{2,1},{3,0},{4,7},{5,6},{6,5},{7,4},{8,11},{9,10},{10,... | collective-permute-start | bytes 1179656 | tf_op jit(solution)/shard_map/ppermute | solution.py:516
  96.8 8.0 %collective-permute-done.13.refs_5_ = bf16[128,1024]{1,0:T(8,128)(2,1)S(1)} collective-permute-done((bf16[128,1024]{1,0:T(8,128)(2,1)S(1)}, bf16[128,1024]{1,0:T(8,128)(2,1)S(1)}, u32[]{:S(2)}, u32[]{:S(2)}) %collective-permute-start.13) | collective-permute-done | bytes 262176 | tf_op jit(solution)/shard_map/ppermute | solution.py:516
  106.8 1.9 %collective-permute-start.20 = (bf16[2,1,512,384]{3,2,1,0:T(8,128)(2,1)}, bf16[2,1,512,384]{3,2,1,0:T(8,128)(2,1)S(1)}, u32[]{:S(2)}, u32[]{:S(2)}) collective-permute-start(bf16[2,1,512,384]{3,2,1,0:T(8,128)(2,1)} %dynamic_slice.20), channel_id=1, source_target_pairs={{0,3},{1,2},{2,1},{3,0},{4,7},{5,6},{6,5},{7,4},{8,11},{9,10},{10,... | collective-permute-start | bytes 2359304 | tf_op jit(solution)/shard_map/ppermute | solution.py:516
  111.1 11.5 %units.1 = (bf16[256,1536]{1,0:T(8,128)(2,1)}, bf16[256,2048]{1,0:T(8,128)(2,1)}, f32[64,1024]{1,0:T(8,128)}, bf16[64,1024]{1,0:T(8,128)(2,1)}, bf16[64,1024]{1,0:T(8,128)(2,1)}, /*index=5*/bf16[64,1024]{1,0:T(8,128)(2,1)}) custom-call(s32[6]{0:T(128)} %copy-done.10, s32[1,16]{1,0:T(1,128)} %constant_dynamic-slice_fusion.table_ref, ...), custom_call_target="tpu_custom_call" | custom-call | flops 1000 | bytes 1000 | tf_op jit(solution)/shard_map/units/pallas_call | solution.py:386
  122.6 4.1 %collective-permute-done.20.refs_5_ = bf16[2,1,512,384]{3,2,1,0:T(8,128)(2,1)S(1)} collective-permute-done((bf16[2,1,512,384]{3,2,1,0:T(8,128)(2,1)}, bf16[2,1,512,384]{3,2,1,0:T(8,128)(2,1)S(1)}, u32[]{:S(2)}, u32[]{:S(2)}) %collective-permute-start.20) | collective-permute-done | bytes 786464 | tf_op jit(solution)/shard_map/ppermute | solution.py:516
  127.4 2.3 %collective-permute-start.17 = (bf16[64,1024]{1,0:T(8,128)(2,1)}, bf16[64,1024]{1,0:T(8,128)(2,1)S(1)}, u32[]{:S(2)}, u32[]{:S(2)}) collective-permute-start(bf16[64,1024]{1,0:T(8,128)(2,1)} %get-tuple-element.88), channel_id=1, source_target_pairs={{0,4},{1,5},{2,6},{3,7},{4,0},{5,1},{6,2},{7,3},{8,12},{9,13},{10,... | collective-permute-start | bytes 393224 | tf_op jit(solution)/shard_map/ppermute | solution.py:516
  129.6 1.9 %collective-permute-start.18 = (bf16[64,1024]{1,0:T(8,128)(2,1)}, bf16[64,1024]{1,0:T(8,128)(2,1)S(1)}, u32[]{:S(2)}, u32[]{:S(2)}) collective-permute-start(bf16[64,1024]{1,0:T(8,128)(2,1)} %get-tuple-element.89), channel_id=1, source_target_pairs={{0,8},{1,9},{2,10},{3,11},{4,12},{5,13},{6,14},{7,15},{8,0},{9,1},... | collective-permute-start | bytes 393224 | tf_op jit(solution)/shard_map/ppermute | solution.py:516
  131.5 1.4 collective-permute-start.19
  134.0 5.7 %features.1 = (bf16[64,1024]{1,0:T(8,128)(2,1)}, bf16[64,1024]{1,0:T(8,128)(2,1)}, bf16[64,1024]{1,0:T(8,128)(2,1)}, bf16[64,1024]{1,0:T(8,128)(2,1)}) custom-call(s32[6]{0:T(128)} %copy-done.10, bf16[256,1536]{1,0:T(8,128)(2,1)} %get-tuple-element.91.hidden_ref, bf16[256,2048]{1,0:T(8,128)(2,1)} %get-tuple-element.92.resid_ref, ...), custom_call_target="tpu_custom_call" | custom-call | flops 1000 | bytes 1000 | tf_op jit(solution)/shard_map/features/pallas_call | solution.py:416
  141.4 3.1 %collective-permute-start.26 = (bf16[64,1024]{1,0:T(8,128)(2,1)}, bf16[64,1024]{1,0:T(8,128)(2,1)S(1)}, u32[]{:S(2)}, u32[]{:S(2)}) collective-permute-start(bf16[64,1024]{1,0:T(8,128)(2,1)} %get-tuple-element.99), channel_id=1, source_target_pairs={{0,9},{1,8},{2,11},{3,10},{4,13},{5,12},{6,15},{7,14},{8,1},{9,0},... | collective-permute-start | bytes 393224 | tf_op jit(solution)/shard_map/ppermute | solution.py:516
  144.5 1.9 %collective-permute-start.27 = (bf16[64,1024]{1,0:T(8,128)(2,1)}, bf16[64,1024]{1,0:T(8,128)(2,1)S(1)}, u32[]{:S(2)}, u32[]{:S(2)}) collective-permute-start(bf16[64,1024]{1,0:T(8,128)(2,1)} %get-tuple-element.100), channel_id=1, source_target_pairs={{0,13},{1,12},{2,15},{3,14},{4,9},{5,8},{6,11},{7,10},{8,5},{9,4},... | collective-permute-start | bytes 393224 | tf_op jit(solution)/shard_map/ppermute | solution.py:516
  146.5 4.2 %collective-permute-done.24.refs_4_ = bf16[64,1024]{1,0:T(8,128)(2,1)S(1)} collective-permute-done((bf16[64,1024]{1,0:T(8,128)(2,1)}, bf16[64,1024]{1,0:T(8,128)(2,1)S(1)}, u32[]{:S(2)}, u32[]{:S(2)}) %collective-permute-start.24) | collective-permute-done | bytes 131104 | tf_op jit(solution)/shard_map/ppermute | solution.py:516
  150.7 4.3 %collective-permute-done.26.refs_6_ = bf16[64,1024]{1,0:T(8,128)(2,1)S(1)} collective-permute-done((bf16[64,1024]{1,0:T(8,128)(2,1)}, bf16[64,1024]{1,0:T(8,128)(2,1)S(1)}, u32[]{:S(2)}, u32[]{:S(2)}) %collective-permute-start.26) | collective-permute-done | bytes 131104 | tf_op jit(solution)/shard_map/ppermute | solution.py:516
  155.0 1.4 mix.1
  (110 shorter events, 16.1 us)
Async XLA Ops:
  0.0 43.3 %collective-permute-start.4 = (bf16[2,3,1024,384]{3,2,1,0:T(8,128)(2,1)}, bf16[2,3,1024,384]{3,2,1,0:T(8,128)(2,1)}, u32[]{:S(2)}, u32[]{:S(2)}) collective-permute-start(bf16[2,3,1024,384]{3,2,1,0:T(8,128)(2,1)} %refs_6_.1), channel_id=1, source_target_pairs={{0,2},{2,0},{4,6},{6,4},{8,10},{10,8},{12,14},{14,12},{1,3},{3,1},... | collective-permute-start | bytes 14155784 | tf_op jit(solution)/shard_map/ppermute | solution.py:519
  3.5 39.8 %collective-permute-start.2 = (bf16[2,2,544,384]{3,2,1,0:T(8,128)(2,1)}, bf16[2,2,544,384]{3,2,1,0:T(8,128)(2,1)}, u32[]{:S(2)}, u32[]{:S(2)}) collective-permute-start(bf16[2,2,544,384]{3,2,1,0:T(8,128)(2,1)} %constant_dynamic-slice_fusion.2), channel_id=1, source_target_pairs={{0,3},{1,2},{2,1},{3,0},{4,7},{5,6},{6,5},{7,4},{8,11},{9,10},{10,... | collective-permute-start | bytes 5013512 | tf_op jit(solution)/shard_map/ppermute | solution.py:516
  6.1 3.4 %collective-permute-start.1 = (bf16[2048,256]{1,0:T(8,128)(2,1)S(1)}, bf16[2048,256]{1,0:T(8,128)(2,1)S(1)}, u32[]{:S(2)}, u32[]{:S(2)}) collective-permute-start(bf16[2048,256]{1,0:T(8,128)(2,1)S(1)} %copy-done.1), channel_id=1, source_target_pairs={{0,2},{2,0},{4,6},{6,4},{8,10},{10,8},{12,14},{14,12},{1,3},{3,1},... | collective-permute-start | bytes 3145736 | tf_op jit(solution)/shard_map/ppermute | solution.py:519
  6.1 36.8 %collective-permute-start = (bf16[2048,256]{1,0:T(8,128)(2,1)S(1)}, bf16[2048,256]{1,0:T(8,128)(2,1)S(1)}, u32[]{:S(2)}, u32[]{:S(2)}) collective-permute-start(bf16[2048,256]{1,0:T(8,128)(2,1)S(1)} %copy-done.1), channel_id=1, source_target_pairs={{0,4},{1,5},{2,6},{3,7},{4,0},{5,1},{6,2},{7,3},{8,12},{9,13},{10,... | collective-permute-start | bytes 3145736 | tf_op jit(solution)/shard_map/ppermute | solution.py:516
  14.5 28.4 %collective-permute-start.3 = (bf16[128,2048]{1,0:T(8,128)(2,1)S(1)}, bf16[128,2048]{1,0:T(8,128)(2,1)S(1)}, u32[]{:S(2)}, u32[]{:S(2)}) collective-permute-start(bf16[128,2048]{1,0:T(8,128)(2,1)S(1)} %attention.1.refs_0_), channel_id=1, source_target_pairs={{0,8},{1,9},{2,10},{3,11},{4,12},{5,13},{6,14},{7,15},{8,0},{9,1},... | collective-permute-start | bytes 1572872 | tf_op jit(solution)/shard_map/ppermute | solution.py:516
  18.7 60.2 %copy-start.10 = (s32[6]{0:T(128)}, s32[6]{0:T(128)S(1)}, u32[]{:S(2)}) copy-start(s32[6]{0:T(128)S(1)} %stack.36.place_ref) | copy-start | bytes 76
  43.3 2.7 %collective-permute-start.5 = (bf16[2048,256]{1,0:T(8,128)(2,1)S(1)}, bf16[2048,256]{1,0:T(8,128)(2,1)S(1)}, u32[]{:S(2)}, u32[]{:S(2)}) collective-permute-start(bf16[2048,256]{1,0:T(8,128)(2,1)S(1)} %collective-permute-done.refs_4_), channel_id=1, source_target_pairs={{0,2},{2,0},{4,6},{6,4},{8,10},{10,8},{12,14},{14,12},{1,3},{3,1},... | collective-permute-start | bytes 3145736 | tf_op jit(solution)/shard_map/ppermute | solution.py:519
  43.4 2.2 %collective-permute-start.6 = (bf16[64,1152]{1,0:T(8,128)(2,1)S(1)}, bf16[64,1152]{1,0:T(8,128)(2,1)S(1)}, u32[]{:S(2)}, u32[]{:S(2)}) collective-permute-start(bf16[64,1152]{1,0:T(8,128)(2,1)S(1)} %get-tuple-element.61), channel_id=1, source_target_pairs={{0,0},{1,8},{2,2},{3,10},{4,4},{5,12},{6,6},{7,14},{8,1},{9,9},{10... | collective-permute-start | bytes 442376 | tf_op jit(solution)/shard_map/ppermute | solution.py:516
  46.9 24.4 %collective-permute-start.8 = (bf16[2,2,544,384]{3,2,1,0:T(8,128)(2,1)}, bf16[2,2,544,384]{3,2,1,0:T(8,128)(2,1)}, u32[]{:S(2)}, u32[]{:S(2)}) collective-permute-start(bf16[2,2,544,384]{3,2,1,0:T(8,128)(2,1)} %collective-permute-done.2.refs_10_), channel_id=1, source_target_pairs={{0,2},{2,0},{4,6},{6,4},{8,10},{10,8},{12,14},{14,12},{1,3},{3,1},... | collective-permute-start | bytes 5013512 | tf_op jit(solution)/shard_map/ppermute | solution.py:519
  47.1 19.2 %collective-permute-start.7 = (bf16[144,1024]{1,0:T(8,128)(2,1)S(1)}, bf16[144,1024]{1,0:T(8,128)(2,1)S(1)}, u32[]{:S(2)}, u32[]{:S(2)}) collective-permute-start(bf16[144,1024]{1,0:T(8,128)(2,1)S(1)} %get-tuple-element.64), channel_id=1, source_target_pairs={{0,1},{1,0},{2,3},{3,2},{4,5},{5,4},{6,7},{7,6},{8,9},{9,8},{10,11... | collective-permute-start | bytes 884744 | tf_op jit(solution)/shard_map/ppermute | solution.py:522
  58.8 47.9 %copy-start.29 = (s32[16]{0:T(128)S(1)}, s32[16]{0:T(128)}, u32[]{:S(2)}) copy-start(s32[16]{0:T(128)} %param.21) | copy-start | bytes 196
  58.8 47.9 %copy-start.30 = (s32[4]{0:T(128)S(1)}, s32[4]{0:T(128)}, u32[]{:S(2)}) copy-start(s32[4]{0:T(128)} %param.23) | copy-start | bytes 52
  58.8 47.9 %copy-start.31 = (s32[16]{0:T(128)S(1)}, s32[16]{0:T(128)}, u32[]{:S(2)}) copy-start(s32[16]{0:T(128)} %param.22) | copy-start | bytes 196
  68.0 38.5 %collective-permute-start.15 = (bf16[2,2,480,384]{3,2,1,0:T(8,128)(2,1)S(1)}, bf16[2,2,480,384]{3,2,1,0:T(8,128)(2,1)}, u32[]{:S(2)}, u32[]{:S(2)}) collective-permute-start(bf16[2,2,480,384]{3,2,1,0:T(8,128)(2,1)S(1)} %constant_dynamic-slice_fusion.1), channel_id=1, source_target_pairs={{0,16},{16,0},{1,17},{17,1},{2,18},{18,2},{3,19},{19,3},{4,20},{20... | collective-permute-start | bytes 4423688 | tf_op jit(solution)/shard_map/ppermute | solution.py:525
  69.6 9.4 %collective-permute-start.9 = (bf16[64,1152]{1,0:T(8,128)(2,1)S(1)}, bf16[64,1152]{1,0:T(8,128)(2,1)S(1)}, u32[]{:S(2)}, u32[]{:S(2)}) collective-permute-start(bf16[64,1152]{1,0:T(8,128)(2,1)S(1)} %copy-done.13), channel_id=1, source_target_pairs={{0,1},{1,9},{2,3},{3,11},{4,5},{5,13},{6,7},{7,15},{8,0},{9,8},{10... | collective-permute-start | bytes 442376 | tf_op jit(solution)/shard_map/ppermute | solution.py:516
  79.6 14.4 %collective-permute-start.12 = (bf16[2,1,256,384]{3,2,1,0:T(8,128)(2,1)S(1)}, bf16[2,1,256,384]{3,2,1,0:T(8,128)(2,1)S(1)}, u32[]{:S(2)}, u32[]{:S(2)}) collective-permute-start(bf16[2,1,256,384]{3,2,1,0:T(8,128)(2,1)S(1)} %copy-done.23), channel_id=1, source_target_pairs={{0,3},{1,2},{2,1},{3,0},{4,7},{5,6},{6,5},{7,4},{8,11},{9,10},{10,... | collective-permute-start | bytes 1179656 | tf_op jit(solution)/shard_map/ppermute | solution.py:516
  79.7 13.6 %collective-permute-start.10 = (bf16[128,1152]{1,0:T(8,128)(2,1)S(1)}, bf16[128,1152]{1,0:T(8,128)(2,1)S(1)}, u32[]{:S(2)}, u32[]{:S(2)}) collective-permute-start(bf16[128,1152]{1,0:T(8,128)(2,1)S(1)} %get-tuple-element.81.refs_2_), channel_id=1, source_target_pairs={{0,4},{1,5},{2,6},{3,7},{4,0},{5,1},{6,2},{7,3},{8,12},{9,13},{10,... | collective-permute-start | bytes 884744 | tf_op jit(solution)/shard_map/ppermute | solution.py:516
  79.8 12.1 %collective-permute-start.11 = (bf16[128,1024]{1,0:T(8,128)(2,1)S(1)}, bf16[128,1024]{1,0:T(8,128)(2,1)S(1)}, u32[]{:S(2)}, u32[]{:S(2)}) collective-permute-start(bf16[128,1024]{1,0:T(8,128)(2,1)S(1)} %get-tuple-element.71), channel_id=1, source_target_pairs={{0,8},{1,9},{2,10},{3,11},{4,12},{5,13},{6,14},{7,15},{8,0},{9,1},... | collective-permute-start | bytes 786440 | tf_op jit(solution)/shard_map/ppermute | solution.py:516
  94.1 11.6 %collective-permute-start.14 = (bf16[2,1,256,384]{3,2,1,0:T(8,128)(2,1)S(1)}, bf16[2,1,256,384]{3,2,1,0:T(8,128)(2,1)S(1)}, u32[]{:S(2)}, u32[]{:S(2)}) collective-permute-start(bf16[2,1,256,384]{3,2,1,0:T(8,128)(2,1)S(1)} %copy-done.22), channel_id=1, source_target_pairs={{0,3},{1,2},{2,1},{3,0},{4,7},{5,6},{6,5},{7,4},{8,11},{9,10},{10,... | collective-permute-start | bytes 1179656 | tf_op jit(solution)/shard_map/ppermute | solution.py:516
  96.4 8.5 %collective-permute-start.13 = (bf16[128,1024]{1,0:T(8,128)(2,1)S(1)}, bf16[128,1024]{1,0:T(8,128)(2,1)S(1)}, u32[]{:S(2)}, u32[]{:S(2)}) collective-permute-start(bf16[128,1024]{1,0:T(8,128)(2,1)S(1)} %collective-permute-done.11.refs_4_), channel_id=1, source_target_pairs={{0,4},{1,5},{2,6},{3,7},{4,0},{5,1},{6,2},{7,3},{8,12},{9,13},{10,... | collective-permute-start | bytes 786440 | tf_op jit(solution)/shard_map/ppermute | solution.py:516
  106.5 3.5 %collective-permute-start.16 = (bf16[2,2,480,384]{3,2,1,0:T(8,128)(2,1)}, bf16[2,2,480,384]{3,2,1,0:T(8,128)(2,1)S(1)}, u32[]{:S(2)}, u32[]{:S(2)}) collective-permute-start(bf16[2,2,480,384]{3,2,1,0:T(8,128)(2,1)} %collective-permute-done.15.refs_11_), channel_id=1, source_target_pairs={{0,2},{2,0},{4,6},{6,4},{8,10},{10,8},{12,14},{14,12},{1,3},{3,1},... | collective-permute-start | bytes 4423688 | tf_op jit(solution)/shard_map/ppermute | solution.py:519
  106.8 19.8 %collective-permute-start.20 = (bf16[2,1,512,384]{3,2,1,0:T(8,128)(2,1)}, bf16[2,1,512,384]{3,2,1,0:T(8,128)(2,1)S(1)}, u32[]{:S(2)}, u32[]{:S(2)}) collective-permute-start(bf16[2,1,512,384]{3,2,1,0:T(8,128)(2,1)} %dynamic_slice.20), channel_id=1, source_target_pairs={{0,3},{1,2},{2,1},{3,0},{4,7},{5,6},{6,5},{7,4},{8,11},{9,10},{10,... | collective-permute-start | bytes 2359304 | tf_op jit(solution)/shard_map/ppermute | solution.py:516
  126.7 6.2 %collective-permute-start.23 = (bf16[2,1,512,384]{3,2,1,0:T(8,128)(2,1)S(1)}, bf16[2,1,512,384]{3,2,1,0:T(8,128)(2,1)S(1)}, u32[]{:S(2)}, u32[]{:S(2)}) collective-permute-start(bf16[2,1,512,384]{3,2,1,0:T(8,128)(2,1)S(1)} %collective-permute-done.20.refs_5_), channel_id=1, source_target_pairs={{0,2},{2,0},{4,6},{6,4},{8,10},{10,8},{12,14},{14,12},{1,3},{3,1},... | collective-permute-start | bytes 2359304 | tf_op jit(solution)/shard_map/ppermute | solution.py:519
  126.8 4.6 %collective-permute-start.21 = (bf16[2,1,256,384]{3,2,1,0:T(8,128)(2,1)S(1)}, bf16[2,1,256,384]{3,2,1,0:T(8,128)(2,1)S(1)}, u32[]{:S(2)}, u32[]{:S(2)}) collective-permute-start(bf16[2,1,256,384]{3,2,1,0:T(8,128)(2,1)S(1)} %collective-permute-done.12.refs_1_), channel_id=1, source_target_pairs={{0,2},{2,0},{4,6},{6,4},{8,10},{10,8},{12,14},{14,12},{1,3},{3,1},... | collective-permute-start | bytes 1179656 | tf_op jit(solution)/shard_map/ppermute | solution.py:519
  127.2 5.7 %collective-permute-start.22 = (bf16[2,1,256,384]{3,2,1,0:T(8,128)(2,1)S(1)}, bf16[2,1,256,384]{3,2,1,0:T(8,128)(2,1)S(1)}, u32[]{:S(2)}, u32[]{:S(2)}) collective-permute-start(bf16[2,1,256,384]{3,2,1,0:T(8,128)(2,1)S(1)} %copy-done.19), channel_id=1, source_target_pairs={{0,2},{2,0},{4,6},{6,4},{8,10},{10,8},{12,14},{14,12},{1,3},{3,1},... | collective-permute-start | bytes 1179656 | tf_op jit(solution)/shard_map/ppermute | solution.py:519
  127.4 14.0 %collective-permute-start.17 = (bf16[64,1024]{1,0:T(8,128)(2,1)}, bf16[64,1024]{1,0:T(8,128)(2,1)S(1)}, u32[]{:S(2)}, u32[]{:S(2)}) collective-permute-start(bf16[64,1024]{1,0:T(8,128)(2,1)} %get-tuple-element.88), channel_id=1, source_target_pairs={{0,4},{1,5},{2,6},{3,7},{4,0},{5,1},{6,2},{7,3},{8,12},{9,13},{10,... | collective-permute-start | bytes 393224 | tf_op jit(solution)/shard_map/ppermute | solution.py:516
  129.6 14.9 %collective-permute-start.18 = (bf16[64,1024]{1,0:T(8,128)(2,1)}, bf16[64,1024]{1,0:T(8,128)(2,1)S(1)}, u32[]{:S(2)}, u32[]{:S(2)}) collective-permute-start(bf16[64,1024]{1,0:T(8,128)(2,1)} %get-tuple-element.89), channel_id=1, source_target_pairs={{0,8},{1,9},{2,10},{3,11},{4,12},{5,13},{6,14},{7,15},{8,0},{9,1},... | collective-permute-start | bytes 393224 | tf_op jit(solution)/shard_map/ppermute | solution.py:516
  131.5 15.0 %collective-permute-start.19 = (bf16[64,1024]{1,0:T(8,128)(2,1)}, bf16[64,1024]{1,0:T(8,128)(2,1)S(1)}, u32[]{:S(2)}, u32[]{:S(2)}) collective-permute-start(bf16[64,1024]{1,0:T(8,128)(2,1)} %get-tuple-element.90), channel_id=1, source_target_pairs={{0,12},{1,13},{2,14},{3,15},{4,8},{5,9},{6,10},{7,11},{8,4},{9,5},... | collective-permute-start | bytes 393224 | tf_op jit(solution)/shard_map/ppermute | solution.py:516
  139.6 11.0 %collective-permute-start.24 = (bf16[64,1024]{1,0:T(8,128)(2,1)}, bf16[64,1024]{1,0:T(8,128)(2,1)S(1)}, u32[]{:S(2)}, u32[]{:S(2)}) collective-permute-start(bf16[64,1024]{1,0:T(8,128)(2,1)} %get-tuple-element.97), channel_id=1, source_target_pairs={{0,1},{1,0},{2,3},{3,2},{4,5},{5,4},{6,7},{7,6},{8,9},{9,8},{10,11... | collective-permute-start | bytes 393224 | tf_op jit(solution)/shard_map/ppermute | solution.py:516
  140.7 10.0 %collective-permute-start.25 = (bf16[64,1024]{1,0:T(8,128)(2,1)}, bf16[64,1024]{1,0:T(8,128)(2,1)S(1)}, u32[]{:S(2)}, u32[]{:S(2)}) collective-permute-start(bf16[64,1024]{1,0:T(8,128)(2,1)} %get-tuple-element.98), channel_id=1, source_target_pairs={{0,5},{1,4},{2,7},{3,6},{4,1},{5,0},{6,3},{7,2},{8,13},{9,12},{10,... | collective-permute-start | bytes 393224 | tf_op jit(solution)/shard_map/ppermute | solution.py:516
  141.4 13.6 %collective-permute-start.26 = (bf16[64,1024]{1,0:T(8,128)(2,1)}, bf16[64,1024]{1,0:T(8,128)(2,1)S(1)}, u32[]{:S(2)}, u32[]{:S(2)}) collective-permute-start(bf16[64,1024]{1,0:T(8,128)(2,1)} %get-tuple-element.99), channel_id=1, source_target_pairs={{0,9},{1,8},{2,11},{3,10},{4,13},{5,12},{6,15},{7,14},{8,1},{9,0},... | collective-permute-start | bytes 393224 | tf_op jit(solution)/shard_map/ppermute | solution.py:516
  144.5 10.4 %collective-permute-start.27 = (bf16[64,1024]{1,0:T(8,128)(2,1)}, bf16[64,1024]{1,0:T(8,128)(2,1)S(1)}, u32[]{:S(2)}, u32[]{:S(2)}) collective-permute-start(bf16[64,1024]{1,0:T(8,128)(2,1)} %get-tuple-element.100), channel_id=1, source_target_pairs={{0,13},{1,12},{2,15},{3,14},{4,9},{5,8},{6,11},{7,10},{8,5},{9,4},... | collective-permute-start | bytes 393224 | tf_op jit(solution)/shard_map/ppermute | solution.py:516
  (28 other events, 358.5 us)

commit v2 on v1

--- a/solution.py
+++ b/solution.py
@@ -198,11 +198,11 @@
 
 
 def residual_kernel(n_tp, place_ref, keep_ref, *refs):
-    t = place_ref[0]
+    z_hi = place_ref[5]
     terms, hidden, out_ref, marked_ref = refs[: n_tp - 1], refs[n_tp - 1 : -2], refs[-2], refs[-1]
     chunk, columns = hidden[0].shape[0], keep_ref.shape[1]
-    for beta, piece in enumerate(hidden):
-        rows = pl.ds(pl.multiple_of(lax.rem(t - beta + n_tp, n_tp) * chunk, chunk), chunk)
+    for dh, piece in enumerate(hidden):
+        rows = pl.ds(pl.multiple_of((z_hi ^ dh) * chunk, chunk), chunk)
         total = keep_ref[rows, :]
         for term in terms:
             total = total + term[rows, :].astype(F32)
@@ -429,31 +429,37 @@
     )(place, hidden, resid, *weights)
 
 
-def message_kernel(n_tp, place_ref, hidden_ref, ids_ref, *outs):
-    z_hi = place_ref[5]
-    chunk, lanes = outs[0].shape[0], outs[0].shape[1] - hidden_ref.shape[1]
+def message_kernel(n_tp, place_ref, hidden_ref, ids_ref, *refs):
+    t, z_hi = place_ref[0], place_ref[5]
+    swapped, outs = refs[: n_tp - 1], refs[n_tp - 1 :]
+    columns = hidden_ref.shape[1]
+    chunk, lanes = outs[0].shape[0], outs[0].shape[1] - columns
     experts = lax.broadcasted_iota(jnp.int32, (chunk, lanes), 1)
-    for beta, out_ref in enumerate(outs):
-        rows = pl.ds(pl.multiple_of(lax.rem(z_hi + beta, n_tp) * chunk, chunk), chunk)
-        ids = ids_ref[rows, :]
-        found = jnp.zeros((chunk, lanes), F32)
-        for k in range(ids.shape[1]):
-            found = found + jnp.where(ids[:, k : k + 1] == experts, F32(1.0), F32(0.0))
-        out_ref[:, pl.ds(0, hidden_ref.shape[1])] = hidden_ref[rows, :]
-        out_ref[:, pl.ds(hidden_ref.shape[1], lanes)] = found.astype(BF16)
-
-
-def messages(n_tp, place, hidden, ids, experts):
+    rows = pl.ds(pl.multiple_of(t * chunk, chunk), chunk)
+    ids = ids_ref[rows, :]
+    found = jnp.zeros((chunk, lanes), F32)
+    for k in range(ids.shape[1]):
+        found = found + jnp.where(ids[:, k : k + 1] == experts, F32(1.0), F32(0.0))
+    for dh, out_ref in enumerate(outs):
+        value = hidden_ref[rows, :]
+        for dt in range(1, n_tp):
+            source = lax.rem(t - dt + n_tp, n_tp)
+            value = jnp.where(source == (z_hi ^ dh), swapped[dt - 1][...], value)
+        out_ref[:, pl.ds(0, columns)] = value
+        out_ref[:, pl.ds(columns, lanes)] = found.astype(BF16)
+
+
+def messages(n_tp, place, hidden, ids, swapped, experts):
     shape = (ids.shape[0] // n_tp, hidden.shape[1] + experts + -experts % LANES)
     return pl.pallas_call(
         functools.partial(message_kernel, n_tp),
         out_shape=[jax.ShapeDtypeStruct(shape, BF16)] * n_tp,
-        in_specs=[scalars(), whole(), whole()],
+        in_specs=[scalars()] + [whole()] * (2 + len(swapped)),
         out_specs=[whole()] * n_tp,
         compiler_params=params(16),
         cost_estimate=COST,
         name="messages",
-    )(place, hidden, ids)
+    )(place, hidden, ids, *swapped)
 
 
 def mix_kernel(n_tp, n_z, place_ref, *refs):
@@ -545,30 +551,38 @@
     def far(block):
         return [send(block, lambda i, k: (i ^ 1, k + dt)) for dt in range(1, n_tp)]
 
+    flat_hidden = hidden_states.reshape(rows, quarter)
+    swapped = [
+        to_tp(
+            lax.dynamic_slice_in_dim(flat_hidden, lax.rem(t + dt, n_tp) * chunk, chunk, 0), dt
+        )
+        for dt in range(1, n_tp)
+    ]
     near = over_z(out_weight, 1, m)
     out_other = to_core(out_weight)
-    share = quarter // n_rep - quarter // 32
-    first = far(block_of(expert_weights, (0, 2), y * share, quarter - share))
-
-    queries = after(queries, out_other)
+    share = quarter // n_rep
+    first = far(after(block_of(expert_weights, (0, 2), y * share, share), swapped))
+
+    queries = after(queries, (out_other, swapped))
     fresh = fresh_key_value.reshape(rows, -1)
     attention = attend(cache_lengths, queries, cache, fresh)
     pieces = over_z(attention, m, n_z)
     own_other = to_core(expert_weights)
-    hidden_states, weights = after((hidden_states, expert_weights), attention)
+    expert_ids, weights, old_slots, router = after(
+        (expert_ids, expert_weights, old_slots, router_weight), attention
+    )
     outgoing = messages(
-        n_tp, place, hidden_states.reshape(rows, quarter), expert_ids.reshape(rows, -1), experts
-    )
-    blocks = [
-        block_of(weights, (2, 3), first * quarter // 4, size * quarter // 4)
-        for first, size in ((0, 1), (1, 1), (2, 2))
-    ]
-    near, old_slots, router, outgoing, blocks, first = after(
-        (near, old_slots, router_weight, outgoing, blocks, first), (pieces[1], own_other)
-    )
+        n_tp, place, flat_hidden, expert_ids.reshape(rows, -1), swapped, experts
+    )
+    blocks = [block_of(weights, (2, 3), n * quarter // 2, quarter // 2) for n in range(2)]
     router = router.T
     tables = slot_tables(old_slots, new_slots, moved_experts)
     table = lax.dynamic_slice_in_dim(tables, t * chunk // tokens, 1, 0)
+    near, table, router, outgoing, blocks, first = after(
+        (near, table, router, outgoing, blocks, first), (pieces[1], own_other)
+    )
+    hidden = [outgoing[0]] + [to_z(outgoing[dh], dh * m) for dh in range(1, n_tp)]
+    passed = [to_rep(array, 1) for array in first]
     crossed = [out_other] + [to_core(array) for array in near[1:]]
     early = [array for pair in zip(near, crossed) for array in pair]
     last = early.pop()
@@ -578,39 +592,23 @@
         last, early = together.transpose(1, 0, 2).reshape(together.shape[1], -1), []
     else:
         early = [project(n_tp, place, pieces, early)]
-    hidden = [
-        send(
-            block,
-            lambda i, k: (
-                (m * k + (i // CORES) % m) * CORES + i % CORES,
-                (i // CORES) // m + beta,
-            ),
-        )
-        for beta, block in enumerate(outgoing)
-    ]
-    last = after(last, hidden[0])
     sums = finish(n_tp, place, router, pieces, last, early)
     terms = [to_tp(sums[dt], dt) for dt in range(1, n_tp)]
-    first_other = [to_core(array) for array in after(first, sums)]
-    first = after(first, terms)
-    passed = [
-        to_rep(lax.dynamic_slice_in_dim(array, y * (quarter - 2 * share), share, 2), 1)
-        for array in first
-    ]
+    first = after(first, sums)
+    first_other = [to_core(array) for array in first]
 
     resid, marked = add_residual(n_tp, place, sums[0], after(terms, first_other), hidden)
     near = over_z(marked, 1, m)
     wide = to_z(resid, m)
     blocks = after(blocks, resid)
     down = [far(blocks[0])]
-    wide, blocks = after((wide, blocks), (wide, near, down))
-    down.append(far(blocks[1]))
+    wide = after(wide, near)
     gathered = near + [wide]
     for dz in range(m + 1, n_z):
         step = dz & -dz
         gathered.append(to_z(gathered[dz ^ step] if dz ^ step else resid, step))
     gathered, blocks = after((gathered, blocks), (gathered, down))
-    down.append(far(blocks[2]))
+    down.append(far(blocks[1]))
 
     passed = after(passed, gathered)
     passed_other = [to_core(array) for array in passed]

time: 157 us -> 136 us (0.87)
  starting transfers between devices: 45.4 us -> 33.4 us
  waiting for transfers between devices: 68.6 us -> 60.8 us
  local copies, waits for them, and re-layouts: 14.5 us -> 11.6 us
    ppermute x1 -> x2, starting transfers between devices: 11.6 us -> 4.24 us  [to_tp(): lax.ppermute(array, 'tp', [(i, (i + shift) % n_tp) for i in range(n_tp)])]
    ppermute x18 -> x16, waiting for transfers between devices: 59.2 us -> 52 us  [send(): return lax.ppermute(array, ('ep', 'tp'), pairs)]
    ppermute x18 -> x16, starting transfers between devices: 30.5 us -> 26.1 us  [send(): return lax.ppermute(array, ('ep', 'tp'), pairs)]
    dynamic_slice x3 -> x2, local copies, waits for them, and re-layouts: 7.35 us -> 5.33 us  [block_of(): lax.dynamic_slice(array, (0, first, first_row, 0), (array.shape[0], last...]
    ppermute x1 -> x2, waiting for transfers between devices: 7.58 us -> 6.19 us  [to_tp(): lax.ppermute(array, 'tp', [(i, (i + shift) % n_tp) for i in range(n_tp)])]
    unnamed x66 -> x51, local copies, waits for them, and re-layouts: 4.9 us -> 4.6 us
  transfers between devices with their start and end apart: 28 -> 26, of which waited for: 14 -> 12; matrix products, arithmetic and copies ran while one was open for 7% -> 7% of each run, Pallas kernels for 15% -> 18%
where the time goes in v2:
time: 136 us; the launch traced here: 135 us
  waiting for transfers between devices  60.8 us (45%)
  starting transfers between devices  33.4 us (25%)
  Pallas kernels  26.7 us (20%)
  local copies, waits for them, and re-layouts  11.6 us (9%)
  other arithmetic  1.92 us (1%)
    ppermute x16, waiting for transfers between devices, send(): return lax.ppermute(array, ('ep', 'tp'), pairs)  52 us
    ppermute x16, starting transfers between devices, send(): return lax.ppermute(array, ('ep', 'tp'), pairs)  26.1 us
    pallas_call x1, Pallas kernels, run_units(): pl.pallas_call(functools.partial(units_kernel, n_tp, n_z, n_rep), out_sha...  11.7 us
    ppermute x2, waiting for transfers between devices, to_tp(): lax.ppermute(array, 'tp', [(i, (i + shift) % n_tp) for i in range(n_tp)])  6.19 us
    dynamic_slice x2, local copies, waits for them, and re-layouts, block_of(): lax.dynamic_slice(array, (0, first, first_row, 0), (array.shape[0], last...  5.33 us
    pallas_call x1, Pallas kernels, run_features(): pl.pallas_call(functools.partial(features_kernel, n_tp, n_z, dt), out_sha...  5.18 us
    unnamed x51, local copies, waits for them, and re-layouts  4.6 us
    ppermute x2, starting transfers between devices, to_tp(): lax.ppermute(array, 'tp', [(i, (i + shift) % n_tp) for i in range(n_tp)])  4.24 us
  transfers between devices with their start and end apart: 26, of which 12 were waited for; matrix products, arithmetic and copies ran while one was open for 7% of the time, Pallas kernels for 18%

profile of v2, /device:TPU:0, one launch (start us, length us, event | category | flops | bytes accessed | tf_op | source)
XLA Modules:
  0.0 135.4 jit_solution(475823103398561808)
XLA Ops:
  1.4 3.0 %collective-permute-start.2 = (bf16[64,1024]{1,0:T(8,128)(2,1)S(1)}, bf16[64,1024]{1,0:T(8,128)(2,1)S(1)}, u32[]{:S(2)}, u32[]{:S(2)}) collective-permute-start(bf16[64,1024]{1,0:T(8,128)(2,1)S(1)} %constant_dynamic-slice_fusion.2), channel_id=1, source_target_pairs={{0,1},{1,0},{2,3},{3,2},{4,5},{5,4},{6,7},{7,6},{8,9},{9,8},{10,11... | collective-permute-start | bytes 393224 | tf_op jit(solution)/shard_map/ppermute | solution.py:528
  4.4 2.9 %constant_dynamic-slice_fusion.1 = bf16[2,2,512,384]{3,2,1,0:T(8,128)(2,1)} fusion(bf16[2,3,1024,384]{3,2,1,0:T(8,128)(2,1)} %refs_6_.1, s32[]{:T(128)S(6)} %select_n.61), kind=kLoop, calls=%fused_computation.10 | loop fusion | bytes 3145732 | tf_op jit(solution)/shard_map/dynamic_slice | solution.py:547
  8.6 1.6 %collective-permute-start = (bf16[2048,256]{1,0:T(8,128)(2,1)S(1)}, bf16[2048,256]{1,0:T(8,128)(2,1)}, u32[]{:S(2)}, u32[]{:S(2)}) collective-permute-start(bf16[2048,256]{1,0:T(8,128)(2,1)S(1)} %copy-done.1), channel_id=1, source_target_pairs={{0,4},{1,5},{2,6},{3,7},{4,0},{5,1},{6,2},{7,3},{8,12},{9,13},{10,... | collective-permute-start | bytes 3145736 | tf_op jit(solution)/shard_map/ppermute | solution.py:522
  11.0 1.2 copy-done.2
  12.2 4.0 %attention.1.refs_0_ = bf16[128,2048]{1,0:T(8,128)(2,1)S(1)} custom-call(s32[1]{0:T(128)S(6)} %copy.16.length_ref, bf16[2,64,2048]{2,1,0:T(8,128)(2,1)S(1)} %copy-done.4, bf16[1,2,1024,256]{3,2,1,0:T(8,128)(2,1)S(1)} %copy-done.2, bf16[128,512]{1,0:T(8,128)(2,1)S(1)} %bitcast.17), custom_call_target="tpu_custom_call" | custom-call | flops 1000 | bytes 1000 | tf_op jit(solution)/shard_map/attention/pallas_call | solution.py:114
  16.2 2.7 %collective-permute-start.4 = (bf16[128,2048]{1,0:T(8,128)(2,1)S(1)}, bf16[128,2048]{1,0:T(8,128)(2,1)S(1)}, u32[]{:S(2)}, u32[]{:S(2)}) collective-permute-start(bf16[128,2048]{1,0:T(8,128)(2,1)S(1)} %attention.1.refs_0_), channel_id=1, source_target_pairs={{0,8},{1,9},{2,10},{3,11},{4,12},{5,13},{6,14},{7,15},{8,0},{9,1},... | collective-permute-start | bytes 1572872 | tf_op jit(solution)/shard_map/ppermute | solution.py:522
  23.1 2.5 %fusion.1 = (bf16[2,1,512,384]{3,2,1,0:T(8,128)(2,1)}, bf16[2,1,512,384]{3,2,1,0:T(8,128)(2,1)S(1)}) fusion(bf16[2,3,1024,384]{3,2,1,0:T(8,128)(2,1)} %refs_6_.1), kind=kLoop, calls=%fused_computation.13 | loop fusion | bytes 3145728 | tf_op jit(solution)/shard_map/dynamic_slice | solution.py:547
  25.6 20.1 %collective-permute-done.refs_4_ = bf16[2048,256]{1,0:T(8,128)(2,1)} collective-permute-done((bf16[2048,256]{1,0:T(8,128)(2,1)S(1)}, bf16[2048,256]{1,0:T(8,128)(2,1)}, u32[]{:S(2)}, u32[]{:S(2)}) %collective-permute-start) | collective-permute-done | bytes 1048608 | tf_op jit(solution)/shard_map/ppermute | solution.py:522
  45.9 2.2 %out_projection.1.refs_3_ = f32[256,768]{1,0:T(8,128)S(1)} custom-call(s32[6]{0:T(128)S(1)} %stack.36.place_ref, bf16[128,2048]{1,0:T(8,128)(2,1)S(1)} %attention.1.refs_0_, bf16[128,2048]{1,0:T(8,128)(2,1)S(1)} %collective-permute-done.4.refs_1_, bf16[2048,256]{1,0:T(8,128)(2,1)S(1)} %copy-done.1, bf16[2048,256]{1,0:T(8,128)(2,1)S(1)} %collective-permute-done.1.refs_3_, ...), custom_call_target="tpu_custom_call" | custom-call | flops 1000 | bytes 1000 | tf_op jit(solution)/shard_map/out_projection/pallas_call | solution.py:144
  49.8 1.5 %collective-permute-start.14 = (bf16[2,2,512,384]{3,2,1,0:T(8,128)(2,1)}, bf16[2,2,512,384]{3,2,1,0:T(8,128)(2,1)S(1)}, u32[]{:S(2)}, u32[]{:S(2)}) collective-permute-start(bf16[2,2,512,384]{3,2,1,0:T(8,128)(2,1)} %collective-permute-done.3.refs_10_), channel_id=1, source_target_pairs={{0,16},{16,0},{1,17},{17,1},{2,18},{18,2},{3,19},{19,3},{4,20},{20... | collective-permute-start | bytes 4718600 | tf_op jit(solution)/shard_map/ppermute | solution.py:531
  51.4 1.2 collective-permute-start.7
  52.6 2.4 %collective-permute-start.9 = (bf16[64,1152]{1,0:T(8,128)(2,1)S(1)}, bf16[64,1152]{1,0:T(8,128)(2,1)S(1)}, u32[]{:S(2)}, u32[]{:S(2)}) collective-permute-start(bf16[64,1152]{1,0:T(8,128)(2,1)S(1)} %get-tuple-element.67), channel_id=1, source_target_pairs={{0,8},{1,9},{2,10},{3,11},{4,12},{5,13},{6,14},{7,15},{8,0},{9,1},... | collective-permute-start | bytes 442376 | tf_op jit(solution)/shard_map/ppermute | solution.py:522
  55.0 5.4 %collective-permute-done.7.refs_0_.refs_1_ = bf16[144,1024]{1,0:T(8,128)(2,1)S(1)} collective-permute-done((bf16[144,1024]{1,0:T(8,128)(2,1)S(1)}, bf16[144,1024]{1,0:T(8,128)(2,1)S(1)}, u32[]{:S(2)}, u32[]{:S(2)}) %collective-permute-start.7) | collective-permute-done | bytes 294944 | tf_op jit(solution)/shard_map/ppermute | solution.py:528
  60.4 1.8 %collective-permute-done.9.refs_2_ = bf16[64,1152]{1,0:T(8,128)(2,1)S(1)} collective-permute-done((bf16[64,1152]{1,0:T(8,128)(2,1)S(1)}, bf16[64,1152]{1,0:T(8,128)(2,1)S(1)}, u32[]{:S(2)}, u32[]{:S(2)}) %collective-permute-start.9) | collective-permute-done | bytes 147488 | tf_op jit(solution)/shard_map/ppermute | solution.py:522
  63.8 3.4 %collective-permute-start.11 = (bf16[128,1024]{1,0:T(8,128)(2,1)S(1)}, bf16[128,1024]{1,0:T(8,128)(2,1)S(1)}, u32[]{:S(2)}, u32[]{:S(2)}) collective-permute-start(bf16[128,1024]{1,0:T(8,128)(2,1)S(1)} %get-tuple-element.69), channel_id=1, source_target_pairs={{0,8},{1,9},{2,10},{3,11},{4,12},{5,13},{6,14},{7,15},{8,0},{9,1},... | collective-permute-start | bytes 786440 | tf_op jit(solution)/shard_map/ppermute | solution.py:522
  67.2 9.5 %collective-permute-done.11.refs_4_ = bf16[128,1024]{1,0:T(8,128)(2,1)S(1)} collective-permute-done((bf16[128,1024]{1,0:T(8,128)(2,1)S(1)}, bf16[128,1024]{1,0:T(8,128)(2,1)S(1)}, u32[]{:S(2)}, u32[]{:S(2)}) %collective-permute-start.11) | collective-permute-done | bytes 262176 | tf_op jit(solution)/shard_map/ppermute | solution.py:522
  76.7 1.7 %collective-permute-done.10.refs_3_ = bf16[128,1152]{1,0:T(8,128)(2,1)S(1)} collective-permute-done((bf16[128,1152]{1,0:T(8,128)(2,1)S(1)}, bf16[128,1152]{1,0:T(8,128)(2,1)S(1)}, u32[]{:S(2)}, u32[]{:S(2)}) %collective-permute-start.10) | collective-permute-done | bytes 294944 | tf_op jit(solution)/shard_map/ppermute | solution.py:522
  78.4 2.1 %collective-permute-start.12 = (bf16[128,1024]{1,0:T(8,128)(2,1)S(1)}, bf16[128,1024]{1,0:T(8,128)(2,1)S(1)}, u32[]{:S(2)}, u32[]{:S(2)}) collective-permute-start(bf16[128,1024]{1,0:T(8,128)(2,1)S(1)} %collective-permute-done.11.refs_4_), channel_id=1, source_target_pairs={{0,4},{1,5},{2,6},{3,7},{4,0},{5,1},{6,2},{7,3},{8,12},{9,13},{10,... | collective-permute-start | bytes 786440 | tf_op jit(solution)/shard_map/ppermute | solution.py:522
  80.5 6.4 %collective-permute-done.12.refs_5_ = bf16[128,1024]{1,0:T(8,128)(2,1)S(1)} collective-permute-done((bf16[128,1024]{1,0:T(8,128)(2,1)S(1)}, bf16[128,1024]{1,0:T(8,128)(2,1)S(1)}, u32[]{:S(2)}, u32[]{:S(2)}) %collective-permute-start.12) | collective-permute-done | bytes 262176 | tf_op jit(solution)/shard_map/ppermute | solution.py:522
  87.0 1.3 collective-permute-start.19
  88.3 2.0 %collective-permute-done.15.refs_9_ = bf16[2,2,512,384]{3,2,1,0:T(8,128)(2,1)S(1)} collective-permute-done((bf16[2,2,512,384]{3,2,1,0:T(8,128)(2,1)S(1)}, bf16[2,2,512,384]{3,2,1,0:T(8,128)(2,1)S(1)}, u32[]{:S(2)}, u32[]{:S(2)}) %collective-permute-start.15) | collective-permute-done | bytes 1572896 | tf_op jit(solution)/shard_map/ppermute | solution.py:525
  91.6 11.7 %units.1 = (bf16[256,1536]{1,0:T(8,128)(2,1)}, bf16[256,2048]{1,0:T(8,128)(2,1)}, f32[64,1024]{1,0:T(8,128)}, bf16[64,1024]{1,0:T(8,128)(2,1)}, bf16[64,1024]{1,0:T(8,128)(2,1)}, /*index=5*/bf16[64,1024]{1,0:T(8,128)(2,1)}) custom-call(s32[6]{0:T(128)} %copy-done.10, s32[1,16]{1,0:T(1,128)} %constant_dynamic-slice_fusion.table_ref, ...), custom_call_target="tpu_custom_call" | custom-call | flops 1000 | bytes 1000 | tf_op jit(solution)/shard_map/units/pallas_call | solution.py:386
  103.3 3.2 %collective-permute-done.19.refs_3_ = bf16[2,1,512,384]{3,2,1,0:T(8,128)(2,1)S(1)} collective-permute-done((bf16[2,1,512,384]{3,2,1,0:T(8,128)(2,1)}, bf16[2,1,512,384]{3,2,1,0:T(8,128)(2,1)S(1)}, u32[]{:S(2)}, u32[]{:S(2)}) %collective-permute-start.19) | collective-permute-done | bytes 786464 | tf_op jit(solution)/shard_map/ppermute | solution.py:522
  107.1 2.1 %collective-permute-start.16 = (bf16[64,1024]{1,0:T(8,128)(2,1)}, bf16[64,1024]{1,0:T(8,128)(2,1)S(1)}, u32[]{:S(2)}, u32[]{:S(2)}) collective-permute-start(bf16[64,1024]{1,0:T(8,128)(2,1)} %get-tuple-element.81), channel_id=1, source_target_pairs={{0,4},{1,5},{2,6},{3,7},{4,0},{5,1},{6,2},{7,3},{8,12},{9,13},{10,... | collective-permute-start | bytes 393224 | tf_op jit(solution)/shard_map/ppermute | solution.py:522
  109.1 1.7 %collective-permute-start.17 = (bf16[64,1024]{1,0:T(8,128)(2,1)}, bf16[64,1024]{1,0:T(8,128)(2,1)S(1)}, u32[]{:S(2)}, u32[]{:S(2)}) collective-permute-start(bf16[64,1024]{1,0:T(8,128)(2,1)} %get-tuple-element.82), channel_id=1, source_target_pairs={{0,8},{1,9},{2,10},{3,11},{4,12},{5,13},{6,14},{7,15},{8,0},{9,1},... | collective-permute-start | bytes 393224 | tf_op jit(solution)/shard_map/ppermute | solution.py:522
  112.7 5.2 %features.1 = (bf16[64,1024]{1,0:T(8,128)(2,1)}, bf16[64,1024]{1,0:T(8,128)(2,1)}, bf16[64,1024]{1,0:T(8,128)(2,1)}, bf16[64,1024]{1,0:T(8,128)(2,1)}) custom-call(s32[6]{0:T(128)} %copy-done.10, bf16[256,1536]{1,0:T(8,128)(2,1)} %get-tuple-element.84.hidden_ref, bf16[256,2048]{1,0:T(8,128)(2,1)} %get-tuple-element.85.resid_ref, ...), custom_call_target="tpu_custom_call" | custom-call | flops 1000 | bytes 1000 | tf_op jit(solution)/shard_map/features/pallas_call | solution.py:416
  117.9 1.3 collective-permute-start.22
  119.2 1.4 collective-permute-start.23
  120.6 3.3 %collective-permute-start.24 = (bf16[64,1024]{1,0:T(8,128)(2,1)}, bf16[64,1024]{1,0:T(8,128)(2,1)S(1)}, u32[]{:S(2)}, u32[]{:S(2)}) collective-permute-start(bf16[64,1024]{1,0:T(8,128)(2,1)} %get-tuple-element.91), channel_id=1, source_target_pairs={{0,9},{1,8},{2,11},{3,10},{4,13},{5,12},{6,15},{7,14},{8,1},{9,0},... | collective-permute-start | bytes 393224 | tf_op jit(solution)/shard_map/ppermute | solution.py:522
  124.8 2.4 %collective-permute-done.22.refs_4_ = bf16[64,1024]{1,0:T(8,128)(2,1)S(1)} collective-permute-done((bf16[64,1024]{1,0:T(8,128)(2,1)}, bf16[64,1024]{1,0:T(8,128)(2,1)S(1)}, u32[]{:S(2)}, u32[]{:S(2)}) %collective-permute-start.22) | collective-permute-done | bytes 131104 | tf_op jit(solution)/shard_map/ppermute | solution.py:522
  127.2 6.8 %collective-permute-done.24.refs_6_ = bf16[64,1024]{1,0:T(8,128)(2,1)S(1)} collective-permute-done((bf16[64,1024]{1,0:T(8,128)(2,1)}, bf16[64,1024]{1,0:T(8,128)(2,1)S(1)}, u32[]{:S(2)}, u32[]{:S(2)}) %collective-permute-start.24) | collective-permute-done | bytes 131104 | tf_op jit(solution)/shard_map/ppermute | solution.py:522
  134.0 1.4 %mix.1 = bf16[128,1024]{1,0:T(8,128)(2,1)} custom-call(s32[6]{0:T(128)S(1)} %copy-done.11, f32[64,1024]{1,0:T(8,128)S(1)} %copy-done.6, bf16[64,1024]{1,0:T(8,128)(2,1)S(1)} %collective-permute-done.16.refs_1_, bf16[64,1024]{1,0:T(8,128)(2,1)S(1)} %collective-permute-done.17.refs_2_, bf16[64,1024]{1,0:T(8,128)(2,1)S(1)} %collective-permute-done.18.refs_3_, ...), custom_call_target="tpu_custom_call" | custom-call | flops 1000 | bytes 1000 | tf_op jit(solution)/shard_map/mix/pallas_call | solution.py:479
  (91 shorter events, 15.1 us)
Async XLA Ops:
  0.0 45.7 %collective-permute-start.5 = (bf16[2,3,1024,384]{3,2,1,0:T(8,128)(2,1)}, bf16[2,3,1024,384]{3,2,1,0:T(8,128)(2,1)}, u32[]{:S(2)}, u32[]{:S(2)}) collective-permute-start(bf16[2,3,1024,384]{3,2,1,0:T(8,128)(2,1)} %refs_6_.1), channel_id=1, source_target_pairs={{0,2},{2,0},{4,6},{6,4},{8,10},{10,8},{12,14},{14,12},{1,3},{3,1},... | collective-permute-start | bytes 14155784 | tf_op jit(solution)/shard_map/ppermute | solution.py:525
  0.5 10.5 %collective-permute-start.1 = (bf16[2048,256]{1,0:T(8,128)(2,1)}, bf16[2048,256]{1,0:T(8,128)(2,1)S(1)}, u32[]{:S(2)}, u32[]{:S(2)}) collective-permute-start(bf16[2048,256]{1,0:T(8,128)(2,1)} %refs_2_), channel_id=1, source_target_pairs={{0,2},{2,0},{4,6},{6,4},{8,10},{10,8},{12,14},{14,12},{1,3},{3,1},... | collective-permute-start | bytes 3145736 | tf_op jit(solution)/shard_map/ppermute | solution.py:525
  1.4 6.7 %collective-permute-start.2 = (bf16[64,1024]{1,0:T(8,128)(2,1)S(1)}, bf16[64,1024]{1,0:T(8,128)(2,1)S(1)}, u32[]{:S(2)}, u32[]{:S(2)}) collective-permute-start(bf16[64,1024]{1,0:T(8,128)(2,1)S(1)} %constant_dynamic-slice_fusion.2), channel_id=1, source_target_pairs={{0,1},{1,0},{2,3},{3,2},{4,5},{5,4},{6,7},{7,6},{8,9},{9,8},{10,11... | collective-permute-start | bytes 393224 | tf_op jit(solution)/shard_map/ppermute | solution.py:528
  8.1 37.6 %collective-permute-start.3 = (bf16[2,2,512,384]{3,2,1,0:T(8,128)(2,1)}, bf16[2,2,512,384]{3,2,1,0:T(8,128)(2,1)}, u32[]{:S(2)}, u32[]{:S(2)}) collective-permute-start(bf16[2,2,512,384]{3,2,1,0:T(8,128)(2,1)} %constant_dynamic-slice_fusion.1), channel_id=1, source_target_pairs={{0,3},{1,2},{2,1},{3,0},{4,7},{5,6},{6,5},{7,4},{8,11},{9,10},{10,... | collective-permute-start | bytes 4718600 | tf_op jit(solution)/shard_map/ppermute | solution.py:522
  8.6 37.1 %collective-permute-start = (bf16[2048,256]{1,0:T(8,128)(2,1)S(1)}, bf16[2048,256]{1,0:T(8,128)(2,1)}, u32[]{:S(2)}, u32[]{:S(2)}) collective-permute-start(bf16[2048,256]{1,0:T(8,128)(2,1)S(1)} %copy-done.1), channel_id=1, source_target_pairs={{0,4},{1,5},{2,6},{3,7},{4,0},{5,1},{6,2},{7,3},{8,12},{9,13},{10,... | collective-permute-start | bytes 3145736 | tf_op jit(solution)/shard_map/ppermute | solution.py:522
  11.0 51.2 %copy-start.10 = (s32[6]{0:T(128)}, s32[6]{0:T(128)S(1)}, u32[]{:S(2)}) copy-start(s32[6]{0:T(128)S(1)} %stack.36.place_ref) | copy-start | bytes 76
  16.2 29.5 %collective-permute-start.4 = (bf16[128,2048]{1,0:T(8,128)(2,1)S(1)}, bf16[128,2048]{1,0:T(8,128)(2,1)S(1)}, u32[]{:S(2)}, u32[]{:S(2)}) collective-permute-start(bf16[128,2048]{1,0:T(8,128)(2,1)S(1)} %attention.1.refs_0_), channel_id=1, source_target_pairs={{0,8},{1,9},{2,10},{3,11},{4,12},{5,13},{6,14},{7,15},{8,0},{9,1},... | collective-permute-start | bytes 1572872 | tf_op jit(solution)/shard_map/ppermute | solution.py:522
  45.7 2.9 %collective-permute-start.6 = (bf16[2048,256]{1,0:T(8,128)(2,1)}, bf16[2048,256]{1,0:T(8,128)(2,1)S(1)}, u32[]{:S(2)}, u32[]{:S(2)}) collective-permute-start(bf16[2048,256]{1,0:T(8,128)(2,1)} %collective-permute-done.refs_4_), channel_id=1, source_target_pairs={{0,2},{2,0},{4,6},{6,4},{8,10},{10,8},{12,14},{14,12},{1,3},{3,1},... | collective-permute-start | bytes 3145736 | tf_op jit(solution)/shard_map/ppermute | solution.py:525
  49.6 10.7 %collective-permute-start.8 = (bf16[2,2,512,384]{3,2,1,0:T(8,128)(2,1)}, bf16[2,2,512,384]{3,2,1,0:T(8,128)(2,1)S(1)}, u32[]{:S(2)}, u32[]{:S(2)}) collective-permute-start(bf16[2,2,512,384]{3,2,1,0:T(8,128)(2,1)} %collective-permute-done.3.refs_10_), channel_id=1, source_target_pairs={{0,2},{2,0},{4,6},{6,4},{8,10},{10,8},{12,14},{14,12},{1,3},{3,1},... | collective-permute-start | bytes 4718600 | tf_op jit(solution)/shard_map/ppermute | solution.py:525
  49.8 37.1 %collective-permute-start.14 = (bf16[2,2,512,384]{3,2,1,0:T(8,128)(2,1)}, bf16[2,2,512,384]{3,2,1,0:T(8,128)(2,1)S(1)}, u32[]{:S(2)}, u32[]{:S(2)}) collective-permute-start(bf16[2,2,512,384]{3,2,1,0:T(8,128)(2,1)} %collective-permute-done.3.refs_10_), channel_id=1, source_target_pairs={{0,16},{16,0},{1,17},{17,1},{2,18},{18,2},{3,19},{19,3},{4,20},{20... | collective-permute-start | bytes 4718600 | tf_op jit(solution)/shard_map/ppermute | solution.py:531
  51.4 9.0 %collective-permute-start.7 = (bf16[144,1024]{1,0:T(8,128)(2,1)S(1)}, bf16[144,1024]{1,0:T(8,128)(2,1)S(1)}, u32[]{:S(2)}, u32[]{:S(2)}) collective-permute-start(bf16[144,1024]{1,0:T(8,128)(2,1)S(1)} %get-tuple-element.61), channel_id=1, source_target_pairs={{0,1},{1,0},{2,3},{3,2},{4,5},{5,4},{6,7},{7,6},{8,9},{9,8},{10,11... | collective-permute-start | bytes 884744 | tf_op jit(solution)/shard_map/ppermute | solution.py:528
  52.6 9.6 %collective-permute-start.9 = (bf16[64,1152]{1,0:T(8,128)(2,1)S(1)}, bf16[64,1152]{1,0:T(8,128)(2,1)S(1)}, u32[]{:S(2)}, u32[]{:S(2)}) collective-permute-start(bf16[64,1152]{1,0:T(8,128)(2,1)S(1)} %get-tuple-element.67), channel_id=1, source_target_pairs={{0,8},{1,9},{2,10},{3,11},{4,12},{5,13},{6,14},{7,15},{8,0},{9,1},... | collective-permute-start | bytes 442376 | tf_op jit(solution)/shard_map/ppermute | solution.py:522
  60.4 30.0 %copy-start = (bf16[144,1024]{1,0:T(8,128)(2,1)}, bf16[144,1024]{1,0:T(8,128)(2,1)S(1)}, u32[]{:S(2)}) copy-start(bf16[144,1024]{1,0:T(8,128)(2,1)S(1)} %collective-permute-done.7.refs_0_.refs_1_) | copy-start | bytes 884740
  60.4 30.0 %copy-start.12 = (bf16[2,2,512,384]{3,2,1,0:T(8,128)(2,1)}, bf16[2,2,512,384]{3,2,1,0:T(8,128)(2,1)S(1)}, u32[]{:S(2)}) copy-start(bf16[2,2,512,384]{3,2,1,0:T(8,128)(2,1)S(1)} %collective-permute-done.8.refs_8_) | copy-start | bytes 4718596
  62.8 27.6 %copy-start.5 = (bf16[128,1152]{1,0:T(8,128)(2,1)}, bf16[128,1152]{1,0:T(8,128)(2,1)S(1)}, u32[]{:S(2)}) copy-start(bf16[128,1152]{1,0:T(8,128)(2,1)S(1)} %get-tuple-element.75.refs_2_) | copy-start | bytes 884740
  62.9 24.0 %collective-permute-start.13 = (bf16[2,1,512,384]{3,2,1,0:T(8,128)(2,1)S(1)}, bf16[2,1,512,384]{3,2,1,0:T(8,128)(2,1)S(1)}, u32[]{:S(2)}, u32[]{:S(2)}) collective-permute-start(bf16[2,1,512,384]{3,2,1,0:T(8,128)(2,1)S(1)} %get-tuple-element.73), channel_id=1, source_target_pairs={{0,3},{1,2},{2,1},{3,0},{4,7},{5,6},{6,5},{7,4},{8,11},{9,10},{10,... | collective-permute-start | bytes 2359304 | tf_op jit(solution)/shard_map/ppermute | solution.py:522
  62.9 15.4 %collective-permute-start.10 = (bf16[128,1152]{1,0:T(8,128)(2,1)S(1)}, bf16[128,1152]{1,0:T(8,128)(2,1)S(1)}, u32[]{:S(2)}, u32[]{:S(2)}) collective-permute-start(bf16[128,1152]{1,0:T(8,128)(2,1)S(1)} %get-tuple-element.75.refs_2_), channel_id=1, source_target_pairs={{0,4},{1,5},{2,6},{3,7},{4,0},{5,1},{6,2},{7,3},{8,12},{9,13},{10,... | collective-permute-start | bytes 884744 | tf_op jit(solution)/shard_map/ppermute | solution.py:522
  63.8 12.9 %collective-permute-start.11 = (bf16[128,1024]{1,0:T(8,128)(2,1)S(1)}, bf16[128,1024]{1,0:T(8,128)(2,1)S(1)}, u32[]{:S(2)}, u32[]{:S(2)}) collective-permute-start(bf16[128,1024]{1,0:T(8,128)(2,1)S(1)} %get-tuple-element.69), channel_id=1, source_target_pairs={{0,8},{1,9},{2,10},{3,11},{4,12},{5,13},{6,14},{7,15},{8,0},{9,1},... | collective-permute-start | bytes 786440 | tf_op jit(solution)/shard_map/ppermute | solution.py:522
  78.4 8.5 %collective-permute-start.12 = (bf16[128,1024]{1,0:T(8,128)(2,1)S(1)}, bf16[128,1024]{1,0:T(8,128)(2,1)S(1)}, u32[]{:S(2)}, u32[]{:S(2)}) collective-permute-start(bf16[128,1024]{1,0:T(8,128)(2,1)S(1)} %collective-permute-done.11.refs_4_), channel_id=1, source_target_pairs={{0,4},{1,5},{2,6},{3,7},{4,0},{5,1},{6,2},{7,3},{8,12},{9,13},{10,... | collective-permute-start | bytes 786440 | tf_op jit(solution)/shard_map/ppermute | solution.py:522
  86.9 3.5 %collective-permute-start.15 = (bf16[2,2,512,384]{3,2,1,0:T(8,128)(2,1)S(1)}, bf16[2,2,512,384]{3,2,1,0:T(8,128)(2,1)S(1)}, u32[]{:S(2)}, u32[]{:S(2)}) collective-permute-start(bf16[2,2,512,384]{3,2,1,0:T(8,128)(2,1)S(1)} %collective-permute-done.14.refs_11_), channel_id=1, source_target_pairs={{0,2},{2,0},{4,6},{6,4},{8,10},{10,8},{12,14},{14,12},{1,3},{3,1},... | collective-permute-start | bytes 4718600 | tf_op jit(solution)/shard_map/ppermute | solution.py:525
  87.0 19.5 %collective-permute-start.19 = (bf16[2,1,512,384]{3,2,1,0:T(8,128)(2,1)}, bf16[2,1,512,384]{3,2,1,0:T(8,128)(2,1)S(1)}, u32[]{:S(2)}, u32[]{:S(2)}) collective-permute-start(bf16[2,1,512,384]{3,2,1,0:T(8,128)(2,1)} %get-tuple-element.86), channel_id=1, source_target_pairs={{0,3},{1,2},{2,1},{3,0},{4,7},{5,6},{6,5},{7,4},{8,11},{9,10},{10,... | collective-permute-start | bytes 2359304 | tf_op jit(solution)/shard_map/ppermute | solution.py:522
  106.6 5.0 %collective-permute-start.20 = (bf16[2,1,512,384]{3,2,1,0:T(8,128)(2,1)S(1)}, bf16[2,1,512,384]{3,2,1,0:T(8,128)(2,1)S(1)}, u32[]{:S(2)}, u32[]{:S(2)}) collective-permute-start(bf16[2,1,512,384]{3,2,1,0:T(8,128)(2,1)S(1)} %collective-permute-done.13.refs_1_), channel_id=1, source_target_pairs={{0,2},{2,0},{4,6},{6,4},{8,10},{10,8},{12,14},{14,12},{1,3},{3,1},... | collective-permute-start | bytes 2359304 | tf_op jit(solution)/shard_map/ppermute | solution.py:525
  106.9 4.6 %collective-permute-start.21 = (bf16[2,1,512,384]{3,2,1,0:T(8,128)(2,1)S(1)}, bf16[2,1,512,384]{3,2,1,0:T(8,128)(2,1)S(1)}, u32[]{:S(2)}, u32[]{:S(2)}) collective-permute-start(bf16[2,1,512,384]{3,2,1,0:T(8,128)(2,1)S(1)} %collective-permute-done.19.refs_3_), channel_id=1, source_target_pairs={{0,2},{2,0},{4,6},{6,4},{8,10},{10,8},{12,14},{14,12},{1,3},{3,1},... | collective-permute-start | bytes 2359304 | tf_op jit(solution)/shard_map/ppermute | solution.py:525
  107.1 13.5 %collective-permute-start.16 = (bf16[64,1024]{1,0:T(8,128)(2,1)}, bf16[64,1024]{1,0:T(8,128)(2,1)S(1)}, u32[]{:S(2)}, u32[]{:S(2)}) collective-permute-start(bf16[64,1024]{1,0:T(8,128)(2,1)} %get-tuple-element.81), channel_id=1, source_target_pairs={{0,4},{1,5},{2,6},{3,7},{4,0},{5,1},{6,2},{7,3},{8,12},{9,13},{10,... | collective-permute-start | bytes 393224 | tf_op jit(solution)/shard_map/ppermute | solution.py:522
  109.1 14.7 %collective-permute-start.17 = (bf16[64,1024]{1,0:T(8,128)(2,1)}, bf16[64,1024]{1,0:T(8,128)(2,1)S(1)}, u32[]{:S(2)}, u32[]{:S(2)}) collective-permute-start(bf16[64,1024]{1,0:T(8,128)(2,1)} %get-tuple-element.82), channel_id=1, source_target_pairs={{0,8},{1,9},{2,10},{3,11},{4,12},{5,13},{6,14},{7,15},{8,0},{9,1},... | collective-permute-start | bytes 393224 | tf_op jit(solution)/shard_map/ppermute | solution.py:522
  110.8 13.9 %collective-permute-start.18 = (bf16[64,1024]{1,0:T(8,128)(2,1)}, bf16[64,1024]{1,0:T(8,128)(2,1)S(1)}, u32[]{:S(2)}, u32[]{:S(2)}) collective-permute-start(bf16[64,1024]{1,0:T(8,128)(2,1)} %get-tuple-element.83), channel_id=1, source_target_pairs={{0,12},{1,13},{2,14},{3,15},{4,8},{5,9},{6,10},{7,11},{8,4},{9,5},... | collective-permute-start | bytes 393224 | tf_op jit(solution)/shard_map/ppermute | solution.py:522
  112.7 21.3 %copy-start.6 = (f32[64,1024]{1,0:T(8,128)S(1)}, f32[64,1024]{1,0:T(8,128)}, u32[]{:S(2)}) copy-start(f32[64,1024]{1,0:T(8,128)} %get-tuple-element.80.refs_0_) | copy-start | bytes 786436
  112.7 21.3 %copy-start.11 = (s32[6]{0:T(128)S(1)}, s32[6]{0:T(128)}, u32[]{:S(2)}) copy-start(s32[6]{0:T(128)} %copy-done.10) | copy-start | bytes 76
  117.9 9.3 %collective-permute-start.22 = (bf16[64,1024]{1,0:T(8,128)(2,1)}, bf16[64,1024]{1,0:T(8,128)(2,1)S(1)}, u32[]{:S(2)}, u32[]{:S(2)}) collective-permute-start(bf16[64,1024]{1,0:T(8,128)(2,1)} %get-tuple-element.89), channel_id=1, source_target_pairs={{0,1},{1,0},{2,3},{3,2},{4,5},{5,4},{6,7},{7,6},{8,9},{9,8},{10,11... | collective-permute-start | bytes 393224 | tf_op jit(solution)/shard_map/ppermute | solution.py:522
  119.2 8.0 %collective-permute-start.23 = (bf16[64,1024]{1,0:T(8,128)(2,1)}, bf16[64,1024]{1,0:T(8,128)(2,1)S(1)}, u32[]{:S(2)}, u32[]{:S(2)}) collective-permute-start(bf16[64,1024]{1,0:T(8,128)(2,1)} %get-tuple-element.90), channel_id=1, source_target_pairs={{0,5},{1,4},{2,7},{3,6},{4,1},{5,0},{6,3},{7,2},{8,13},{9,12},{10,... | collective-permute-start | bytes 393224 | tf_op jit(solution)/shard_map/ppermute | solution.py:522
  120.6 13.5 %collective-permute-start.24 = (bf16[64,1024]{1,0:T(8,128)(2,1)}, bf16[64,1024]{1,0:T(8,128)(2,1)S(1)}, u32[]{:S(2)}, u32[]{:S(2)}) collective-permute-start(bf16[64,1024]{1,0:T(8,128)(2,1)} %get-tuple-element.91), channel_id=1, source_target_pairs={{0,9},{1,8},{2,11},{3,10},{4,13},{5,12},{6,15},{7,14},{8,1},{9,0},... | collective-permute-start | bytes 393224 | tf_op jit(solution)/shard_map/ppermute | solution.py:522
  123.8 10.2 %collective-permute-start.25 = (bf16[64,1024]{1,0:T(8,128)(2,1)}, bf16[64,1024]{1,0:T(8,128)(2,1)S(1)}, u32[]{:S(2)}, u32[]{:S(2)}) collective-permute-start(bf16[64,1024]{1,0:T(8,128)(2,1)} %get-tuple-element.92), channel_id=1, source_target_pairs={{0,13},{1,12},{2,15},{3,14},{4,9},{5,8},{6,11},{7,10},{8,5},{9,4},... | collective-permute-start | bytes 393224 | tf_op jit(solution)/shard_map/ppermute | solution.py:522
  (19 other events, 124.6 us)

commit v3 on v2

--- a/solution.py
+++ b/solution.py
@@ -26,7 +26,7 @@
 
 
 def unplaced():
-    return pl.BlockSpec(memory_space=pl.ANY)
+    return pl.BlockSpec(memory_space=pltpu.HBM)
 
 
 def params(mib):
@@ -226,43 +226,50 @@
     )(place, keep, *terms, *hidden)
 
 
+def hold_kernel(count, *refs):
+    sems = refs[-1]
+    copies = [
+        pltpu.make_async_copy(refs[n], refs[count + n], sems.at[n]) for n in range(count)
+    ]
+    for copy in copies:
+        copy.start()
+    for copy in copies:
+        copy.wait()
+
+
+def hold(arrays):
+    return pl.pallas_call(
+        functools.partial(hold_kernel, len(arrays)),
+        out_shape=[pltpu.VMEM(array.shape, array.dtype) for array in arrays],
+        in_specs=[unplaced()] * len(arrays),
+        out_specs=[whole()] * len(arrays),
+        scratch_shapes=[pltpu.SemaphoreType.DMA((len(arrays),))],
+        compiler_params=params(2),
+        cost_estimate=COST,
+        name="hold",
+    )(*arrays)
+
+
 def units_kernel(n_tp, n_z, n_rep, place_ref, table_ref, *refs):
     t, z, core, rep = place_ref[0], place_ref[1], place_ref[2], place_ref[3]
     z_lo, z_hi = place_ref[4], place_ref[5]
     m = n_z // n_tp
     routers, pieces, refs = refs[:n_tp], refs[n_tp : n_tp + n_z], refs[n_tp + n_z :]
     own_refs, refs = refs[:CORES], refs[CORES:]
-    n_far = CORES * (n_tp - 1) * n_rep
-    far_refs, refs = refs[:n_far], refs[n_far:]
-    hidden_ref, resid_ref, *outs = refs[:-6]
-    normed, chosen_ref, total, near_held, far_held, sems = refs[-6:]
+    n_far = CORES * (n_tp - 1)
+    first_refs, passed_refs, refs = refs[:n_far], refs[n_far : 2 * n_far], refs[2 * n_far :]
+    hidden_ref, far_resid_ref, *outs = refs[:-6]
+    resid_ref, normed, chosen_ref, total, passed_held, sems = refs[-6:]
     local, _, quarter, units = own_refs[0].shape
     tokens, width = resid_ref.shape
     chunk = tokens // n_z
     experts = routers[0].shape[0]
-    slots = CORES * local
-
-    arriving, later = [[] for _ in range(slots)], []
-    for slot in range(slots):
-        other, s = slot // local, slot % local
-        sources = [(own_refs[other].at[s, pl.ds(0, 2)], near_held.at[slot, pl.ds(0, 2)])]
-        for dt in range(1, n_tp):
-            for dy in range(n_rep):
-                far = far_refs[((dt - 1) * CORES + other) * n_rep + dy]
-                size = far.shape[2]
-                row = lax.rem(rep + dy, n_rep) * (quarter - size)
-                rows = pl.ds(pl.multiple_of(row, math.gcd(size, quarter - size)), size)
-                sources.append((far.at[s], far_held.at[dt - 1, slot, :, rows]))
-        for n, (source, target) in enumerate(sources):
-            copy = pltpu.make_async_copy(source, target, sems.at[slot, n])
-            copy.start()
-            arriving[slot].append(copy)
-    for slot in range(slots):
-        copy = pltpu.make_async_copy(
-            own_refs[slot // local].at[slot % local, 2], near_held.at[slot, 2], sems.at[slot, len(sources)]
-        )
+
+    arriving = []
+    for n in range(n_far):
+        copy = pltpu.make_async_copy(passed_refs[n], passed_held.at[n], sems.at[n])
         copy.start()
-        later.append(copy)
+        arriving.append(copy)
 
     for dz in range(n_z):
         row = pl.multiple_of((z_lo ^ (dz % m)) * (n_tp * chunk), n_tp * chunk)
@@ -287,29 +294,38 @@
     raised = jnp.where(chosen > 0, jnp.exp(logits), F32(0.0))
     combine = raised / jnp.sum(raised, 1, keepdims=True)
 
-    for slot in range(slots):
+    shares = []
+    for slot in range(CORES * local):
         other, s = slot // local, slot % local
         holder = jnp.where(core == 0, other, 1 - other)
         number = (z * CORES + holder) * local + s
-        share_of = jnp.sum(
-            jnp.where(table_ref[...] == number, combine, F32(0.0)), 1, keepdims=True
+        shares.append(
+            jnp.sum(jnp.where(table_ref[...] == number, combine, F32(0.0)), 1, keepdims=True)
         )
-        for copy in arriving[slot]:
+    share = quarter // n_rep
+    near = normed[:, pl.ds(pl.multiple_of(t * quarter, quarter), quarter)]
+    for other in range(CORES):
+        for copy in arriving[other * (n_tp - 1) : (other + 1) * (n_tp - 1)]:
             copy.wait()
-        x = normed[:, pl.ds(pl.multiple_of(t * quarter, quarter), quarter)]
-        gate = jnp.dot(x, near_held[slot, 0], preferred_element_type=F32)
-        up = jnp.dot(x, near_held[slot, 1], preferred_element_type=F32)
-        for dt in range(1, n_tp):
-            at = lax.rem(t - dt + n_tp, n_tp) * quarter
-            x = normed[:, pl.ds(pl.multiple_of(at, quarter), quarter)]
-            gate = gate + jnp.dot(x, far_held[dt - 1, slot, 0], preferred_element_type=F32)
-            up = up + jnp.dot(x, far_held[dt - 1, slot, 1], preferred_element_type=F32)
-        acted = (gate / (1.0 + jnp.exp(-gate))) * up
-        hidden_ref[:, pl.ds(slot * units, units)] = (acted * share_of).astype(BF16)
-
-    for copy in later:
-        copy.wait()
-    lower([(near_held, slot, 2) for slot in range(slots)], hidden_ref, total, 0)
+        for s in range(local):
+            both = []
+            for matrix in range(2):
+                terms = jnp.dot(near, own_refs[other][s, matrix], preferred_element_type=F32)
+                for dt in range(1, n_tp):
+                    n = other * (n_tp - 1) + dt - 1
+                    base = lax.rem(t - dt + n_tp, n_tp) * quarter
+                    for dy, ref in ((0, first_refs[n]), (1, passed_held.at[n])):
+                        at = base + lax.rem(rep + dy, n_rep) * share
+                        x = normed[:, pl.ds(pl.multiple_of(at, share), share)]
+                        terms = terms + jnp.dot(x, ref[s, matrix], preferred_element_type=F32)
+                both.append(terms)
+            gate, up = both
+            acted = (gate / (1.0 + jnp.exp(-gate))) * up
+            slot = other * local + s
+            hidden_ref[:, pl.ds(slot * units, units)] = (acted * shares[slot]).astype(BF16)
+
+    down = [(own_refs[slot // local], slot % local, 2) for slot in range(CORES * local)]
+    lower(down, hidden_ref, total, 0, quarter)
     resid_lanes = pl.ds(pl.multiple_of(t * quarter, quarter), quarter)
     for dz in range(n_z):
         rows = token_rows(z_lo, z_hi, dz, m, n_tp, chunk)
@@ -317,6 +333,10 @@
         if dz == 0:
             value = value + resid_ref[rows, resid_lanes].astype(F32)
         outs[dz][...] = value.astype(outs[dz].dtype)
+    own_rows = token_rows(z_lo, z_hi, 0, m, n_tp, chunk)
+    for dt in range(1, n_tp):
+        lanes = pl.multiple_of(lax.rem(t - dt + n_tp, n_tp) * quarter, quarter)
+        far_resid_ref[dt - 1] = resid_ref[own_rows, pl.ds(lanes, quarter)]
 
 
 def token_rows(z_lo, z_hi, dz, m, n_tp, chunk):
@@ -324,106 +344,98 @@
     return pl.ds(pl.multiple_of(at * chunk, chunk), chunk)
 
 
-def lower(down, hidden_ref, total, start):
+def lower(down, hidden_ref, total, start, width):
     units = hidden_ref.shape[1] // len(down)
-    width = down[0][0].shape[-2]
     step = min(512, width)
     for at in range(0, width, step):
+        size = min(step, width - at)
         part = None
         for i, (ref, *index) in enumerate(down):
             term = lax.dot_general(
                 hidden_ref[:, pl.ds(i * units, units)],
-                ref[(*index, pl.ds(at, step))],
+                ref[(*index, pl.ds(at, size))],
                 (((1,), (1,)), ((), ())),
                 preferred_element_type=F32,
             )
             part = term if part is None else part + term
-        total[:, pl.ds(pl.multiple_of(start + at, step), step)] = part
+        total[:, pl.ds(start + at, size)] = part
 
 
 def features_kernel(n_tp, n_z, dt, place_ref, hidden_ref, resid_ref, *refs):
-    t, z_lo, z_hi = place_ref[0], place_ref[4], place_ref[5]
+    z_lo, z_hi = place_ref[4], place_ref[5]
     m = n_z // n_tp
-    sources, outs, (total, held, sems) = refs[:-3][: -n_z], refs[:-3][-n_z:], refs[-3:]
+    sources, refs = refs[: 2 * CORES], refs[2 * CORES :]
+    outs, total, helds, sems = refs[:n_z], refs[n_z], refs[n_z + 1 : -1], refs[-1]
     local = sources[0].shape[0]
-    parts = len(sources) // CORES
-    quarter = total.shape[1]
     chunk = hidden_ref.shape[0] // n_z
-    copies, at = [], 0
-    for part in range(parts):
-        size = sources[part * CORES].shape[2]
-        for other in range(CORES):
-            copy = pltpu.make_async_copy(
-                sources[part * CORES + other].at[:, 0],
-                held.at[pl.ds(other * local, local), pl.ds(at, size), :],
-                sems.at[part, other],
-            )
-            copy.start()
-            copies.append((copy, at, size))
-        at += size
-    for part in range(parts):
-        for copy, at, size in copies[part * CORES : (part + 1) * CORES]:
+    copies = []
+    for n, source in enumerate(sources):
+        copy = pltpu.make_async_copy(source, helds[n // CORES].at[n % CORES], sems.at[n])
+        copy.start()
+        copies.append(copy)
+    start = 0
+    for n, held in enumerate(helds):
+        for copy in copies[n * CORES : (n + 1) * CORES]:
             copy.wait()
-        down = [(held.at[:, pl.ds(at, size)], slot) for slot in range(CORES * local)]
-        lower(down, hidden_ref, total, at)
-    resid_lanes = pl.ds(pl.multiple_of(lax.rem(t - dt + n_tp, n_tp) * quarter, quarter), quarter)
+        down = [(held.at[slot // local], slot % local, 0) for slot in range(CORES * local)]
+        lower(down, hidden_ref, total, start, held.shape[3])
+        start += held.shape[3]
     for dz in range(n_z):
-        rows = token_rows(z_lo, z_hi, dz, m, n_tp, chunk)
-        value = total[rows, :]
+        value = total[token_rows(z_lo, z_hi, dz, m, n_tp, chunk), :]
         if dz == 0:
-            value = value + resid_ref[rows, resid_lanes].astype(F32)
+            value = value + resid_ref[dt - 1].astype(F32)
         outs[dz][...] = value.astype(outs[dz].dtype)
 
 
-def run_units(n_tp, n_rep, place, table, routers, pieces, weights):
+def run_units(n_tp, n_rep, place, table, routers, pieces, own, first, passed):
     n_z = len(pieces)
-    local, _, quarter, units = weights[0].shape
+    local, _, quarter, units = own[0].shape
     width = quarter * n_tp
     lanes = pieces[0].shape[1] - quarter
     tokens = pieces[0].shape[0] * (n_z // n_tp)
     part = (tokens // n_z, quarter)
     slots = CORES * local
+    n_far = CORES * (n_tp - 1)
     found = pl.pallas_call(
         functools.partial(units_kernel, n_tp, n_z, n_rep),
         out_shape=[
-            jax.ShapeDtypeStruct((tokens, CORES * local * units), BF16),
-            jax.ShapeDtypeStruct((tokens, width), BF16),
+            pltpu.VMEM((tokens, slots * units), BF16),
+            jax.ShapeDtypeStruct((n_tp - 1, *part), BF16),
         ]
         + [jax.ShapeDtypeStruct(part, BF16 if dz else F32) for dz in range(n_z)],
         in_specs=[scalars()]
-        + [whole()] * (1 + n_tp + len(pieces))
-        + [unplaced()] * len(weights),
+        + [whole()] * (1 + n_tp + len(pieces) + len(own) + len(first))
+        + [unplaced()] * n_far,
         out_specs=[whole()] * (2 + n_z),
         scratch_shapes=[
             pltpu.VMEM((tokens, width), BF16),
+            pltpu.VMEM((tokens, width), BF16),
             pltpu.VMEM((tokens, lanes), BF16),
             pltpu.VMEM((tokens, quarter), F32),
-            pltpu.VMEM((slots, 3, quarter, units), BF16),
-            pltpu.VMEM((n_tp - 1, slots, 2, quarter, units), BF16),
-            pltpu.SemaphoreType.DMA((slots, 2 + (n_tp - 1) * n_rep)),
+            pltpu.VMEM((n_far, *passed[0].shape), BF16),
+            pltpu.SemaphoreType.DMA((n_far,)),
         ],
-        compiler_params=params(56),
+        compiler_params=params(28),
         cost_estimate=COST,
         name="units",
-    )(place, table, *routers, *pieces, *weights)
+    )(place, table, *routers, *pieces, *own, *first, *passed)
     return found[0], found[1], found[2:]
 
 
-def run_features(n_tp, n_z, dt, place, hidden, resid, quarter, weights):
+def run_features(n_tp, n_z, dt, place, hidden, resid, weights):
     tokens = hidden.shape[0]
-    local = weights[0].shape[0]
-    part = (tokens // n_z, quarter)
+    part = resid.shape[1:]
     return pl.pallas_call(
         functools.partial(features_kernel, n_tp, n_z, dt),
         out_shape=[jax.ShapeDtypeStruct(part, BF16)] * n_z,
         in_specs=[scalars()] + [whole()] * 2 + [unplaced()] * len(weights),
         out_specs=[whole()] * n_z,
         scratch_shapes=[
-            pltpu.VMEM((tokens, quarter), F32),
-            pltpu.VMEM((CORES * local, quarter, hidden.shape[1] // (CORES * local)), BF16),
-            pltpu.SemaphoreType.DMA((len(weights) // CORES, CORES)),
+            pltpu.VMEM((tokens, part[1]), F32),
+            *[pltpu.VMEM((CORES, *array.shape), BF16) for array in weights[::CORES]],
+            pltpu.SemaphoreType.DMA((len(weights),)),
         ],
-        compiler_params=params(56),
+        compiler_params=params(16),
         cost_estimate=COST,
         name="features",
     )(place, hidden, resid, *weights)
@@ -568,18 +580,23 @@
     attention = attend(cache_lengths, queries, cache, fresh)
     pieces = over_z(attention, m, n_z)
     own_other = to_core(expert_weights)
+    own = hold(after([expert_weights, own_other], attention))
     expert_ids, weights, old_slots, router = after(
-        (expert_ids, expert_weights, old_slots, router_weight), attention
+        (expert_ids, expert_weights, old_slots, router_weight), own
     )
     outgoing = messages(
         n_tp, place, flat_hidden, expert_ids.reshape(rows, -1), swapped, experts
     )
-    blocks = [block_of(weights, (2, 3), n * quarter // 2, quarter // 2) for n in range(2)]
+    edge = max(LANES, 5 * quarter // 8 // LANES * LANES)
+    blocks = [
+        block_of(weights, (2, 3), first_row, last_row - first_row)
+        for first_row, last_row in ((0, edge), (edge, quarter))
+    ]
     router = router.T
     tables = slot_tables(old_slots, new_slots, moved_experts)
     table = lax.dynamic_slice_in_dim(tables, t * chunk // tokens, 1, 0)
     near, table, router, outgoing, blocks, first = after(
-        (near, table, router, outgoing, blocks, first), (pieces[1], own_other)
+        (near, table, router, outgoing, blocks, first), (pieces[1], own)
     )
     hidden = [outgoing[0]] + [to_z(outgoing[dh], dh * m) for dh in range(1, n_tp)]
     passed = [to_rep(array, 1) for array in first]
@@ -602,7 +619,8 @@
     wide = to_z(resid, m)
     blocks = after(blocks, resid)
     down = [far(blocks[0])]
-    wide = after(wide, near)
+    held = hold(after(first_other + first, resid))
+    wide = after(wide, (near, held))
     gathered = near + [wide]
     for dz in range(m + 1, n_z):
         step = dz & -dz
@@ -610,13 +628,18 @@
     gathered, blocks = after((gathered, blocks), (gathered, down))
     down.append(far(blocks[1]))
 
-    passed = after(passed, gathered)
+    passed, down[0] = after((passed, down[0]), gathered)
     passed_other = [to_core(array) for array in passed]
-    weights = [expert_weights, own_other]
-    for dt in range(n_tp - 1):
-        weights += [first_other[dt], passed_other[dt], first[dt], passed[dt]]
-    units, resid_all, own_parts = run_units(
-        n_tp, n_rep, place, table, [router] + terms, gathered, weights
+    units, far_resid, own_parts = run_units(
+        n_tp,
+        n_rep,
+        place,
+        table,
+        [router] + terms,
+        gathered,
+        own,
+        held,
+        passed_other + passed,
     )
     parts = [own_parts[0]] + [to_z(own_parts[dz], dz) for dz in range(1, n_z)]
     down = after(down, units)
@@ -624,7 +647,7 @@
         sources = []
         for arrays in down:
             sources += [to_core(arrays[dt - 1]), arrays[dt - 1]]
-        found = run_features(n_tp, n_z, dt, place, units, resid_all, quarter, sources)
+        found = run_features(n_tp, n_z, dt, place, units, far_resid, sources)
         parts += [to_z(found[dz], dz, n_tp - dt) for dz in range(n_z)]
     return mix(n_tp, n_z, place, parts).reshape(2, tokens, quarter)
 

time: 136 us -> 132 us (0.971)
  waiting for transfers between devices: 60.8 us -> 54.3 us
  local copies, waits for them, and re-layouts: 11.6 us -> 16.7 us
  Pallas kernels: 26.7 us -> 24.8 us
    ppermute x16, waiting for transfers between devices: 52 us -> 45.8 us  [send(): return lax.ppermute(array, ('ep', 'tp'), pairs)]
    unnamed x51 -> x41, local copies, waits for them, and re-layouts: 4.6 us -> 9.63 us
    pallas_call x1, Pallas kernels: 11.7 us -> 8.35 us  [run_units(): pl.pallas_call(functools.partial(units_kernel, n_tp, n_z, n_rep), out_sha...]
    pallas_call x0 -> x2, Pallas kernels: none -> 2.9 us  [hold(): pl.pallas_call(functools.partial(hold_kernel, len(arrays)), out_shape=[pl...]
    pallas_call x1, Pallas kernels: 5.18 us -> 3.25 us  [run_features(): pl.pallas_call(functools.partial(features_kernel, n_tp, n_z, dt), out_sha...]
    dynamic_slice x2 -> x3, local copies, waits for them, and re-layouts: 5.33 us -> 5.95 us  [block_of(): lax.dynamic_slice(array, (0, first, first_row, 0), (array.shape[0], last...]
  transfers between devices with their start and end apart: 26 -> 26, of which waited for: 12 -> 13; matrix products, arithmetic and copies ran while one was open for 7% -> 6% of each run, Pallas kernels for 18% -> 17%
where the time goes in v3:
time: 132 us
  waiting for transfers between devices  54.3 us (41%)
  starting transfers between devices  34.3 us (26%)
  Pallas kernels  24.8 us (19%)
  local copies, waits for them, and re-layouts  16.7 us (13%)
    ppermute x16, waiting for transfers between devices, send(): return lax.ppermute(array, ('ep', 'tp'), pairs)  45.8 us
    ppermute x16, starting transfers between devices, send(): return lax.ppermute(array, ('ep', 'tp'), pairs)  27 us
    unnamed x41, local copies, waits for them, and re-layouts  9.63 us
    pallas_call x1, Pallas kernels, run_units(): pl.pallas_call(functools.partial(units_kernel, n_tp, n_z, n_rep), out_sha...  8.35 us
    ppermute x2, waiting for transfers between devices, to_tp(): lax.ppermute(array, 'tp', [(i, (i + shift) % n_tp) for i in range(n_tp)])  6.25 us
    dynamic_slice x3, local copies, waits for them, and re-layouts, block_of(): lax.dynamic_slice(array, (0, first, first_row, 0), (array.shape[0], last...  5.95 us
    ppermute x2, starting transfers between devices, to_tp(): lax.ppermute(array, 'tp', [(i, (i + shift) % n_tp) for i in range(n_tp)])  4.23 us
    pallas_call x1, Pallas kernels, attend(): pl.pallas_call(functools.partial(attention_kernel, cache.shape[3] // HEAD...  3.99 us
  transfers between devices with their start and end apart: 26, of which 13 were waited for; matrix products, arithmetic and copies ran while one was open for 6% of the time, Pallas kernels for 17%

profile of v3, /device:TPU:0, one launch (start us, length us, event | category | flops | bytes accessed | tf_op | source)
XLA Modules:
  0.0 131.5 jit_solution(2318551234729758515)
XLA Ops:
  1.4 3.0 %collective-permute-start.3 = (bf16[64,1024]{1,0:T(8,128)(2,1)S(1)}, bf16[64,1024]{1,0:T(8,128)(2,1)S(1)}, u32[]{:S(2)}, u32[]{:S(2)}) collective-permute-start(bf16[64,1024]{1,0:T(8,128)(2,1)S(1)} %constant_dynamic-slice_fusion.2), channel_id=1, source_target_pairs={{0,1},{1,0},{2,3},{3,2},{4,5},{5,4},{6,7},{7,6},{8,9},{9,8},{10,11... | collective-permute-start | bytes 393224 | tf_op jit(solution)/shard_map/ppermute | solution.py:540
  4.4 2.8 %constant_dynamic-slice_fusion.1 = bf16[2,2,512,384]{3,2,1,0:T(8,128)(2,1)} fusion(bf16[2,3,1024,384]{3,2,1,0:T(8,128)(2,1)} %refs_0_, s32[]{:T(128)S(6)} %select_n.61), kind=kLoop, calls=%fused_computation.10 | loop fusion | bytes 3145732 | tf_op jit(solution)/shard_map/dynamic_slice | solution.py:559
  9.2 1.6 %collective-permute-start = (bf16[2048,256]{1,0:T(8,128)(2,1)}, bf16[2048,256]{1,0:T(8,128)(2,1)}, u32[]{:S(2)}, u32[]{:S(2)}) collective-permute-start(bf16[2048,256]{1,0:T(8,128)(2,1)} %refs_2_), channel_id=1, source_target_pairs={{0,4},{1,5},{2,6},{3,7},{4,0},{5,1},{6,2},{7,3},{8,12},{9,13},{10,... | collective-permute-start | bytes 3145736 | tf_op jit(solution)/shard_map/ppermute | solution.py:534
  13.9 4.0 %attention.1.refs_0_ = bf16[128,2048]{1,0:T(8,128)(2,1)S(1)} custom-call(s32[1]{0:T(128)S(6)} %copy.16.length_ref, bf16[2,64,2048]{2,1,0:T(8,128)(2,1)S(1)} %copy-done.7, bf16[1,2,1024,256]{3,2,1,0:T(8,128)(2,1)S(1)} %copy-done.5, bf16[128,512]{1,0:T(8,128)(2,1)S(1)} %bitcast.21), custom_call_target="tpu_custom_call" | custom-call | flops 1000 | bytes 1000 | tf_op jit(solution)/shard_map/attention/pallas_call | solution.py:114
  17.9 2.6 %collective-permute-start.5 = (bf16[128,2048]{1,0:T(8,128)(2,1)S(1)}, bf16[128,2048]{1,0:T(8,128)(2,1)S(1)}, u32[]{:S(2)}, u32[]{:S(2)}) collective-permute-start(bf16[128,2048]{1,0:T(8,128)(2,1)S(1)} %attention.1.refs_0_), channel_id=1, source_target_pairs={{0,8},{1,9},{2,10},{3,11},{4,12},{5,13},{6,14},{7,15},{8,0},{9,1},... | collective-permute-start | bytes 1572872 | tf_op jit(solution)/shard_map/ppermute | solution.py:534
  20.6 2.3 %copy-done = bf16[2,3,1024,384]{3,2,1,0:T(8,128)(2,1)S(1)} copy-done((bf16[2,3,1024,384]{3,2,1,0:T(8,128)(2,1)S(1)}, bf16[2,3,1024,384]{3,2,1,0:T(8,128)(2,1)}, u32[]{:S(2)}) %copy-start) | copy-done | bytes 4718616
  22.9 2.7 %hold.2 = (bf16[2,3,1024,384]{3,2,1,0:T(8,128)(2,1)S(1)}, bf16[2,3,1024,384]{3,2,1,0:T(8,128)(2,1)S(1)}) custom-call(bf16[2,3,1024,384]{3,2,1,0:T(8,128)(2,1)S(1)} %copy-done, bf16[2,3,1024,384]{3,2,1,0:T(8,128)(2,1)} %collective-permute-done.1.refs_1_), custom_call_target="tpu_custom_call" | custom-call | flops 1000 | bytes 1000 | tf_op jit(solution)/shard_map/hold/pallas_call | solution.py:241
  25.6 2.1 %copy-done.1 = bf16[2,3,1024,384]{3,2,1,0:T(8,128)(2,1)} copy-done((bf16[2,3,1024,384]{3,2,1,0:T(8,128)(2,1)}, bf16[2,3,1024,384]{3,2,1,0:T(8,128)(2,1)S(1)}, u32[]{:S(2)}) %copy-start.1) | copy-done | bytes 4718616
  27.7 2.2 %copy-done.2 = bf16[2,3,1024,384]{3,2,1,0:T(8,128)(2,1)} copy-done((bf16[2,3,1024,384]{3,2,1,0:T(8,128)(2,1)}, bf16[2,3,1024,384]{3,2,1,0:T(8,128)(2,1)S(1)}, u32[]{:S(2)}) %copy-start.2) | copy-done | bytes 4718616
  32.1 1.9 %dynamic_slice.17 = bf16[2,1,640,384]{3,2,1,0:T(8,128)(2,1)S(1)} slice(bf16[2,3,1024,384]{3,2,1,0:T(8,128)(2,1)} %refs_0_), slice={[0:2], [2:3], [0:640], [0:384]} | slice | bytes 1966080 | tf_op jit(solution)/shard_map/dynamic_slice | solution.py:559
  34.6 12.0 %collective-permute-done.refs_4_ = bf16[2048,256]{1,0:T(8,128)(2,1)} collective-permute-done((bf16[2048,256]{1,0:T(8,128)(2,1)}, bf16[2048,256]{1,0:T(8,128)(2,1)}, u32[]{:S(2)}, u32[]{:S(2)}) %collective-permute-start) | collective-permute-done | bytes 1048608 | tf_op jit(solution)/shard_map/ppermute | solution.py:534
  46.7 2.6 %out_projection.1.refs_3_ = f32[256,768]{1,0:T(8,128)S(1)} custom-call(s32[6]{0:T(128)S(1)} %stack.36.place_ref, bf16[128,2048]{1,0:T(8,128)(2,1)S(1)} %attention.1.refs_0_, bf16[128,2048]{1,0:T(8,128)(2,1)S(1)} %collective-permute-done.5.refs_1_, bf16[2048,256]{1,0:T(8,128)(2,1)} %refs_2_, bf16[2048,256]{1,0:T(8,128)(2,1)S(1)} %copy-done.4, ...), custom_call_target="tpu_custom_call" | custom-call | flops 1000 | bytes 1000 | tf_op jit(solution)/shard_map/out_projection/pallas_call | solution.py:144
  50.7 1.5 %collective-permute-start.14 = (bf16[2,2,512,384]{3,2,1,0:T(8,128)(2,1)S(1)}, bf16[2,2,512,384]{3,2,1,0:T(8,128)(2,1)S(1)}, u32[]{:S(2)}, u32[]{:S(2)}) collective-permute-start(bf16[2,2,512,384]{3,2,1,0:T(8,128)(2,1)S(1)} %collective-permute-done.4.refs_1_), channel_id=1, source_target_pairs={{0,16},{16,0},{1,17},{17,1},{2,18},{18,2},{3,19},{19,3},{4,20},{20... | collective-permute-start | bytes 4718600 | tf_op jit(solution)/shard_map/ppermute | solution.py:543
  53.5 2.4 %collective-permute-start.9 = (bf16[64,1152]{1,0:T(8,128)(2,1)S(1)}, bf16[64,1152]{1,0:T(8,128)(2,1)S(1)}, u32[]{:S(2)}, u32[]{:S(2)}) collective-permute-start(bf16[64,1152]{1,0:T(8,128)(2,1)S(1)} %get-tuple-element.80), channel_id=1, source_target_pairs={{0,8},{1,9},{2,10},{3,11},{4,12},{5,13},{6,14},{7,15},{8,0},{9,1},... | collective-permute-start | bytes 442376 | tf_op jit(solution)/shard_map/ppermute | solution.py:534
  55.9 5.4 %collective-permute-done.7.refs_0_.refs_1_ = bf16[144,1024]{1,0:T(8,128)(2,1)S(1)} collective-permute-done((bf16[144,1024]{1,0:T(8,128)(2,1)S(1)}, bf16[144,1024]{1,0:T(8,128)(2,1)S(1)}, u32[]{:S(2)}, u32[]{:S(2)}) %collective-permute-start.7) | collective-permute-done | bytes 294944 | tf_op jit(solution)/shard_map/ppermute | solution.py:540
  61.2 1.8 %collective-permute-done.9.refs_2_ = bf16[64,1152]{1,0:T(8,128)(2,1)S(1)} collective-permute-done((bf16[64,1152]{1,0:T(8,128)(2,1)S(1)}, bf16[64,1152]{1,0:T(8,128)(2,1)S(1)}, u32[]{:S(2)}, u32[]{:S(2)}) %collective-permute-start.9) | collective-permute-done | bytes 147488 | tf_op jit(solution)/shard_map/ppermute | solution.py:534
  64.6 3.4 %collective-permute-start.11 = (bf16[128,1024]{1,0:T(8,128)(2,1)S(1)}, bf16[128,1024]{1,0:T(8,128)(2,1)S(1)}, u32[]{:S(2)}, u32[]{:S(2)}) collective-permute-start(bf16[128,1024]{1,0:T(8,128)(2,1)S(1)} %get-tuple-element.82), channel_id=1, source_target_pairs={{0,8},{1,9},{2,10},{3,11},{4,12},{5,13},{6,14},{7,15},{8,0},{9,1},... | collective-permute-start | bytes 786440 | tf_op jit(solution)/shard_map/ppermute | solution.py:534
  68.2 9.3 %collective-permute-done.11.refs_4_ = bf16[128,1024]{1,0:T(8,128)(2,1)S(1)} collective-permute-done((bf16[128,1024]{1,0:T(8,128)(2,1)S(1)}, bf16[128,1024]{1,0:T(8,128)(2,1)S(1)}, u32[]{:S(2)}, u32[]{:S(2)}) %collective-permute-start.11) | collective-permute-done | bytes 262176 | tf_op jit(solution)/shard_map/ppermute | solution.py:534
  77.5 1.7 %collective-permute-done.10.refs_3_ = bf16[128,1152]{1,0:T(8,128)(2,1)S(1)} collective-permute-done((bf16[128,1152]{1,0:T(8,128)(2,1)S(1)}, bf16[128,1152]{1,0:T(8,128)(2,1)S(1)}, u32[]{:S(2)}, u32[]{:S(2)}) %collective-permute-start.10) | collective-permute-done | bytes 294944 | tf_op jit(solution)/shard_map/ppermute | solution.py:534
  79.2 2.1 %collective-permute-start.12 = (bf16[128,1024]{1,0:T(8,128)(2,1)S(1)}, bf16[128,1024]{1,0:T(8,128)(2,1)S(1)}, u32[]{:S(2)}, u32[]{:S(2)}) collective-permute-start(bf16[128,1024]{1,0:T(8,128)(2,1)S(1)} %collective-permute-done.11.refs_4_), channel_id=1, source_target_pairs={{0,4},{1,5},{2,6},{3,7},{4,0},{5,1},{6,2},{7,3},{8,12},{9,13},{10,... | collective-permute-start | bytes 786440 | tf_op jit(solution)/shard_map/ppermute | solution.py:534
  81.3 6.4 %collective-permute-done.12.refs_5_ = bf16[128,1024]{1,0:T(8,128)(2,1)S(1)} collective-permute-done((bf16[128,1024]{1,0:T(8,128)(2,1)S(1)}, bf16[128,1024]{1,0:T(8,128)(2,1)S(1)}, u32[]{:S(2)}, u32[]{:S(2)}) %collective-permute-start.12) | collective-permute-done | bytes 262176 | tf_op jit(solution)/shard_map/ppermute | solution.py:534
  89.0 2.1 %collective-permute-done.15.refs_10_ = bf16[2,2,512,384]{3,2,1,0:T(8,128)(2,1)S(1)} collective-permute-done((bf16[2,2,512,384]{3,2,1,0:T(8,128)(2,1)S(1)}, bf16[2,2,512,384]{3,2,1,0:T(8,128)(2,1)S(1)}, u32[]{:S(2)}, u32[]{:S(2)}) %collective-permute-start.15) | collective-permute-done | bytes 1572896 | tf_op jit(solution)/shard_map/ppermute | solution.py:537
  91.1 8.3 %units.1 = (bf16[256,1536]{1,0:T(8,128)(2,1)S(1)}, bf16[1,64,1024]{2,1,0:T(8,128)(2,1)S(1)}, f32[64,1024]{1,0:T(8,128)S(1)}, bf16[64,1024]{1,0:T(8,128)(2,1)S(1)...) custom-call(s32[6]{0:T(128)S(1)} %stack.36.place_ref, s32[1,16]{1,0:T(1,128)S(1)} %constant_dynamic-slice_fusion.table_ref, ...), custom_call_target="tpu_custom_call" | custom-call | flops 1000 | bytes 1000 | tf_op jit(solution)/shard_map/units/pallas_call | solution.py:399
  99.5 3.3 %collective-permute-done.19.refs_3_ = bf16[2,1,384,384]{3,2,1,0:T(8,128)(2,1)S(1)} collective-permute-done((bf16[2,1,384,384]{3,2,1,0:T(8,128)(2,1)S(1)}, bf16[2,1,384,384]{3,2,1,0:T(8,128)(2,1)S(1)}, u32[]{:S(2)}, u32[]{:S(2)}) %collective-permute-start.19) | collective-permute-done | bytes 589856 | tf_op jit(solution)/shard_map/ppermute | solution.py:534
  103.3 2.0 %collective-permute-start.16 = (bf16[64,1024]{1,0:T(8,128)(2,1)S(1)}, bf16[64,1024]{1,0:T(8,128)(2,1)S(1)}, u32[]{:S(2)}, u32[]{:S(2)}) collective-permute-start(bf16[64,1024]{1,0:T(8,128)(2,1)S(1)} %get-tuple-element.98), channel_id=1, source_target_pairs={{0,4},{1,5},{2,6},{3,7},{4,0},{5,1},{6,2},{7,3},{8,12},{9,13},{10,... | collective-permute-start | bytes 393224 | tf_op jit(solution)/shard_map/ppermute | solution.py:534
  105.3 2.0 %collective-permute-start.17 = (bf16[64,1024]{1,0:T(8,128)(2,1)S(1)}, bf16[64,1024]{1,0:T(8,128)(2,1)S(1)}, u32[]{:S(2)}, u32[]{:S(2)}) collective-permute-start(bf16[64,1024]{1,0:T(8,128)(2,1)S(1)} %get-tuple-element.99), channel_id=1, source_target_pairs={{0,8},{1,9},{2,10},{3,11},{4,12},{5,13},{6,14},{7,15},{8,0},{9,1},... | collective-permute-start | bytes 393224 | tf_op jit(solution)/shard_map/ppermute | solution.py:534
  107.7 3.2 %features.1 = (bf16[64,1024]{1,0:T(8,128)(2,1)S(1)}, bf16[64,1024]{1,0:T(8,128)(2,1)S(1)}, bf16[64,1024]{1,0:T(8,128)(2,1)S(1)}, bf16[64,1024]{1,0:T(8,128)(2,1)S(1)}) custom-call(s32[6]{0:T(128)S(1)} %stack.36.place_ref, bf16[256,1536]{1,0:T(8,128)(2,1)S(1)} %get-tuple-element.101.hidden_ref, bf16[1,64,1024]{2,1,0:T(8,128)(2,1)S(1)} %get-tuple-element.102.resid_ref, ...), custom_call_target="tpu_custom_call" | custom-call | flops 1000 | bytes 1000 | tf_op jit(solution)/shard_map/features/pallas_call | solution.py:428
  113.6 3.3 %collective-permute-start.24 = (bf16[64,1024]{1,0:T(8,128)(2,1)S(1)}, bf16[64,1024]{1,0:T(8,128)(2,1)S(1)}, u32[]{:S(2)}, u32[]{:S(2)}) collective-permute-start(bf16[64,1024]{1,0:T(8,128)(2,1)S(1)} %get-tuple-element.109), channel_id=1, source_target_pairs={{0,9},{1,8},{2,11},{3,10},{4,13},{5,12},{6,15},{7,14},{8,1},{9,0},... | collective-permute-start | bytes 393224 | tf_op jit(solution)/shard_map/ppermute | solution.py:534
  116.9 1.4 %collective-permute-done.17.refs_2_ = bf16[64,1024]{1,0:T(8,128)(2,1)S(1)} collective-permute-done((bf16[64,1024]{1,0:T(8,128)(2,1)S(1)}, bf16[64,1024]{1,0:T(8,128)(2,1)S(1)}, u32[]{:S(2)}, u32[]{:S(2)}) %collective-permute-start.17) | collective-permute-done | bytes 131104 | tf_op jit(solution)/shard_map/ppermute | solution.py:534
  118.3 2.0 %collective-permute-start.25 = (bf16[64,1024]{1,0:T(8,128)(2,1)S(1)}, bf16[64,1024]{1,0:T(8,128)(2,1)S(1)}, u32[]{:S(2)}, u32[]{:S(2)}) collective-permute-start(bf16[64,1024]{1,0:T(8,128)(2,1)S(1)} %get-tuple-element.110), channel_id=1, source_target_pairs={{0,13},{1,12},{2,15},{3,14},{4,9},{5,8},{6,11},{7,10},{8,5},{9,4},... | collective-permute-start | bytes 393224 | tf_op jit(solution)/shard_map/ppermute | solution.py:534
  121.0 9.2 %collective-permute-done.24.refs_6_ = bf16[64,1024]{1,0:T(8,128)(2,1)S(1)} collective-permute-done((bf16[64,1024]{1,0:T(8,128)(2,1)S(1)}, bf16[64,1024]{1,0:T(8,128)(2,1)S(1)}, u32[]{:S(2)}, u32[]{:S(2)}) %collective-permute-start.24) | collective-permute-done | bytes 131104 | tf_op jit(solution)/shard_map/ppermute | solution.py:534
  130.2 1.4 %mix.1 = bf16[128,1024]{1,0:T(8,128)(2,1)} custom-call(s32[6]{0:T(128)S(1)} %stack.36.place_ref, f32[64,1024]{1,0:T(8,128)S(1)} %get-tuple-element.97.refs_0_, bf16[64,1024]{1,0:T(8,128)(2,1)S(1)} %collective-permute-done.16.refs_1_, bf16[64,1024]{1,0:T(8,128)(2,1)S(1)} %collective-permute-done.17.refs_2_, ...), custom_call_target="tpu_custom_call" | custom-call | flops 1000 | bytes 1000 | tf_op jit(solution)/shard_map/mix/pallas_call | solution.py:491
  (86 shorter events, 18.7 us)
Async XLA Ops:
  0.0 20.6 %collective-permute-start.1 = (bf16[2,3,1024,384]{3,2,1,0:T(8,128)(2,1)}, bf16[2,3,1024,384]{3,2,1,0:T(8,128)(2,1)}, u32[]{:S(2)}, u32[]{:S(2)}) collective-permute-start(bf16[2,3,1024,384]{3,2,1,0:T(8,128)(2,1)} %refs_0_), channel_id=1, source_target_pairs={{0,2},{2,0},{4,6},{6,4},{8,10},{10,8},{12,14},{14,12},{1,3},{3,1},... | collective-permute-start | bytes 14155784 | tf_op jit(solution)/shard_map/ppermute | solution.py:537
  0.5 11.2 %collective-permute-start.2 = (bf16[2048,256]{1,0:T(8,128)(2,1)}, bf16[2048,256]{1,0:T(8,128)(2,1)S(1)}, u32[]{:S(2)}, u32[]{:S(2)}) collective-permute-start(bf16[2048,256]{1,0:T(8,128)(2,1)} %refs_2_), channel_id=1, source_target_pairs={{0,2},{2,0},{4,6},{6,4},{8,10},{10,8},{12,14},{14,12},{1,3},{3,1},... | collective-permute-start | bytes 3145736 | tf_op jit(solution)/shard_map/ppermute | solution.py:537
  1.4 6.7 %collective-permute-start.3 = (bf16[64,1024]{1,0:T(8,128)(2,1)S(1)}, bf16[64,1024]{1,0:T(8,128)(2,1)S(1)}, u32[]{:S(2)}, u32[]{:S(2)}) collective-permute-start(bf16[64,1024]{1,0:T(8,128)(2,1)S(1)} %constant_dynamic-slice_fusion.2), channel_id=1, source_target_pairs={{0,1},{1,0},{2,3},{3,2},{4,5},{5,4},{6,7},{7,6},{8,9},{9,8},{10,11... | collective-permute-start | bytes 393224 | tf_op jit(solution)/shard_map/ppermute | solution.py:540
  8.8 37.8 %collective-permute-start.4 = (bf16[2,2,512,384]{3,2,1,0:T(8,128)(2,1)}, bf16[2,2,512,384]{3,2,1,0:T(8,128)(2,1)S(1)}, u32[]{:S(2)}, u32[]{:S(2)}) collective-permute-start(bf16[2,2,512,384]{3,2,1,0:T(8,128)(2,1)} %constant_dynamic-slice_fusion.1), channel_id=1, source_target_pairs={{0,3},{1,2},{2,1},{3,0},{4,7},{5,6},{6,5},{7,4},{8,11},{9,10},{10,... | collective-permute-start | bytes 4718600 | tf_op jit(solution)/shard_map/ppermute | solution.py:534
  9.2 37.3 %collective-permute-start = (bf16[2048,256]{1,0:T(8,128)(2,1)}, bf16[2048,256]{1,0:T(8,128)(2,1)}, u32[]{:S(2)}, u32[]{:S(2)}) collective-permute-start(bf16[2048,256]{1,0:T(8,128)(2,1)} %refs_2_), channel_id=1, source_target_pairs={{0,4},{1,5},{2,6},{3,7},{4,0},{5,1},{6,2},{7,3},{8,12},{9,13},{10,... | collective-permute-start | bytes 3145736 | tf_op jit(solution)/shard_map/ppermute | solution.py:534
  17.9 28.6 %collective-permute-start.5 = (bf16[128,2048]{1,0:T(8,128)(2,1)S(1)}, bf16[128,2048]{1,0:T(8,128)(2,1)S(1)}, u32[]{:S(2)}, u32[]{:S(2)}) collective-permute-start(bf16[128,2048]{1,0:T(8,128)(2,1)S(1)} %attention.1.refs_0_), channel_id=1, source_target_pairs={{0,8},{1,9},{2,10},{3,11},{4,12},{5,13},{6,14},{7,15},{8,0},{9,1},... | collective-permute-start | bytes 1572872 | tf_op jit(solution)/shard_map/ppermute | solution.py:534
  30.0 16.7 %copy-start.4 = (bf16[2048,256]{1,0:T(8,128)(2,1)S(1)}, bf16[2048,256]{1,0:T(8,128)(2,1)}, u32[]{:S(2)}) copy-start(bf16[2048,256]{1,0:T(8,128)(2,1)} %copy-done.3) | copy-start | bytes 3145732
  30.0 19.5 %copy-start.8 = (bf16[1024,16]{0,1:T(8,128)(2,1)S(1)}, bf16[1024,16]{0,1:T(8,128)(2,1)}, u32[]{:S(2)}) copy-start(bf16[1024,16]{0,1:T(8,128)(2,1)} %param.18) | copy-start | bytes 98308
  30.7 60.3 %slice-start = ((s8[4718592]{0:T(1024)(128)(4,1)}), s8[4194304]{0:T(1024)(128)(4,1)S(1)}, s32[]{:S(2)}) async-start(s8[4718592]{0:T(1024)(128)(4,1)} %bitcast.15), calls=%async_computation | async-start | bytes 8388608
  30.8 60.3 %slice-start.2 = ((s8[4718592]{0:T(1024)(128)(4,1)}), s8[4194304]{0:T(1024)(128)(4,1)S(1)}, s32[]{:S(2)}) async-start(s8[4718592]{0:T(1024)(128)(4,1)} %bitcast.17), calls=%async_computation.2 | async-start | bytes 8388608
  46.5 44.6 %slice-start.1 = ((s8[4718592]{0:T(1024)(128)(4,1)}), s8[524288]{0:T(1024)(128)(4,1)S(1)}, s32[]{:S(2)}) async-start(s8[4718592]{0:T(1024)(128)(4,1)} %bitcast.15), calls=%async_computation.1 | async-start | bytes 1048576
  46.5 44.6 %slice-start.3 = ((s8[4718592]{0:T(1024)(128)(4,1)}), s8[524288]{0:T(1024)(128)(4,1)S(1)}, s32[]{:S(2)}) async-start(s8[4718592]{0:T(1024)(128)(4,1)} %bitcast.17), calls=%async_computation.3 | async-start | bytes 1048576
  46.5 2.9 %collective-permute-start.6 = (bf16[2048,256]{1,0:T(8,128)(2,1)}, bf16[2048,256]{1,0:T(8,128)(2,1)S(1)}, u32[]{:S(2)}, u32[]{:S(2)}) collective-permute-start(bf16[2048,256]{1,0:T(8,128)(2,1)} %collective-permute-done.refs_4_), channel_id=1, source_target_pairs={{0,2},{2,0},{4,6},{6,4},{8,10},{10,8},{12,14},{14,12},{1,3},{3,1},... | collective-permute-start | bytes 3145736 | tf_op jit(solution)/shard_map/ppermute | solution.py:537
  50.5 10.7 %collective-permute-start.8 = (bf16[2,2,512,384]{3,2,1,0:T(8,128)(2,1)S(1)}, bf16[2,2,512,384]{3,2,1,0:T(8,128)(2,1)S(1)}, u32[]{:S(2)}, u32[]{:S(2)}) collective-permute-start(bf16[2,2,512,384]{3,2,1,0:T(8,128)(2,1)S(1)} %collective-permute-done.4.refs_1_), channel_id=1, source_target_pairs={{0,2},{2,0},{4,6},{6,4},{8,10},{10,8},{12,14},{14,12},{1,3},{3,1},... | collective-permute-start | bytes 4718600 | tf_op jit(solution)/shard_map/ppermute | solution.py:537
  50.7 36.9 %collective-permute-start.14 = (bf16[2,2,512,384]{3,2,1,0:T(8,128)(2,1)S(1)}, bf16[2,2,512,384]{3,2,1,0:T(8,128)(2,1)S(1)}, u32[]{:S(2)}, u32[]{:S(2)}) collective-permute-start(bf16[2,2,512,384]{3,2,1,0:T(8,128)(2,1)S(1)} %collective-permute-done.4.refs_1_), channel_id=1, source_target_pairs={{0,16},{16,0},{1,17},{17,1},{2,18},{18,2},{3,19},{19,3},{4,20},{20... | collective-permute-start | bytes 4718600 | tf_op jit(solution)/shard_map/ppermute | solution.py:543
  52.3 8.9 %collective-permute-start.7 = (bf16[144,1024]{1,0:T(8,128)(2,1)S(1)}, bf16[144,1024]{1,0:T(8,128)(2,1)S(1)}, u32[]{:S(2)}, u32[]{:S(2)}) collective-permute-start(bf16[144,1024]{1,0:T(8,128)(2,1)S(1)} %get-tuple-element.74), channel_id=1, source_target_pairs={{0,1},{1,0},{2,3},{3,2},{4,5},{5,4},{6,7},{7,6},{8,9},{9,8},{10,11... | collective-permute-start | bytes 884744 | tf_op jit(solution)/shard_map/ppermute | solution.py:540
  53.5 9.6 %collective-permute-start.9 = (bf16[64,1152]{1,0:T(8,128)(2,1)S(1)}, bf16[64,1152]{1,0:T(8,128)(2,1)S(1)}, u32[]{:S(2)}, u32[]{:S(2)}) collective-permute-start(bf16[64,1152]{1,0:T(8,128)(2,1)S(1)} %get-tuple-element.80), channel_id=1, source_target_pairs={{0,8},{1,9},{2,10},{3,11},{4,12},{5,13},{6,14},{7,15},{8,0},{9,1},... | collective-permute-start | bytes 442376 | tf_op jit(solution)/shard_map/ppermute | solution.py:534
  63.7 24.0 %collective-permute-start.13 = (bf16[2,1,640,384]{3,2,1,0:T(8,128)(2,1)S(1)}, bf16[2,1,640,384]{3,2,1,0:T(8,128)(2,1)S(1)}, u32[]{:S(2)}, u32[]{:S(2)}) collective-permute-start(bf16[2,1,640,384]{3,2,1,0:T(8,128)(2,1)S(1)} %dynamic_slice.17), channel_id=1, source_target_pairs={{0,3},{1,2},{2,1},{3,0},{4,7},{5,6},{6,5},{7,4},{8,11},{9,10},{10,... | collective-permute-start | bytes 2949128 | tf_op jit(solution)/shard_map/ppermute | solution.py:534
  63.8 15.4 %collective-permute-start.10 = (bf16[128,1152]{1,0:T(8,128)(2,1)S(1)}, bf16[128,1152]{1,0:T(8,128)(2,1)S(1)}, u32[]{:S(2)}, u32[]{:S(2)}) collective-permute-start(bf16[128,1152]{1,0:T(8,128)(2,1)S(1)} %get-tuple-element.92.refs_2_), channel_id=1, source_target_pairs={{0,4},{1,5},{2,6},{3,7},{4,0},{5,1},{6,2},{7,3},{8,12},{9,13},{10,... | collective-permute-start | bytes 884744 | tf_op jit(solution)/shard_map/ppermute | solution.py:534
  64.6 12.9 %collective-permute-start.11 = (bf16[128,1024]{1,0:T(8,128)(2,1)S(1)}, bf16[128,1024]{1,0:T(8,128)(2,1)S(1)}, u32[]{:S(2)}, u32[]{:S(2)}) collective-permute-start(bf16[128,1024]{1,0:T(8,128)(2,1)S(1)} %get-tuple-element.82), channel_id=1, source_target_pairs={{0,8},{1,9},{2,10},{3,11},{4,12},{5,13},{6,14},{7,15},{8,0},{9,1},... | collective-permute-start | bytes 786440 | tf_op jit(solution)/shard_map/ppermute | solution.py:534
  79.2 8.5 %collective-permute-start.12 = (bf16[128,1024]{1,0:T(8,128)(2,1)S(1)}, bf16[128,1024]{1,0:T(8,128)(2,1)S(1)}, u32[]{:S(2)}, u32[]{:S(2)}) collective-permute-start(bf16[128,1024]{1,0:T(8,128)(2,1)S(1)} %collective-permute-done.11.refs_4_), channel_id=1, source_target_pairs={{0,4},{1,5},{2,6},{3,7},{4,0},{5,1},{6,2},{7,3},{8,12},{9,13},{10,... | collective-permute-start | bytes 786440 | tf_op jit(solution)/shard_map/ppermute | solution.py:534
  87.7 3.4 %collective-permute-start.15 = (bf16[2,2,512,384]{3,2,1,0:T(8,128)(2,1)S(1)}, bf16[2,2,512,384]{3,2,1,0:T(8,128)(2,1)S(1)}, u32[]{:S(2)}, u32[]{:S(2)}) collective-permute-start(bf16[2,2,512,384]{3,2,1,0:T(8,128)(2,1)S(1)} %collective-permute-done.14.refs_11_), channel_id=1, source_target_pairs={{0,2},{2,0},{4,6},{6,4},{8,10},{10,8},{12,14},{14,12},{1,3},{3,1},... | collective-permute-start | bytes 4718600 | tf_op jit(solution)/shard_map/ppermute | solution.py:537
  87.7 15.1 %collective-permute-start.19 = (bf16[2,1,384,384]{3,2,1,0:T(8,128)(2,1)S(1)}, bf16[2,1,384,384]{3,2,1,0:T(8,128)(2,1)S(1)}, u32[]{:S(2)}, u32[]{:S(2)}) collective-permute-start(bf16[2,1,384,384]{3,2,1,0:T(8,128)(2,1)S(1)} %dynamic_slice.18), channel_id=1, source_target_pairs={{0,3},{1,2},{2,1},{3,0},{4,7},{5,6},{6,5},{7,4},{8,11},{9,10},{10,... | collective-permute-start | bytes 1769480 | tf_op jit(solution)/shard_map/ppermute | solution.py:534
  102.8 4.9 %collective-permute-start.20 = (bf16[2,1,640,384]{3,2,1,0:T(8,128)(2,1)S(1)}, bf16[2,1,640,384]{3,2,1,0:T(8,128)(2,1)S(1)}, u32[]{:S(2)}, u32[]{:S(2)}) collective-permute-start(bf16[2,1,640,384]{3,2,1,0:T(8,128)(2,1)S(1)} %collective-permute-done.13.refs_1_), channel_id=1, source_target_pairs={{0,2},{2,0},{4,6},{6,4},{8,10},{10,8},{12,14},{14,12},{1,3},{3,1},... | collective-permute-start | bytes 2949128 | tf_op jit(solution)/shard_map/ppermute | solution.py:537
  103.2 4.5 %collective-permute-start.21 = (bf16[2,1,384,384]{3,2,1,0:T(8,128)(2,1)S(1)}, bf16[2,1,384,384]{3,2,1,0:T(8,128)(2,1)S(1)}, u32[]{:S(2)}, u32[]{:S(2)}) collective-permute-start(bf16[2,1,384,384]{3,2,1,0:T(8,128)(2,1)S(1)} %collective-permute-done.19.refs_3_), channel_id=1, source_target_pairs={{0,2},{2,0},{4,6},{6,4},{8,10},{10,8},{12,14},{14,12},{1,3},{3,1},... | collective-permute-start | bytes 1769480 | tf_op jit(solution)/shard_map/ppermute | solution.py:537
  103.3 10.3 %collective-permute-start.16 = (bf16[64,1024]{1,0:T(8,128)(2,1)S(1)}, bf16[64,1024]{1,0:T(8,128)(2,1)S(1)}, u32[]{:S(2)}, u32[]{:S(2)}) collective-permute-start(bf16[64,1024]{1,0:T(8,128)(2,1)S(1)} %get-tuple-element.98), channel_id=1, source_target_pairs={{0,4},{1,5},{2,6},{3,7},{4,0},{5,1},{6,2},{7,3},{8,12},{9,13},{10,... | collective-permute-start | bytes 393224 | tf_op jit(solution)/shard_map/ppermute | solution.py:534
  105.3 12.9 %collective-permute-start.17 = (bf16[64,1024]{1,0:T(8,128)(2,1)S(1)}, bf16[64,1024]{1,0:T(8,128)(2,1)S(1)}, u32[]{:S(2)}, u32[]{:S(2)}) collective-permute-start(bf16[64,1024]{1,0:T(8,128)(2,1)S(1)} %get-tuple-element.99), channel_id=1, source_target_pairs={{0,8},{1,9},{2,10},{3,11},{4,12},{5,13},{6,14},{7,15},{8,0},{9,1},... | collective-permute-start | bytes 393224 | tf_op jit(solution)/shard_map/ppermute | solution.py:534
  107.3 12.9 %collective-permute-start.18 = (bf16[64,1024]{1,0:T(8,128)(2,1)S(1)}, bf16[64,1024]{1,0:T(8,128)(2,1)S(1)}, u32[]{:S(2)}, u32[]{:S(2)}) collective-permute-start(bf16[64,1024]{1,0:T(8,128)(2,1)S(1)} %get-tuple-element.100), channel_id=1, source_target_pairs={{0,12},{1,13},{2,14},{3,15},{4,8},{5,9},{6,10},{7,11},{8,4},{9,5},... | collective-permute-start | bytes 393224 | tf_op jit(solution)/shard_map/ppermute | solution.py:534
  111.0 9.2 %collective-permute-start.22 = (bf16[64,1024]{1,0:T(8,128)(2,1)S(1)}, bf16[64,1024]{1,0:T(8,128)(2,1)S(1)}, u32[]{:S(2)}, u32[]{:S(2)}) collective-permute-start(bf16[64,1024]{1,0:T(8,128)(2,1)S(1)} %get-tuple-element.107), channel_id=1, source_target_pairs={{0,1},{1,0},{2,3},{3,2},{4,5},{5,4},{6,7},{7,6},{8,9},{9,8},{10,11... | collective-permute-start | bytes 393224 | tf_op jit(solution)/shard_map/ppermute | solution.py:534
  112.3 8.7 %collective-permute-start.23 = (bf16[64,1024]{1,0:T(8,128)(2,1)S(1)}, bf16[64,1024]{1,0:T(8,128)(2,1)S(1)}, u32[]{:S(2)}, u32[]{:S(2)}) collective-permute-start(bf16[64,1024]{1,0:T(8,128)(2,1)S(1)} %get-tuple-element.108), channel_id=1, source_target_pairs={{0,5},{1,4},{2,7},{3,6},{4,1},{5,0},{6,3},{7,2},{8,13},{9,12},{10,... | collective-permute-start | bytes 393224 | tf_op jit(solution)/shard_map/ppermute | solution.py:534
  113.6 16.6 %collective-permute-start.24 = (bf16[64,1024]{1,0:T(8,128)(2,1)S(1)}, bf16[64,1024]{1,0:T(8,128)(2,1)S(1)}, u32[]{:S(2)}, u32[]{:S(2)}) collective-permute-start(bf16[64,1024]{1,0:T(8,128)(2,1)S(1)} %get-tuple-element.109), channel_id=1, source_target_pairs={{0,9},{1,8},{2,11},{3,10},{4,13},{5,12},{6,15},{7,14},{8,1},{9,0},... | collective-permute-start | bytes 393224 | tf_op jit(solution)/shard_map/ppermute | solution.py:534
  118.3 11.9 %collective-permute-start.25 = (bf16[64,1024]{1,0:T(8,128)(2,1)S(1)}, bf16[64,1024]{1,0:T(8,128)(2,1)S(1)}, u32[]{:S(2)}, u32[]{:S(2)}) collective-permute-start(bf16[64,1024]{1,0:T(8,128)(2,1)S(1)} %get-tuple-element.110), channel_id=1, source_target_pairs={{0,13},{1,12},{2,15},{3,14},{4,9},{5,8},{6,11},{7,10},{8,5},{9,4},... | collective-permute-start | bytes 393224 | tf_op jit(solution)/shard_map/ppermute | solution.py:534
  (14 other events, 75.9 us)

commit v4 on v3

--- a/solution.py
+++ b/solution.py
@@ -227,27 +227,46 @@
 
 
 def hold_kernel(count, *refs):
-    sems = refs[-1]
+    token_ref, sems = refs[-2:]
     copies = [
         pltpu.make_async_copy(refs[n], refs[count + n], sems.at[n]) for n in range(count)
     ]
     for copy in copies:
         copy.start()
+    token_ref[...] = jnp.zeros_like(token_ref)
     for copy in copies:
         copy.wait()
 
 
 def hold(arrays):
-    return pl.pallas_call(
+    found = pl.pallas_call(
         functools.partial(hold_kernel, len(arrays)),
-        out_shape=[pltpu.VMEM(array.shape, array.dtype) for array in arrays],
+        out_shape=[pltpu.VMEM(array.shape, array.dtype) for array in arrays]
+        + [jax.ShapeDtypeStruct((8, LANES), F32)],
         in_specs=[unplaced()] * len(arrays),
-        out_specs=[whole()] * len(arrays),
+        out_specs=[whole()] * (len(arrays) + 1),
         scratch_shapes=[pltpu.SemaphoreType.DMA((len(arrays),))],
         compiler_params=params(2),
         cost_estimate=COST,
         name="hold",
     )(*arrays)
+    return found[:-1], found[-1]
+
+
+def touch_kernel(array_ref, token_ref):
+    token_ref[...] = jnp.zeros_like(token_ref)
+
+
+def touch(array):
+    return pl.pallas_call(
+        touch_kernel,
+        out_shape=jax.ShapeDtypeStruct((8, LANES), F32),
+        in_specs=[pl.BlockSpec(memory_space=pl.ANY)],
+        out_specs=whole(),
+        compiler_params=params(56),
+        cost_estimate=COST,
+        name="touch",
+    )(array)
 
 
 def units_kernel(n_tp, n_z, n_rep, place_ref, table_ref, *refs):
@@ -474,22 +493,24 @@
     )(place, hidden, ids, *swapped)
 
 
-def mix_kernel(n_tp, n_z, place_ref, *refs):
+def mix_kernel(n_tp, owners, place_ref, *refs):
     t = place_ref[0]
     parts, out_ref = refs[:-1], refs[-1]
     chunk = parts[0].shape[0]
     for dt in range(n_tp):
-        value = parts[dt * n_z][...].astype(F32)
-        for dz in range(1, n_z):
-            value = value + parts[dt * n_z + dz][...].astype(F32)
+        value = None
+        for owner, part in zip(owners, parts):
+            if owner == dt:
+                term = part[...].astype(F32)
+                value = term if value is None else value + term
         row = pl.multiple_of(lax.rem(t + dt, n_tp) * chunk, chunk)
         out_ref[pl.ds(row, chunk), :] = value.astype(BF16)
 
 
-def mix(n_tp, n_z, place, parts):
+def mix(n_tp, owners, place, parts):
     chunk, span = parts[0].shape
     return pl.pallas_call(
-        functools.partial(mix_kernel, n_tp, n_z),
+        functools.partial(mix_kernel, n_tp, owners),
         out_shape=jax.ShapeDtypeStruct((chunk * n_tp, span), BF16),
         in_specs=[scalars()] + [whole()] * len(parts),
         out_specs=whole(),
@@ -580,14 +601,14 @@
     attention = attend(cache_lengths, queries, cache, fresh)
     pieces = over_z(attention, m, n_z)
     own_other = to_core(expert_weights)
-    own = hold(after([expert_weights, own_other], attention))
+    own_held = touch(after(own_other, attention))
     expert_ids, weights, old_slots, router = after(
-        (expert_ids, expert_weights, old_slots, router_weight), own
+        (expert_ids, expert_weights, old_slots, router_weight), (own_held, near)
     )
     outgoing = messages(
         n_tp, place, flat_hidden, expert_ids.reshape(rows, -1), swapped, experts
     )
-    edge = max(LANES, 5 * quarter // 8 // LANES * LANES)
+    edge = 11 * quarter // 16
     blocks = [
         block_of(weights, (2, 3), first_row, last_row - first_row)
         for first_row, last_row in ((0, edge), (edge, quarter))
@@ -595,11 +616,10 @@
     router = router.T
     tables = slot_tables(old_slots, new_slots, moved_experts)
     table = lax.dynamic_slice_in_dim(tables, t * chunk // tokens, 1, 0)
-    near, table, router, outgoing, blocks, first = after(
-        (near, table, router, outgoing, blocks, first), (pieces[1], own)
+    near, table, router, outgoing, blocks = after(
+        (near, table, router, outgoing, blocks), (pieces[1], own_held)
     )
     hidden = [outgoing[0]] + [to_z(outgoing[dh], dh * m) for dh in range(1, n_tp)]
-    passed = [to_rep(array, 1) for array in first]
     crossed = [out_other] + [to_core(array) for array in near[1:]]
     early = [array for pair in zip(near, crossed) for array in pair]
     last = early.pop()
@@ -612,6 +632,7 @@
     sums = finish(n_tp, place, router, pieces, last, early)
     terms = [to_tp(sums[dt], dt) for dt in range(1, n_tp)]
     first = after(first, sums)
+    passed = [to_rep(array, 1) for array in first]
     first_other = [to_core(array) for array in first]
 
     resid, marked = add_residual(n_tp, place, sums[0], after(terms, first_other), hidden)
@@ -619,8 +640,9 @@
     wide = to_z(resid, m)
     blocks = after(blocks, resid)
     down = [far(blocks[0])]
-    held = hold(after(first_other + first, resid))
-    wide = after(wide, (near, held))
+    held, all_held = hold(after([expert_weights, own_other] + first_other + first, resid))
+    own, held = held[:CORES], held[CORES:]
+    wide = after(wide, (near, held[0]))
     gathered = near + [wide]
     for dz in range(m + 1, n_z):
         step = dz & -dz
@@ -641,15 +663,19 @@
         held,
         passed_other + passed,
     )
-    parts = [own_parts[0]] + [to_z(own_parts[dz], dz) for dz in range(1, n_z)]
+    order = list(range(m, n_z)) + list(range(1, m)) + [0]
+    parts = {(0, dz): to_z(own_parts[dz], dz) if dz else own_parts[0] for dz in order}
     down = after(down, units)
     for dt in range(1, n_tp):
         sources = []
         for arrays in down:
             sources += [to_core(arrays[dt - 1]), arrays[dt - 1]]
         found = run_features(n_tp, n_z, dt, place, units, far_resid, sources)
-        parts += [to_z(found[dz], dz, n_tp - dt) for dz in range(n_z)]
-    return mix(n_tp, n_z, place, parts).reshape(2, tokens, quarter)
+        for dz in order:
+            parts[dt, dz] = to_z(found[dz], dz, n_tp - dt)
+    owners = [(dt, dz) for far in (True, False) for dt in range(n_tp) for dz in order if (dz >= m) == far]
+    parts = [parts[owner] for owner in owners]
+    return mix(n_tp, [dt for dt, _ in owners], place, parts).reshape(2, tokens, quarter)
 
 
 def solution(mesh):

time: 132 us -> 129 us (0.977)
  waiting for transfers between devices: 54.3 us -> 63.3 us
  starting transfers between devices: 34.3 us -> 25.3 us
  local copies, waits for them, and re-layouts: 16.7 us -> 13.1 us
    ppermute x16, waiting for transfers between devices: 45.8 us -> 53.9 us  [send(): return lax.ppermute(array, ('ep', 'tp'), pairs)]
    ppermute x16, starting transfers between devices: 27 us -> 19.2 us  [send(): return lax.ppermute(array, ('ep', 'tp'), pairs)]
    unnamed x41 -> x31, local copies, waits for them, and re-layouts: 9.63 us -> 4.93 us
    pallas_call x2 -> x1, Pallas kernels: 2.9 us -> 3.28 us  [hold(): pl.pallas_call(functools.partial(hold_kernel, len(arrays)), out_shape=[pl...]
  transfers between devices with their start and end apart: 26 -> 26, of which waited for: 13 -> 13; matrix products, arithmetic and copies ran while one was open for 6% -> 7% of each run, Pallas kernels for 17% -> 19%
where the time goes in v4:
time: 129 us; the launch traced here: 128 us
  waiting for transfers between devices  63.3 us (49%)
  starting transfers between devices  25.3 us (20%)
  Pallas kernels  25.3 us (20%)
  local copies, waits for them, and re-layouts  13.1 us (10%)
    ppermute x16, waiting for transfers between devices, send(): return lax.ppermute(array, ('ep', 'tp'), pairs)  53.9 us
    ppermute x16, starting transfers between devices, send(): return lax.ppermute(array, ('ep', 'tp'), pairs)  19.2 us
    pallas_call x1, Pallas kernels, run_units(): pl.pallas_call(functools.partial(units_kernel, n_tp, n_z, n_rep), out_sha...  8.33 us
    ppermute x2, waiting for transfers between devices, to_tp(): lax.ppermute(array, 'tp', [(i, (i + shift) % n_tp) for i in range(n_tp)])  7.11 us
    dynamic_slice x3, local copies, waits for them, and re-layouts, block_of(): lax.dynamic_slice(array, (0, first, first_row, 0), (array.shape[0], last...  7.05 us
    unnamed x31, local copies, waits for them, and re-layouts  4.93 us
    pallas_call x1, Pallas kernels, attend(): pl.pallas_call(functools.partial(attention_kernel, cache.shape[3] // HEAD...  3.99 us
    pallas_call x1, Pallas kernels, run_features(): pl.pallas_call(functools.partial(features_kernel, n_tp, n_z, dt), out_sha...  3.83 us
  transfers between devices with their start and end apart: 26, of which 13 were waited for; matrix products, arithmetic and copies ran while one was open for 7% of the time, Pallas kernels for 19%

profile of v4, /device:TPU:0, one launch (start us, length us, event | category | flops | bytes accessed | tf_op | source)
XLA Modules:
  0.0 128.4 jit_solution(17015536989004528270)
XLA Ops:
  0.5 3.0 %collective-permute-start = (bf16[2048,256]{1,0:T(8,128)(2,1)}, bf16[2048,256]{1,0:T(8,128)(2,1)}, u32[]{:S(2)}, u32[]{:S(2)}) collective-permute-start(bf16[2048,256]{1,0:T(8,128)(2,1)} %refs_2_), channel_id=1, source_target_pairs={{0,4},{1,5},{2,6},{3,7},{4,0},{5,1},{6,2},{7,3},{8,12},{9,13},{10,... | collective-permute-start | bytes 3145736 | tf_op jit(solution)/shard_map/ppermute | solution.py:555
  4.5 1.6 %collective-permute-start.3 = (bf16[64,1024]{1,0:T(8,128)(2,1)S(1)}, bf16[64,1024]{1,0:T(8,128)(2,1)S(1)}, u32[]{:S(2)}, u32[]{:S(2)}) collective-permute-start(bf16[64,1024]{1,0:T(8,128)(2,1)S(1)} %constant_dynamic-slice_fusion.2), channel_id=1, source_target_pairs={{0,1},{1,0},{2,3},{3,2},{4,5},{5,4},{6,7},{7,6},{8,9},{9,8},{10,11... | collective-permute-start | bytes 393224 | tf_op jit(solution)/shard_map/ppermute | solution.py:561
  7.7 2.9 %constant_dynamic-slice_fusion.1 = bf16[2,2,512,384]{3,2,1,0:T(8,128)(2,1)} fusion(bf16[2,3,1024,384]{3,2,1,0:T(8,128)(2,1)} %refs_0_, s32[]{:T(128)S(6)} %select_n.61), kind=kLoop, calls=%fused_computation.10 | loop fusion | bytes 3145732 | tf_op jit(solution)/shard_map/dynamic_slice | solution.py:580
  11.6 4.0 %attention.1.refs_0_ = bf16[128,2048]{1,0:T(8,128)(2,1)S(1)} custom-call(s32[1]{0:T(128)S(6)} %copy.16.length_ref, bf16[2,64,2048]{2,1,0:T(8,128)(2,1)S(1)} %copy-done.5, bf16[1,2,1024,256]{3,2,1,0:T(8,128)(2,1)S(1)} %copy-done.3, bf16[128,512]{1,0:T(8,128)(2,1)S(1)} %bitcast.19), custom_call_target="tpu_custom_call" | custom-call | flops 1000 | bytes 1000 | tf_op jit(solution)/shard_map/attention/pallas_call | solution.py:114
  15.7 2.7 %collective-permute-start.4 = (bf16[128,2048]{1,0:T(8,128)(2,1)S(1)}, bf16[128,2048]{1,0:T(8,128)(2,1)S(1)}, u32[]{:S(2)}, u32[]{:S(2)}) collective-permute-start(bf16[128,2048]{1,0:T(8,128)(2,1)S(1)} %attention.1.refs_0_), channel_id=1, source_target_pairs={{0,8},{1,9},{2,10},{3,11},{4,12},{5,13},{6,14},{7,15},{8,0},{9,1},... | collective-permute-start | bytes 1572872 | tf_op jit(solution)/shard_map/ppermute | solution.py:555
  18.3 18.3 %collective-permute-done.refs_4_ = bf16[2048,256]{1,0:T(8,128)(2,1)} collective-permute-done((bf16[2048,256]{1,0:T(8,128)(2,1)}, bf16[2048,256]{1,0:T(8,128)(2,1)}, u32[]{:S(2)}, u32[]{:S(2)}) %collective-permute-start) | collective-permute-done | bytes 1048608 | tf_op jit(solution)/shard_map/ppermute | solution.py:555
  36.6 2.3 %dynamic_slice.17 = bf16[2,1,704,384]{3,2,1,0:T(8,128)(2,1)} slice(bf16[2,3,1024,384]{3,2,1,0:T(8,128)(2,1)} %refs_0_), slice={[0:2], [2:3], [0:704], [0:384]} | slice | bytes 2162688 | tf_op jit(solution)/shard_map/dynamic_slice | solution.py:580
  38.9 1.8 %dynamic_slice.18 = bf16[2,1,320,384]{3,2,1,0:T(8,128)(2,1)} slice(bf16[2,3,1024,384]{3,2,1,0:T(8,128)(2,1)} %refs_0_), slice={[0:2], [2:3], [704:1024], [0:384]} | slice | bytes 983040 | tf_op jit(solution)/shard_map/dynamic_slice | solution.py:580
  42.4 1.4 %copy-done = bf16[2048,256]{1,0:T(8,128)(2,1)S(1)} copy-done((bf16[2048,256]{1,0:T(8,128)(2,1)S(1)}, bf16[2048,256]{1,0:T(8,128)(2,1)}, u32[]{:S(2)}) %copy-start) | copy-done | bytes 1048600
  43.8 1.6 %copy-done.2 = bf16[2048,256]{1,0:T(8,128)(2,1)S(1)} copy-done((bf16[2048,256]{1,0:T(8,128)(2,1)S(1)}, bf16[2048,256]{1,0:T(8,128)(2,1)}, u32[]{:S(2)}) %copy-start.2) | copy-done | bytes 1048600
  45.4 2.2 %out_projection.1.refs_3_ = f32[256,768]{1,0:T(8,128)S(1)} custom-call(s32[6]{0:T(128)S(1)} %stack.36.place_ref, bf16[128,2048]{1,0:T(8,128)(2,1)S(1)} %attention.1.refs_0_, bf16[128,2048]{1,0:T(8,128)(2,1)S(1)} %collective-permute-done.4.refs_1_, bf16[2048,256]{1,0:T(8,128)(2,1)S(1)} %copy-done, bf16[2048,256]{1,0:T(8,128)(2,1)S(1)} %copy-done.2, ...), custom_call_target="tpu_custom_call" | custom-call | flops 1000 | bytes 1000 | tf_op jit(solution)/shard_map/out_projection/pallas_call | solution.py:144
  49.0 1.6 %collective-permute-start.14 = (bf16[2,2,512,384]{3,2,1,0:T(8,128)(2,1)S(1)}, bf16[2,2,512,384]{3,2,1,0:T(8,128)(2,1)S(1)}, u32[]{:S(2)}, u32[]{:S(2)}) collective-permute-start(bf16[2,2,512,384]{3,2,1,0:T(8,128)(2,1)S(1)} %collective-permute-done.7.refs_3_), channel_id=1, source_target_pairs={{0,16},{16,0},{1,17},{17,1},{2,18},{18,2},{3,19},{19,3},{4,20},{20... | collective-permute-start | bytes 4718600 | tf_op jit(solution)/shard_map/ppermute | solution.py:564
  50.6 1.5 %collective-permute-start.6 = (bf16[144,1024]{1,0:T(8,128)(2,1)S(1)}, bf16[144,1024]{1,0:T(8,128)(2,1)S(1)}, u32[]{:S(2)}, u32[]{:S(2)}) collective-permute-start(bf16[144,1024]{1,0:T(8,128)(2,1)S(1)} %get-tuple-element.70), channel_id=1, source_target_pairs={{0,1},{1,0},{2,3},{3,2},{4,5},{5,4},{6,7},{7,6},{8,9},{9,8},{10,11... | collective-permute-start | bytes 884744 | tf_op jit(solution)/shard_map/ppermute | solution.py:561
  52.3 7.1 %collective-permute-done.6.refs_0_.refs_1_ = bf16[144,1024]{1,0:T(8,128)(2,1)S(1)} collective-permute-done((bf16[144,1024]{1,0:T(8,128)(2,1)S(1)}, bf16[144,1024]{1,0:T(8,128)(2,1)S(1)}, u32[]{:S(2)}, u32[]{:S(2)}) %collective-permute-start.6) | collective-permute-done | bytes 294944 | tf_op jit(solution)/shard_map/ppermute | solution.py:561
  59.4 2.1 %collective-permute-done.9.refs_2_ = bf16[64,1152]{1,0:T(8,128)(2,1)S(1)} collective-permute-done((bf16[64,1152]{1,0:T(8,128)(2,1)S(1)}, bf16[64,1152]{1,0:T(8,128)(2,1)S(1)}, u32[]{:S(2)}, u32[]{:S(2)}) %collective-permute-start.9) | collective-permute-done | bytes 147488 | tf_op jit(solution)/shard_map/ppermute | solution.py:555
  62.3 2.5 %collective-permute-start.11 = (bf16[128,1024]{1,0:T(8,128)(2,1)S(1)}, bf16[128,1024]{1,0:T(8,128)(2,1)S(1)}, u32[]{:S(2)}, u32[]{:S(2)}) collective-permute-start(bf16[128,1024]{1,0:T(8,128)(2,1)S(1)} %get-tuple-element.78), channel_id=1, source_target_pairs={{0,8},{1,9},{2,10},{3,11},{4,12},{5,13},{6,14},{7,15},{8,0},{9,1},... | collective-permute-start | bytes 786440 | tf_op jit(solution)/shard_map/ppermute | solution.py:555
  64.8 3.3 %hold.1 = (bf16[2,3,1024,384]{3,2,1,0:T(8,128)(2,1)S(1)}, bf16[2,3,1024,384]{3,2,1,0:T(8,128)(2,1)S(1)}, bf16[2,2,512,384]{3,2,1,0:T(8,128)(2,1)S(1)}, bf16[2,2,512,384]{3,2,1,0:T(8,128)(2,1)S(1)}, f32[8,128]{1,0:T(8,128)}) custom-call(bf16[2,3,1024,384]{3,2,1,0:T(8,128)(2,1)S(1)} %bitcast.16, bf16[2,3,1024,384]{3,2,1,0:T(8,128)(2,1)} %collective-permute-done.1.refs_1_, ...), custom_call_target="tpu_custom_call" | custom-call | flops 1000 | bytes 1000 | tf_op jit(solution)/shard_map/hold/pallas_call | solution.py:242
  68.1 7.1 %collective-permute-done.11.refs_4_ = bf16[128,1024]{1,0:T(8,128)(2,1)S(1)} collective-permute-done((bf16[128,1024]{1,0:T(8,128)(2,1)S(1)}, bf16[128,1024]{1,0:T(8,128)(2,1)S(1)}, u32[]{:S(2)}, u32[]{:S(2)}) %collective-permute-start.11) | collective-permute-done | bytes 262176 | tf_op jit(solution)/shard_map/ppermute | solution.py:555
  75.2 2.1 %collective-permute-done.10.refs_3_ = bf16[128,1152]{1,0:T(8,128)(2,1)S(1)} collective-permute-done((bf16[128,1152]{1,0:T(8,128)(2,1)S(1)}, bf16[128,1152]{1,0:T(8,128)(2,1)S(1)}, u32[]{:S(2)}, u32[]{:S(2)}) %collective-permute-start.10) | collective-permute-done | bytes 294944 | tf_op jit(solution)/shard_map/ppermute | solution.py:555
  78.3 7.1 %collective-permute-done.12.refs_5_ = bf16[128,1024]{1,0:T(8,128)(2,1)S(1)} collective-permute-done((bf16[128,1024]{1,0:T(8,128)(2,1)S(1)}, bf16[128,1024]{1,0:T(8,128)(2,1)S(1)}, u32[]{:S(2)}, u32[]{:S(2)}) %collective-permute-start.12) | collective-permute-done | bytes 262176 | tf_op jit(solution)/shard_map/ppermute | solution.py:555
  85.4 2.4 %collective-permute-done.13.refs_1_ = bf16[2,1,704,384]{3,2,1,0:T(8,128)(2,1)S(1)} collective-permute-done((bf16[2,1,704,384]{3,2,1,0:T(8,128)(2,1)S(1)}, bf16[2,1,704,384]{3,2,1,0:T(8,128)(2,1)S(1)}, u32[]{:S(2)}, u32[]{:S(2)}) %collective-permute-start.13) | collective-permute-done | bytes 1081376 | tf_op jit(solution)/shard_map/ppermute | solution.py:555
  89.0 2.3 %collective-permute-done.15.refs_10_ = bf16[2,2,512,384]{3,2,1,0:T(8,128)(2,1)S(1)} collective-permute-done((bf16[2,2,512,384]{3,2,1,0:T(8,128)(2,1)S(1)}, bf16[2,2,512,384]{3,2,1,0:T(8,128)(2,1)S(1)}, u32[]{:S(2)}, u32[]{:S(2)}) %collective-permute-start.15) | collective-permute-done | bytes 1572896 | tf_op jit(solution)/shard_map/ppermute | solution.py:558
  91.2 8.3 %units.1 = (bf16[256,1536]{1,0:T(8,128)(2,1)S(1)}, bf16[1,64,1024]{2,1,0:T(8,128)(2,1)S(1)}, f32[64,1024]{1,0:T(8,128)S(1)}, bf16[64,1024]{1,0:T(8,128)(2,1)S(1)...) custom-call(s32[6]{0:T(128)S(1)} %stack.36.place_ref, s32[1,16]{1,0:T(1,128)S(1)} %constant_dynamic-slice_fusion.table_ref, ...), custom_call_target="tpu_custom_call" | custom-call | flops 1000 | bytes 1000 | tf_op jit(solution)/shard_map/units/pallas_call | solution.py:418
  99.6 1.3 collective-permute-done.18.refs_3_
  101.4 2.0 %collective-permute-start.17 = (bf16[64,1024]{1,0:T(8,128)(2,1)S(1)}, bf16[64,1024]{1,0:T(8,128)(2,1)S(1)}, u32[]{:S(2)}, u32[]{:S(2)}) collective-permute-start(bf16[64,1024]{1,0:T(8,128)(2,1)S(1)} %get-tuple-element.98), channel_id=1, source_target_pairs={{0,12},{1,13},{2,14},{3,15},{4,8},{5,9},{6,10},{7,11},{8,4},{9,5},... | collective-permute-start | bytes 393224 | tf_op jit(solution)/shard_map/ppermute | solution.py:555
  103.3 1.5 %collective-permute-start.23 = (bf16[64,1024]{1,0:T(8,128)(2,1)S(1)}, bf16[64,1024]{1,0:T(8,128)(2,1)S(1)}, u32[]{:S(2)}, u32[]{:S(2)}) collective-permute-start(bf16[64,1024]{1,0:T(8,128)(2,1)S(1)} %get-tuple-element.107), channel_id=1, source_target_pairs={{0,4},{1,5},{2,6},{3,7},{4,0},{5,1},{6,2},{7,3},{8,12},{9,13},{10,... | collective-permute-start | bytes 393224 | tf_op jit(solution)/shard_map/ppermute | solution.py:555
  104.9 3.8 %features.1 = (bf16[64,1024]{1,0:T(8,128)(2,1)S(1)}, bf16[64,1024]{1,0:T(8,128)(2,1)S(1)}, bf16[64,1024]{1,0:T(8,128)(2,1)S(1)}, bf16[64,1024]{1,0:T(8,128)(2,1)S(1)}) custom-call(s32[6]{0:T(128)S(1)} %stack.36.place_ref, bf16[256,1536]{1,0:T(8,128)(2,1)S(1)} %get-tuple-element.99.hidden_ref, bf16[1,64,1024]{2,1,0:T(8,128)(2,1)S(1)} %get-tuple-element.100.resid_ref, ...), custom_call_target="tpu_custom_call" | custom-call | flops 1000 | bytes 1000 | tf_op jit(solution)/shard_map/features/pallas_call | solution.py:447
  108.7 1.6 %collective-permute-start.21 = (bf16[64,1024]{1,0:T(8,128)(2,1)S(1)}, bf16[64,1024]{1,0:T(8,128)(2,1)S(1)}, u32[]{:S(2)}, u32[]{:S(2)}) collective-permute-start(bf16[64,1024]{1,0:T(8,128)(2,1)S(1)} %get-tuple-element.105), channel_id=1, source_target_pairs={{0,9},{1,8},{2,11},{3,10},{4,13},{5,12},{6,15},{7,14},{8,1},{9,0},... | collective-permute-start | bytes 393224 | tf_op jit(solution)/shard_map/ppermute | solution.py:555
  110.3 2.3 %collective-permute-start.22 = (bf16[64,1024]{1,0:T(8,128)(2,1)S(1)}, bf16[64,1024]{1,0:T(8,128)(2,1)S(1)}, u32[]{:S(2)}, u32[]{:S(2)}) collective-permute-start(bf16[64,1024]{1,0:T(8,128)(2,1)S(1)} %get-tuple-element.106), channel_id=1, source_target_pairs={{0,13},{1,12},{2,15},{3,14},{4,9},{5,8},{6,11},{7,10},{8,5},{9,4},... | collective-permute-start | bytes 393224 | tf_op jit(solution)/shard_map/ppermute | solution.py:555
  114.6 10.4 %collective-permute-done.21.refs_2_ = bf16[64,1024]{1,0:T(8,128)(2,1)S(1)} collective-permute-done((bf16[64,1024]{1,0:T(8,128)(2,1)S(1)}, bf16[64,1024]{1,0:T(8,128)(2,1)S(1)}, u32[]{:S(2)}, u32[]{:S(2)}) %collective-permute-start.21) | collective-permute-done | bytes 131104 | tf_op jit(solution)/shard_map/ppermute | solution.py:555
  125.0 2.0 %collective-permute-done.25.refs_7_ = bf16[64,1024]{1,0:T(8,128)(2,1)S(1)} collective-permute-done((bf16[64,1024]{1,0:T(8,128)(2,1)S(1)}, bf16[64,1024]{1,0:T(8,128)(2,1)S(1)}, u32[]{:S(2)}, u32[]{:S(2)}) %collective-permute-start.25) | collective-permute-done | bytes 131104 | tf_op jit(solution)/shard_map/ppermute | solution.py:555
  127.0 1.4 %mix.1 = bf16[128,1024]{1,0:T(8,128)(2,1)} custom-call(s32[6]{0:T(128)S(1)} %stack.36.place_ref, bf16[64,1024]{1,0:T(8,128)(2,1)S(1)} %collective-permute-done.16.refs_0_, bf16[64,1024]{1,0:T(8,128)(2,1)S(1)} %collective-permute-done.17.refs_1_, bf16[64,1024]{1,0:T(8,128)(2,1)S(1)} %collective-permute-done.21.refs_2_, ...), custom_call_target="tpu_custom_call" | custom-call | flops 1000 | bytes 1000 | tf_op jit(solution)/shard_map/mix/pallas_call | solution.py:512
  (74 shorter events, 12.1 us)
Async XLA Ops:
  0.0 18.3 %collective-permute-start.1 = (bf16[2,3,1024,384]{3,2,1,0:T(8,128)(2,1)}, bf16[2,3,1024,384]{3,2,1,0:T(8,128)(2,1)}, u32[]{:S(2)}, u32[]{:S(2)}) collective-permute-start(bf16[2,3,1024,384]{3,2,1,0:T(8,128)(2,1)} %refs_0_), channel_id=1, source_target_pairs={{0,2},{2,0},{4,6},{6,4},{8,10},{10,8},{12,14},{14,12},{1,3},{3,1},... | collective-permute-start | bytes 14155784 | tf_op jit(solution)/shard_map/ppermute | solution.py:558
  0.5 10.1 %collective-permute-start.2 = (bf16[2048,256]{1,0:T(8,128)(2,1)}, bf16[2048,256]{1,0:T(8,128)(2,1)S(1)}, u32[]{:S(2)}, u32[]{:S(2)}) collective-permute-start(bf16[2048,256]{1,0:T(8,128)(2,1)} %refs_2_), channel_id=1, source_target_pairs={{0,2},{2,0},{4,6},{6,4},{8,10},{10,8},{12,14},{14,12},{1,3},{3,1},... | collective-permute-start | bytes 3145736 | tf_op jit(solution)/shard_map/ppermute | solution.py:558
  0.5 36.1 %collective-permute-start = (bf16[2048,256]{1,0:T(8,128)(2,1)}, bf16[2048,256]{1,0:T(8,128)(2,1)}, u32[]{:S(2)}, u32[]{:S(2)}) collective-permute-start(bf16[2048,256]{1,0:T(8,128)(2,1)} %refs_2_), channel_id=1, source_target_pairs={{0,4},{1,5},{2,6},{3,7},{4,0},{5,1},{6,2},{7,3},{8,12},{9,13},{10,... | collective-permute-start | bytes 3145736 | tf_op jit(solution)/shard_map/ppermute | solution.py:555
  4.5 6.1 %collective-permute-start.3 = (bf16[64,1024]{1,0:T(8,128)(2,1)S(1)}, bf16[64,1024]{1,0:T(8,128)(2,1)S(1)}, u32[]{:S(2)}, u32[]{:S(2)}) collective-permute-start(bf16[64,1024]{1,0:T(8,128)(2,1)S(1)} %constant_dynamic-slice_fusion.2), channel_id=1, source_target_pairs={{0,1},{1,0},{2,3},{3,2},{4,5},{5,4},{6,7},{7,6},{8,9},{9,8},{10,11... | collective-permute-start | bytes 393224 | tf_op jit(solution)/shard_map/ppermute | solution.py:561
  10.6 38.0 %collective-permute-start.7 = (bf16[2,2,512,384]{3,2,1,0:T(8,128)(2,1)}, bf16[2,2,512,384]{3,2,1,0:T(8,128)(2,1)S(1)}, u32[]{:S(2)}, u32[]{:S(2)}) collective-permute-start(bf16[2,2,512,384]{3,2,1,0:T(8,128)(2,1)} %constant_dynamic-slice_fusion.1), channel_id=1, source_target_pairs={{0,3},{1,2},{2,1},{3,0},{4,7},{5,6},{6,5},{7,4},{8,11},{9,10},{10,... | collective-permute-start | bytes 4718600 | tf_op jit(solution)/shard_map/ppermute | solution.py:555
  15.6 25.2 %copy-start.10 = (s32[16]{0:T(128)S(1)}, s32[16]{0:T(128)}, u32[]{:S(2)}) copy-start(s32[16]{0:T(128)} %param.21) | copy-start | bytes 196
  15.6 25.1 %copy-start.11 = (s32[4]{0:T(128)S(1)}, s32[4]{0:T(128)}, u32[]{:S(2)}) copy-start(s32[4]{0:T(128)} %param.23) | copy-start | bytes 52
  15.6 25.1 %copy-start.12 = (s32[16]{0:T(128)S(1)}, s32[16]{0:T(128)}, u32[]{:S(2)}) copy-start(s32[16]{0:T(128)} %param.22) | copy-start | bytes 196
  15.7 25.5 %copy-start.9 = (s32[2,64,8]{1,2,0:T(8,128)S(1)}, s32[2,64,8]{1,2,0:T(8,128)}, u32[]{:S(2)}) copy-start(s32[2,64,8]{1,2,0:T(8,128)} %param.20) | copy-start | bytes 12292
  15.7 25.6 %copy-start.4 = (bf16[2,64,1024]{2,1,0:T(8,128)(2,1)S(1)}, bf16[2,64,1024]{2,1,0:T(8,128)(2,1)}, u32[]{:S(2)}) copy-start(bf16[2,64,1024]{2,1,0:T(8,128)(2,1)} %param.12) | copy-start | bytes 786436
  15.7 26.7 %collective-permute-start.4 = (bf16[128,2048]{1,0:T(8,128)(2,1)S(1)}, bf16[128,2048]{1,0:T(8,128)(2,1)S(1)}, u32[]{:S(2)}, u32[]{:S(2)}) collective-permute-start(bf16[128,2048]{1,0:T(8,128)(2,1)S(1)} %attention.1.refs_0_), channel_id=1, source_target_pairs={{0,8},{1,9},{2,10},{3,11},{4,12},{5,13},{6,14},{7,15},{8,0},{9,1},... | collective-permute-start | bytes 1572872 | tf_op jit(solution)/shard_map/ppermute | solution.py:555
  42.4 5.2 %collective-permute-start.5 = (bf16[2048,256]{1,0:T(8,128)(2,1)}, bf16[2048,256]{1,0:T(8,128)(2,1)S(1)}, u32[]{:S(2)}, u32[]{:S(2)}) collective-permute-start(bf16[2048,256]{1,0:T(8,128)(2,1)} %collective-permute-done.refs_4_), channel_id=1, source_target_pairs={{0,2},{2,0},{4,6},{6,4},{8,10},{10,8},{12,14},{14,12},{1,3},{3,1},... | collective-permute-start | bytes 3145736 | tf_op jit(solution)/shard_map/ppermute | solution.py:558
  48.6 10.7 %collective-permute-start.8 = (bf16[2,2,512,384]{3,2,1,0:T(8,128)(2,1)S(1)}, bf16[2,2,512,384]{3,2,1,0:T(8,128)(2,1)S(1)}, u32[]{:S(2)}, u32[]{:S(2)}) collective-permute-start(bf16[2,2,512,384]{3,2,1,0:T(8,128)(2,1)S(1)} %collective-permute-done.7.refs_3_), channel_id=1, source_target_pairs={{0,2},{2,0},{4,6},{6,4},{8,10},{10,8},{12,14},{14,12},{1,3},{3,1},... | collective-permute-start | bytes 4718600 | tf_op jit(solution)/shard_map/ppermute | solution.py:558
  49.0 38.8 %collective-permute-start.14 = (bf16[2,2,512,384]{3,2,1,0:T(8,128)(2,1)S(1)}, bf16[2,2,512,384]{3,2,1,0:T(8,128)(2,1)S(1)}, u32[]{:S(2)}, u32[]{:S(2)}) collective-permute-start(bf16[2,2,512,384]{3,2,1,0:T(8,128)(2,1)S(1)} %collective-permute-done.7.refs_3_), channel_id=1, source_target_pairs={{0,16},{16,0},{1,17},{17,1},{2,18},{18,2},{3,19},{19,3},{4,20},{20... | collective-permute-start | bytes 4718600 | tf_op jit(solution)/shard_map/ppermute | solution.py:564
  50.6 8.7 %collective-permute-start.6 = (bf16[144,1024]{1,0:T(8,128)(2,1)S(1)}, bf16[144,1024]{1,0:T(8,128)(2,1)S(1)}, u32[]{:S(2)}, u32[]{:S(2)}) collective-permute-start(bf16[144,1024]{1,0:T(8,128)(2,1)S(1)} %get-tuple-element.70), channel_id=1, source_target_pairs={{0,1},{1,0},{2,3},{3,2},{4,5},{5,4},{6,7},{7,6},{8,9},{9,8},{10,11... | collective-permute-start | bytes 884744 | tf_op jit(solution)/shard_map/ppermute | solution.py:561
  52.1 9.4 %collective-permute-start.9 = (bf16[64,1152]{1,0:T(8,128)(2,1)S(1)}, bf16[64,1152]{1,0:T(8,128)(2,1)S(1)}, u32[]{:S(2)}, u32[]{:S(2)}) collective-permute-start(bf16[64,1152]{1,0:T(8,128)(2,1)S(1)} %get-tuple-element.76), channel_id=1, source_target_pairs={{0,8},{1,9},{2,10},{3,11},{4,12},{5,13},{6,14},{7,15},{8,0},{9,1},... | collective-permute-start | bytes 442376 | tf_op jit(solution)/shard_map/ppermute | solution.py:555
  62.1 25.7 %collective-permute-start.13 = (bf16[2,1,704,384]{3,2,1,0:T(8,128)(2,1)S(1)}, bf16[2,1,704,384]{3,2,1,0:T(8,128)(2,1)S(1)}, u32[]{:S(2)}, u32[]{:S(2)}) collective-permute-start(bf16[2,1,704,384]{3,2,1,0:T(8,128)(2,1)S(1)} %copy-done.7), channel_id=1, source_target_pairs={{0,3},{1,2},{2,1},{3,0},{4,7},{5,6},{6,5},{7,4},{8,11},{9,10},{10,... | collective-permute-start | bytes 3244040 | tf_op jit(solution)/shard_map/ppermute | solution.py:555
  62.2 25.6 %copy-start.8 = (bf16[2,1,320,384]{3,2,1,0:T(8,128)(2,1)S(1)}, bf16[2,1,320,384]{3,2,1,0:T(8,128)(2,1)}, u32[]{:S(2)}) copy-start(bf16[2,1,320,384]{3,2,1,0:T(8,128)(2,1)} %dynamic_slice.18) | copy-start | bytes 1474564
  62.2 15.2 %collective-permute-start.10 = (bf16[128,1152]{1,0:T(8,128)(2,1)S(1)}, bf16[128,1152]{1,0:T(8,128)(2,1)S(1)}, u32[]{:S(2)}, u32[]{:S(2)}) collective-permute-start(bf16[128,1152]{1,0:T(8,128)(2,1)S(1)} %get-tuple-element.89.refs_2_), channel_id=1, source_target_pairs={{0,4},{1,5},{2,6},{3,7},{4,0},{5,1},{6,2},{7,3},{8,12},{9,13},{10,... | collective-permute-start | bytes 884744 | tf_op jit(solution)/shard_map/ppermute | solution.py:555
  62.3 12.9 %collective-permute-start.11 = (bf16[128,1024]{1,0:T(8,128)(2,1)S(1)}, bf16[128,1024]{1,0:T(8,128)(2,1)S(1)}, u32[]{:S(2)}, u32[]{:S(2)}) collective-permute-start(bf16[128,1024]{1,0:T(8,128)(2,1)S(1)} %get-tuple-element.78), channel_id=1, source_target_pairs={{0,8},{1,9},{2,10},{3,11},{4,12},{5,13},{6,14},{7,15},{8,0},{9,1},... | collective-permute-start | bytes 786440 | tf_op jit(solution)/shard_map/ppermute | solution.py:555
  77.4 8.0 %collective-permute-start.12 = (bf16[128,1024]{1,0:T(8,128)(2,1)S(1)}, bf16[128,1024]{1,0:T(8,128)(2,1)S(1)}, u32[]{:S(2)}, u32[]{:S(2)}) collective-permute-start(bf16[128,1024]{1,0:T(8,128)(2,1)S(1)} %collective-permute-done.11.refs_4_), channel_id=1, source_target_pairs={{0,4},{1,5},{2,6},{3,7},{4,0},{5,1},{6,2},{7,3},{8,12},{9,13},{10,... | collective-permute-start | bytes 786440 | tf_op jit(solution)/shard_map/ppermute | solution.py:555
  87.8 3.4 %collective-permute-start.15 = (bf16[2,2,512,384]{3,2,1,0:T(8,128)(2,1)S(1)}, bf16[2,2,512,384]{3,2,1,0:T(8,128)(2,1)S(1)}, u32[]{:S(2)}, u32[]{:S(2)}) collective-permute-start(bf16[2,2,512,384]{3,2,1,0:T(8,128)(2,1)S(1)} %collective-permute-done.14.refs_11_), channel_id=1, source_target_pairs={{0,2},{2,0},{4,6},{6,4},{8,10},{10,8},{12,14},{14,12},{1,3},{3,1},... | collective-permute-start | bytes 4718600 | tf_op jit(solution)/shard_map/ppermute | solution.py:558
  87.8 13.0 %collective-permute-start.18 = (bf16[2,1,320,384]{3,2,1,0:T(8,128)(2,1)S(1)}, bf16[2,1,320,384]{3,2,1,0:T(8,128)(2,1)S(1)}, u32[]{:S(2)}, u32[]{:S(2)}) collective-permute-start(bf16[2,1,320,384]{3,2,1,0:T(8,128)(2,1)S(1)} %copy-done.8), channel_id=1, source_target_pairs={{0,3},{1,2},{2,1},{3,0},{4,7},{5,6},{6,5},{7,4},{8,11},{9,10},{10,... | collective-permute-start | bytes 1474568 | tf_op jit(solution)/shard_map/ppermute | solution.py:555
  100.8 4.0 %collective-permute-start.19 = (bf16[2,1,704,384]{3,2,1,0:T(8,128)(2,1)S(1)}, bf16[2,1,704,384]{3,2,1,0:T(8,128)(2,1)S(1)}, u32[]{:S(2)}, u32[]{:S(2)}) collective-permute-start(bf16[2,1,704,384]{3,2,1,0:T(8,128)(2,1)S(1)} %collective-permute-done.13.refs_1_), channel_id=1, source_target_pairs={{0,2},{2,0},{4,6},{6,4},{8,10},{10,8},{12,14},{14,12},{1,3},{3,1},... | collective-permute-start | bytes 3244040 | tf_op jit(solution)/shard_map/ppermute | solution.py:558
  101.2 3.6 %collective-permute-start.20 = (bf16[2,1,320,384]{3,2,1,0:T(8,128)(2,1)S(1)}, bf16[2,1,320,384]{3,2,1,0:T(8,128)(2,1)S(1)}, u32[]{:S(2)}, u32[]{:S(2)}) collective-permute-start(bf16[2,1,320,384]{3,2,1,0:T(8,128)(2,1)S(1)} %collective-permute-done.18.refs_3_), channel_id=1, source_target_pairs={{0,2},{2,0},{4,6},{6,4},{8,10},{10,8},{12,14},{14,12},{1,3},{3,1},... | collective-permute-start | bytes 1474568 | tf_op jit(solution)/shard_map/ppermute | solution.py:558
  101.4 12.0 %collective-permute-start.16 = (bf16[64,1024]{1,0:T(8,128)(2,1)S(1)}, bf16[64,1024]{1,0:T(8,128)(2,1)S(1)}, u32[]{:S(2)}, u32[]{:S(2)}) collective-permute-start(bf16[64,1024]{1,0:T(8,128)(2,1)S(1)} %get-tuple-element.97), channel_id=1, source_target_pairs={{0,8},{1,9},{2,10},{3,11},{4,12},{5,13},{6,14},{7,15},{8,0},{9,1},... | collective-permute-start | bytes 393224 | tf_op jit(solution)/shard_map/ppermute | solution.py:555
  101.4 12.4 %collective-permute-start.17 = (bf16[64,1024]{1,0:T(8,128)(2,1)S(1)}, bf16[64,1024]{1,0:T(8,128)(2,1)S(1)}, u32[]{:S(2)}, u32[]{:S(2)}) collective-permute-start(bf16[64,1024]{1,0:T(8,128)(2,1)S(1)} %get-tuple-element.98), channel_id=1, source_target_pairs={{0,12},{1,13},{2,14},{3,15},{4,8},{5,9},{6,10},{7,11},{8,4},{9,5},... | collective-permute-start | bytes 393224 | tf_op jit(solution)/shard_map/ppermute | solution.py:555
  103.3 11.3 %collective-permute-start.23 = (bf16[64,1024]{1,0:T(8,128)(2,1)S(1)}, bf16[64,1024]{1,0:T(8,128)(2,1)S(1)}, u32[]{:S(2)}, u32[]{:S(2)}) collective-permute-start(bf16[64,1024]{1,0:T(8,128)(2,1)S(1)} %get-tuple-element.107), channel_id=1, source_target_pairs={{0,4},{1,5},{2,6},{3,7},{4,0},{5,1},{6,2},{7,3},{8,12},{9,13},{10,... | collective-permute-start | bytes 393224 | tf_op jit(solution)/shard_map/ppermute | solution.py:555
  108.7 16.3 %collective-permute-start.21 = (bf16[64,1024]{1,0:T(8,128)(2,1)S(1)}, bf16[64,1024]{1,0:T(8,128)(2,1)S(1)}, u32[]{:S(2)}, u32[]{:S(2)}) collective-permute-start(bf16[64,1024]{1,0:T(8,128)(2,1)S(1)} %get-tuple-element.105), channel_id=1, source_target_pairs={{0,9},{1,8},{2,11},{3,10},{4,13},{5,12},{6,15},{7,14},{8,1},{9,0},... | collective-permute-start | bytes 393224 | tf_op jit(solution)/shard_map/ppermute | solution.py:555
  110.3 14.7 %collective-permute-start.22 = (bf16[64,1024]{1,0:T(8,128)(2,1)S(1)}, bf16[64,1024]{1,0:T(8,128)(2,1)S(1)}, u32[]{:S(2)}, u32[]{:S(2)}) collective-permute-start(bf16[64,1024]{1,0:T(8,128)(2,1)S(1)} %get-tuple-element.106), channel_id=1, source_target_pairs={{0,13},{1,12},{2,15},{3,14},{4,9},{5,8},{6,11},{7,10},{8,5},{9,4},... | collective-permute-start | bytes 393224 | tf_op jit(solution)/shard_map/ppermute | solution.py:555
  113.3 11.7 %collective-permute-start.24 = (bf16[64,1024]{1,0:T(8,128)(2,1)S(1)}, bf16[64,1024]{1,0:T(8,128)(2,1)S(1)}, u32[]{:S(2)}, u32[]{:S(2)}) collective-permute-start(bf16[64,1024]{1,0:T(8,128)(2,1)S(1)} %get-tuple-element.109), channel_id=1, source_target_pairs={{0,5},{1,4},{2,7},{3,6},{4,1},{5,0},{6,3},{7,2},{8,13},{9,12},{10,... | collective-permute-start | bytes 393224 | tf_op jit(solution)/shard_map/ppermute | solution.py:555
  113.8 13.3 %collective-permute-start.25 = (bf16[64,1024]{1,0:T(8,128)(2,1)S(1)}, bf16[64,1024]{1,0:T(8,128)(2,1)S(1)}, u32[]{:S(2)}, u32[]{:S(2)}) collective-permute-start(bf16[64,1024]{1,0:T(8,128)(2,1)S(1)} %get-tuple-element.110), channel_id=1, source_target_pairs={{0,1},{1,0},{2,3},{3,2},{4,5},{5,4},{6,7},{7,6},{8,9},{9,8},{10,11... | collective-permute-start | bytes 393224 | tf_op jit(solution)/shard_map/ppermute | solution.py:555
  (9 other events, 73.4 us)
